TPU v7x, 128 devices: a whole 4x4x4 slice. The times are simulated.
128 devices in a mesh: layer: 16 (over y, z_lo, core), tile: 8 (over x, z_hi).
Axes of the slice: x: 4, y: 4, z: 4 (z_hi: 2, z_lo: 2; z = z_hi * 2 + z_lo), core: 2. Of those that a mesh axis runs over, the one named last changes fastest.
Arguments:
- incident: bfloat16 [4096, 128], P('tile'), may hold values from -6 to 6
- interface: bfloat16 [32, 4096, 4096], P('layer', 'tile'), may hold values from -0.09375 to 0.09375
- eigvec: bfloat16 [32, 4096, 4096], P('layer', 'tile'), may hold values from -0.09375 to 0.09375
- angle: float32 [32, 4096], P('layer'), may hold values from -3.140625 to 3.140625
- decay: float32 [32, 4096], P('layer'), may hold values from 0.002 to 0.15
Outputs:
- fields: bfloat16 [32, 4096, 512], P('layer', 'tile')
- leaving: float32 [32, 4096, 128], P('layer', 'tile')
All inputs are finite; a program needn't handle non-finite values.
Results may differ from a plain program's by a relative error of at most 0.035.
Values sent between devices are 32-bit elements; how exact they have to be, the bound alone decides.
No kernel may reach another device: no remote copies, remote signals or barrier semaphores. Data moves between devices by JAX's collectives and lax.ppermute only.
A program may use at most 128 MiB of HBM per device.

v0:
```python
import functools

import jax
import jax.numpy as jnp
from jax import lax
from jax.experimental import pallas as pl
from jax.experimental.pallas import tpu as pltpu
from jax.sharding import PartitionSpec as P

DEPTHS = 4
CHUNKS = 2
CORES = 2
PIECES = 8
NT = (((1,), (1,)), ((), ()))
VMEM = pl.BlockSpec(memory_space=pltpu.VMEM)
ANYWHERE = pl.BlockSpec(memory_space=pl.ANY)
VMEM_LIMIT = 48 * 1024 * 1024


def widen_kernel(mat_ref, after_ref, out_ref):
    out_ref[...] = mat_ref[0].astype(jnp.float32)


def widen(mats, layer, after):
    rows, orders = mats.shape[1:]
    piece = rows // PIECES
    return pl.pallas_call(
        widen_kernel,
        out_shape=jax.ShapeDtypeStruct((rows, orders), jnp.float32),
        grid=(PIECES,),
        in_specs=[pl.BlockSpec((1, piece, orders), lambda p: (layer, p, 0)), ANYWHERE],
        out_specs=pl.BlockSpec((piece, orders), lambda p: (p, 0)),
        compiler_params=pltpu.CompilerParams(vmem_limit_bytes=VMEM_LIMIT),
    )(mats, after)


def narrow_kernel(mat_ref, *refs):
    refs[-1][0] = mat_ref[...].astype(jnp.bfloat16)


def narrow(mat, layer, layers, before):
    rows, orders = mat.shape
    piece = rows // PIECES
    return pl.pallas_call(
        narrow_kernel,
        out_shape=jax.ShapeDtypeStruct((layers, rows, orders), jnp.bfloat16),
        grid=(PIECES,),
        in_specs=[pl.BlockSpec((piece, orders), lambda p: (p, 0))] + [ANYWHERE] * len(before),
        out_specs=pl.BlockSpec((1, piece, orders), lambda p: (layer, p, 0)),
        input_output_aliases={1: 0} if before else {},
        compiler_params=pltpu.CompilerParams(vmem_limit_bytes=VMEM_LIMIT),
    )(mat, *before)


def step_kernel(
    core_ref, full_ref, phase_ref, own_ref, other_ref, out_ref, row_buf, mat_buf, row_sem, sems,
    *, half, layer, number
):
    blocks, wide, rows = full_ref.shape
    split = wide // 2
    row_copy = pltpu.make_async_copy(phase_ref.at[number], row_buf, row_sem)
    row_copy.start()

    def copies(mats_ref):
        return [
            pltpu.make_async_copy(
                mats_ref.at[layer, :, pl.ds(b * rows, rows)], mat_buf.at[b], sems.at[b]
            )
            for b in range(blocks)
        ]

    @pl.when(core_ref[0] == half)
    def _():
        for copy in copies(own_ref):
            copy.start()

    @pl.when(core_ref[0] != half)
    def _():
        for copy in copies(other_ref):
            copy.start()

    arrivals = copies(own_ref)
    total = jnp.zeros((wide, rows), jnp.float32)
    row_copy.wait()
    for b in range(blocks):
        cosine = row_buf[0, b : b + 1, :]
        sine = row_buf[1, b : b + 1, :]
        real_part = full_ref[b, :split, :]
        imag_part = full_ref[b, split:, :]
        phased = jnp.concatenate(
            [cosine * real_part - sine * imag_part, sine * real_part + cosine * imag_part], axis=0
        ).astype(jnp.bfloat16)
        arrivals[b].wait()
        total += lax.dot_general(phased, mat_buf[b], NT, preferred_element_type=jnp.float32)
    for b in range(blocks):
        out_ref[b] = total


def layer_step(core, full, phases, own, other, half, layer, number):
    blocks, wide, rows = full.shape
    return pl.pallas_call(
        functools.partial(step_kernel, half=half, layer=layer, number=number),
        out_shape=jax.ShapeDtypeStruct(full.shape, jnp.float32),
        in_specs=[pl.BlockSpec(memory_space=pltpu.SMEM), VMEM] + [ANYWHERE] * 3,
        out_specs=VMEM,
        scratch_shapes=[
            pltpu.VMEM(phases.shape[1:], jnp.float32),
            pltpu.VMEM((blocks, rows, rows), jnp.bfloat16),
            pltpu.SemaphoreType.DMA,
            pltpu.SemaphoreType.DMA((blocks,)),
        ],
        compiler_params=pltpu.CompilerParams(vmem_limit_bytes=VMEM_LIMIT),
        cost_estimate=pl.CostEstimate(
            flops=2 * wide * rows * rows * blocks,
            bytes_accessed=2 * blocks * rows * rows,
            transcendentals=0,
        ),
    )(core, full, phases, own, other)


def fields_kernel(core_ref, own_ref, other_ref, cos_ref, sin_ref, mat_ref, *refs):
    out_ref, total = refs[-2:]
    step = pl.program_id(0)
    chunks, wide, rows = own_ref.shape[1], own_ref.shape[3], own_ref.shape[4]
    half = wide // 2
    first = core_ref[0] == 0

    def columns(part):
        own = own_ref[0, :, 0, part, :].reshape(chunks * half, rows)
        other = other_ref[0, :, 0, part, :].reshape(chunks * half, rows)
        low = jnp.where(first, own, other)
        high = jnp.where(first, other, own)
        return jnp.concatenate([low, high], axis=0)

    real_part = columns(slice(0, half))
    imag_part = columns(slice(half, wide))
    parts = [real_part.astype(jnp.bfloat16), imag_part.astype(jnp.bfloat16)]
    for depth in range(DEPTHS - 1):
        cosine = cos_ref[0, depth : depth + 1, :]
        sine = sin_ref[0, depth : depth + 1, :]
        parts.append((cosine * real_part - sine * imag_part).astype(jnp.bfloat16))
        parts.append((sine * real_part + cosine * imag_part).astype(jnp.bfloat16))
    depths = jnp.concatenate(parts, axis=0)
    partial = lax.dot_general(mat_ref[0], depths, NT, preferred_element_type=jnp.float32)

    @pl.when(step == 0)
    def _():
        total[...] = partial

    @pl.when(step > 0)
    def _():
        total[...] += partial

    @pl.when(step == pl.num_programs(0) - 1)
    def _():
        out_ref[0] = total[...].astype(jnp.bfloat16)


def layer_fields(core, own, other, cosines, sines, eigvec, layer, before):
    chunks = other.shape[1]
    wide, rows = other.shape[3], other.shape[4]
    blocks = eigvec.shape[2] // rows
    cols = DEPTHS * CORES * chunks * wide
    coef = pl.BlockSpec((1, DEPTHS, rows), lambda b, c: (b, 0, 0))
    return pl.pallas_call(
        fields_kernel,
        out_shape=jax.ShapeDtypeStruct((eigvec.shape[0], rows, cols), jnp.bfloat16),
        grid_spec=pltpu.PrefetchScalarGridSpec(
            num_scalar_prefetch=1,
            grid=(blocks,),
            in_specs=[
                pl.BlockSpec((1, chunks, 1, wide, rows), lambda b, c: (c[0], 0, b, 0, 0)),
                pl.BlockSpec((1, chunks, 1, wide, rows), lambda b, c: (0, 0, b, 0, 0)),
                coef,
                coef,
                pl.BlockSpec((1, rows, rows), lambda b, c: (layer, 0, b)),
            ]
            + [ANYWHERE] * len(before),
            out_specs=pl.BlockSpec((1, rows, cols), lambda b, c: (layer, 0, 0)),
            scratch_shapes=[pltpu.VMEM((rows, cols), jnp.float32)],
        ),
        input_output_aliases={6: 0} if before else {},
        compiler_params=pltpu.CompilerParams(vmem_limit_bytes=VMEM_LIMIT),
    )(core, own, other, cosines, sines, eigvec, *before)


def to_all(block):
    return lax.all_to_all(block, "tile", split_axis=0, concat_axis=0, tiled=False)


def on_device(incident, interface, eigvec, angle, decay):
    groups = lax.axis_size("layer")
    tiles = lax.axis_size("tile")
    member = lax.axis_index("layer")
    core = member % CORES
    stage = member // CORES
    stages = groups // CORES
    layers, rows, orders = interface.shape
    width = incident.shape[1]
    part = width // 2 // CORES // CHUNKS
    wide = 2 * part
    core_arg = core.astype(jnp.int32).reshape(1)
    partner = [(i, i ^ 1) for i in range(groups)]
    ring = [(i, (i + CORES) % groups) for i in range(groups)]

    phases = jnp.stack([angle, decay]).reshape(2, layers, tiles, rows)
    other_phases = lax.ppermute(phases, "layer", partner)
    wide_mats = []
    arrived = []
    for layer in range(layers):
        wide_mats.append(widen(interface, layer, wide_mats[-1] if layer else incident))
        arrived.append(lax.ppermute(wide_mats[layer], "layer", partner))
    others = ()
    early = jnp.where(core == 0, phases, other_phases)
    late = jnp.where(core == 0, other_phases, phases)
    all_phases = jnp.concatenate([early, late], axis=1)
    scale = jnp.exp(-all_phases[1])
    whole = jnp.stack([scale * jnp.cos(all_phases[0]), scale * jnp.sin(all_phases[0])], axis=1)
    fracs = (jnp.arange(1, DEPTHS + 1, dtype=jnp.float32) / DEPTHS).reshape(1, 1, DEPTHS, 1)
    scale = jnp.exp(-fracs * phases[1][:, :, None, :])
    cosines = scale * jnp.cos(fracs * phases[0][:, :, None, :])
    sines = scale * jnp.sin(fracs * phases[0][:, :, None, :])

    start = incident.astype(jnp.float32).T.reshape(2, CORES, CHUNKS, part, rows)
    start = jnp.where(core == 0, start[:, 0], start[:, 1])
    start = start.transpose(1, 0, 2, 3).reshape(CHUNKS, wide, rows)

    saved = [
        jnp.zeros((CORES, CHUNKS + 1, tiles + 1, wide, rows), jnp.float32) for _ in range(layers)
    ]
    fields = []
    leaving = []

    def finish(layer):
        shape = (1, CHUNKS, tiles + 1, wide, rows)
        send = lax.dynamic_slice(saved[layer], (1 - core, 0, 0, 0, 0), shape)
        other = lax.ppermute(send, "layer", partner)
        fields[:] = [
            layer_fields(
                core_arg, saved[layer], other, cosines[layer], sines[layer], eigvec, layer, fields
            )
        ]
        shape = (1, CHUNKS, 1, wide, rows)
        own_leave = lax.dynamic_slice(saved[layer], (core, 0, tiles, 0, 0), shape)
        other_leave = other[:, :, tiles:]
        leave = jnp.concatenate(
            [
                jnp.where(core == 0, own_leave, other_leave),
                jnp.where(core == 0, other_leave, own_leave),
            ]
        ).reshape(CORES, CHUNKS, 2, part, rows)
        leaving.append(leave.transpose(4, 2, 0, 1, 3).reshape(rows, width))

    received = None
    for tick in range(stages + CHUNKS - 1):
        inbox = start[min(tick, CHUNKS - 1)]
        if tick > 0:
            inbox = jnp.where(stage == 0, inbox, received)
        slot = tick - stage
        slot = jnp.where((slot >= 0) & (slot < CHUNKS), slot, CHUNKS)
        spread = jnp.broadcast_to(inbox[None], (tiles, wide, rows))
        for layer in range(CORES * layers):
            own, half = layer % layers, layer // layers
            full = to_all(spread)
            if tick == 0 and layer < layers:
                others = (narrow(arrived[layer], layer, layers, others + (spread,) * layer),)
            spread = layer_step(core_arg, full, whole, interface, others[0], half, own, layer)
            place = (half, slot, 0, 0, 0)
            saved[own] = lax.dynamic_update_slice(saved[own], full[None, None], place)
            place = (half, slot, tiles, 0, 0)
            saved[own] = lax.dynamic_update_slice(saved[own], spread[None, None, :1], place)
        received = lax.ppermute(spread[0], "layer", ring)

    finish(0)
    finish(1)
    return fields[0], jnp.stack(leaving)


def solution(mesh):
    in_specs = (
        P("tile", None),
        P("layer", "tile", None),
        P("layer", "tile", None),
        P("layer", None),
        P("layer", None),
    )
    out_specs = (P("layer", "tile", None), P("layer", "tile", None))
    return jax.shard_map(
        on_device, mesh=mesh, in_specs=in_specs, out_specs=out_specs, check_vma=False
    )
```

profile of v0, /device:TPU:25, one launch (start us, length us, event | category | flops | bytes accessed | tf_op | source)
XLA Modules:
  0.0 722.2 jit_solution(12089547620734367730)
XLA Ops:
  1.5 7.3 %shard_map.68.after_ref = f32[512,4096]{1,0:T(8,128)} custom-call(bf16[2,512,4096]{2,1,0:T(8,128)(2,1)} %own_ref.71, bf16[512,128]{1,0:T(8,128)(2,1)S(1)} %copy-done.7), custom_call_target="tpu_custom_call" | custom-call | tf_op jit(solution)/shard_map/pallas_call | solution.py:27
  9.5 7.3 %shard_map.71 = f32[512,4096]{1,0:T(8,128)} custom-call(bf16[2,512,4096]{2,1,0:T(8,128)(2,1)} %own_ref.71, f32[512,4096]{1,0:T(8,128)} %shard_map.68.after_ref), custom_call_target="tpu_custom_call" | custom-call | tf_op jit(solution)/shard_map/pallas_call | solution.py:27
  19.6 7.3 %all-to-all-start = ((f32[8,32,512]{2,1,0:T(8,128)}), f32[8,32,512]{2,1,0:T(8,128)S(1)}, u32[]{:S(2)}, u32[]{:S(2)}) async-start(f32[8,32,512]{2,1,0:T(8,128)} %broadcast_in_dim.272), calls=%async_computation | async-start | bytes 1048576 | tf_op jit(solution)/shard_map/all_to_all | solution.py:188
  27.3 7.7 %shard_map.69.other_ref.refs_0_ = bf16[2,512,4096]{2,1,0:T(8,128)(2,1)} custom-call(f32[512,4096]{1,0:T(8,128)} %collective-permute-done.1.mat_ref), custom_call_target="tpu_custom_call" | custom-call | tf_op jit(solution)/shard_map/pallas_call | solution.py:44
  41.0 4.2 all-to-all-start.1
  45.2 7.7 %shard_map.72.other_ref = bf16[2,512,4096]{2,1,0:T(8,128)(2,1)} custom-call(f32[512,4096]{1,0:T(8,128)} %collective-permute-done.2.mat_ref, bf16[2,512,4096]{2,1,0:T(8,128)(2,1)} %shard_map.69.other_ref.refs_0_, f32[8,32,512]{2,1,0:T(8,128)} %shard_map.70.refs_1_), custom_call_target="tpu_custom_call", output_to_operand_aliasing={{}: (1, {})} | custom-call | tf_op jit(solution)/shard_map/pallas_call | solution.py:44
  59.2 13.1 %all_to_all.180.full_ref = f32[8,32,512]{2,1,0:T(8,128)S(1)} all-to-all(f32[8,32,512]{2,1,0:T(8,128)S(1)} %shard_map.73), channel_id=1, replica_groups=mesh['layer'=16,'tile'=8] {'tile'}, dimensions={0} | all-to-all | bytes 1048576 | tf_op jit(solution)/shard_map/all_to_all | solution.py:188
  75.0 11.7 %all_to_all.181.full_ref = f32[8,32,512]{2,1,0:T(8,128)S(1)} all-to-all(f32[8,32,512]{2,1,0:T(8,128)S(1)} %shard_map.74), channel_id=1, replica_groups=mesh['layer'=16,'tile'=8] {'tile'}, dimensions={0} | all-to-all | bytes 1048576 | tf_op jit(solution)/shard_map/all_to_all | solution.py:188
  101.3 5.2 all-to-all-done.4.full_ref
  131.4 6.1 all-to-all-done.6.full_ref
  145.9 7.0 all-to-all-done.7.full_ref
  166.8 6.2 all-to-all-done.8.full_ref
  182.5 6.1 all-to-all-done.9.full_ref
  198.0 6.1 all-to-all-done.10.full_ref
  213.5 6.7 all-to-all-done.11.full_ref
  228.0 4.2 all-to-all-start.12
  234.5 6.2 all-to-all-done.12.full_ref
  250.2 6.1 all-to-all-done.13.full_ref
  265.6 6.1 all-to-all-done.14.full_ref
  280.3 7.0 all-to-all-done.15.full_ref
  301.2 6.3 all-to-all-done.16.full_ref
  316.9 6.1 all-to-all-done.17.full_ref
  331.5 7.0 all-to-all-done.18.full_ref
  347.9 6.1 all-to-all-done.19.full_ref
  362.3 4.9 all-to-all-start.20
  369.6 6.1 all-to-all-done.20.full_ref
  385.1 6.1 all-to-all-done.21.full_ref
  399.7 7.0 all-to-all-done.22.full_ref
  416.1 6.1 all-to-all-done.23.full_ref
  425.0 5.8 collective-permute-start.8
  433.1 4.5 all-to-all-start.24
  439.9 6.3 all-to-all-done.24.full_ref
  449.7 5.1 all-to-all-start.25
  456.3 7.2 all-to-all-done.25.full_ref
  467.0 5.2 all-to-all-start.26
  474.5 6.2 all-to-all-done.26.full_ref
  490.1 6.1 all-to-all-done.27.full_ref
  510.0 6.1 all-to-all-done.28.full_ref
  524.7 7.0 all-to-all-done.29.full_ref
  541.0 6.2 all-to-all-done.30.full_ref
  556.9 8.2 %all-to-all-done.31.full_ref = f32[8,32,512]{2,1,0:T(8,128)S(1)} async-done(((f32[8,32,512]{2,1,0:T(8,128)}), f32[8,32,512]{2,1,0:T(8,128)S(1)}, u32[]{:S(2)}, u32[]{:S(2)}) %all-to-all-start.31) | async-done | bytes 524320 | tf_op jit(solution)/shard_map/all_to_all | solution.py:188
  577.8 7.4 %all-to-all-done.32.full_ref = f32[8,32,512]{2,1,0:T(8,128)S(1)} async-done(((f32[8,32,512]{2,1,0:T(8,128)}), f32[8,32,512]{2,1,0:T(8,128)S(1)}, u32[]{:S(2)}, u32[]{:S(2)}) %all-to-all-start.32) | async-done | bytes 524320 | tf_op jit(solution)/shard_map/all_to_all | solution.py:188
  594.6 8.1 %all-to-all-done.33.full_ref = f32[8,32,512]{2,1,0:T(8,128)S(1)} async-done(((f32[8,32,512]{2,1,0:T(8,128)}), f32[8,32,512]{2,1,0:T(8,128)S(1)}, u32[]{:S(2)}, u32[]{:S(2)}) %all-to-all-start.33) | async-done | bytes 524320 | tf_op jit(solution)/shard_map/all_to_all | solution.py:188
  612.1 7.9 %all-to-all-done.34.full_ref = f32[8,32,512]{2,1,0:T(8,128)S(1)} async-done(((f32[8,32,512]{2,1,0:T(8,128)}), f32[8,32,512]{2,1,0:T(8,128)S(1)}, u32[]{:S(2)}, u32[]{:S(2)}) %all-to-all-start.34) | async-done | bytes 524320 | tf_op jit(solution)/shard_map/all_to_all | solution.py:188
  632.1 57.3 %collective-permute-start.12 = (f32[1,2,9,32,512]{4,3,2,1,0:T(8,128)}, f32[1,2,9,32,512]{4,3,2,1,0:T(8,128)S(1)}, u32[]{:S(2)}, u32[]{:S(2)}) collective-permute-start(f32[1,2,9,32,512]{4,3,2,1,0:T(8,128)} %constant_dynamic-slice_fusion), channel_id=1, source_target_pairs={{0,8},{8,0},{16,24},{24,16},{32,40},{40,32},{48,56},{56,48},{64,72... | collective-permute-start | bytes 3538952 | tf_op jit(solution)/shard_map/ppermute | solution.py:237
  696.1 4.7 collective-permute-start.11
  703.0 8.4 %shard_map.108.refs_0_ = bf16[2,512,512]{2,1,0:T(8,128)(2,1)} custom-call(s32[1]{0:T(128)} %bitcast.core_ref, f32[2,3,9,32,512]{4,3,2,1,0:T(8,128)} %fusion.6.own_ref, f32[1,2,9,32,512]{4,3,2,1,0:T(8,128)S(1)} %collective-permute-done.12.other_ref, f32[8,4,512]{2,1,0:T(4,128)S(1)} %get-tuple-element.25.cos_ref, f32[8,4,512]{2,1,0:T(4,128)S(1)} %get-tuple-element.8.sin_ref, ...), custom_call_target="tpu_custom_call" | custom-call | tf_op jit(solution)/shard_map/pallas_call | solution.py:165
  713.4 8.3 %shard_map.109 = bf16[2,512,512]{2,1,0:T(8,128)(2,1)} custom-call(s32[1]{0:T(128)} %bitcast.core_ref, f32[2,3,9,32,512]{4,3,2,1,0:T(8,128)} %fusion.24.own_ref, f32[1,2,9,32,512]{4,3,2,1,0:T(8,128)S(1)} %collective-permute-done.11.other_ref, f32[8,4,512]{2,1,0:T(4,128)S(1)} %get-tuple-element.24.cos_ref, ...), custom_call_target="tpu_custom_call", output_to_operand_aliasing={{}: (6, {})} | custom-call | tf_op jit(solution)/shard_map/pallas_call | solution.py:165
  (236 shorter events, 349.5 us)
Async XLA Ops:
  8.8 18.4 %collective-permute-start.1 = (f32[512,4096]{1,0:T(8,128)}, f32[512,4096]{1,0:T(8,128)}, u32[]{:S(2)}, u32[]{:S(2)}) collective-permute-start(f32[512,4096]{1,0:T(8,128)} %shard_map.68.after_ref), channel_id=1, source_target_pairs={{0,8},{8,0},{16,24},{24,16},{32,40},{40,32},{48,56},{56,48},{64,72... | collective-permute-start | bytes 25165832 | tf_op jit(solution)/shard_map/ppermute | solution.py:212
  16.8 28.3 %collective-permute-start.2 = (f32[512,4096]{1,0:T(8,128)}, f32[512,4096]{1,0:T(8,128)}, u32[]{:S(2)}, u32[]{:S(2)}) collective-permute-start(f32[512,4096]{1,0:T(8,128)} %shard_map.71), channel_id=1, source_target_pairs={{0,8},{8,0},{16,24},{24,16},{32,40},{40,32},{48,56},{56,48},{64,72... | collective-permute-start | bytes 25165832 | tf_op jit(solution)/shard_map/ppermute | solution.py:212
  18.1 8.9 %collective-permute-start = (f32[2,2,8,512]{3,2,1,0:T(8,128)S(1)}, f32[2,2,8,512]{3,2,1,0:T(8,128)S(1)}, u32[]{:S(2)}, u32[]{:S(2)}) collective-permute-start(f32[2,2,8,512]{3,2,1,0:T(8,128)S(1)} %get-tuple-element.21), channel_id=1, source_target_pairs={{0,8},{8,0},{16,24},{24,16},{32,40},{40,32},{48,56},{56,48},{64,72... | collective-permute-start | bytes 196616 | tf_op jit(solution)/shard_map/ppermute | solution.py:207
  19.6 17.8 %all-to-all-start = ((f32[8,32,512]{2,1,0:T(8,128)}), f32[8,32,512]{2,1,0:T(8,128)S(1)}, u32[]{:S(2)}, u32[]{:S(2)}) async-start(f32[8,32,512]{2,1,0:T(8,128)} %broadcast_in_dim.272), calls=%async_computation | async-start | bytes 1048576 | tf_op jit(solution)/shard_map/all_to_all | solution.py:188
  41.0 14.7 %all-to-all-start.1 = ((f32[8,32,512]{2,1,0:T(8,128)}), f32[8,32,512]{2,1,0:T(8,128)S(1)}, u32[]{:S(2)}, u32[]{:S(2)}) async-start(f32[8,32,512]{2,1,0:T(8,128)} %shard_map.70.refs_1_), calls=%async_computation.1 | async-start | bytes 1048576 | tf_op jit(solution)/shard_map/all_to_all | solution.py:188
  89.5 4.1 collective-permute-start.3
  94.5 11.9 %all-to-all-start.4 = ((f32[8,32,512]{2,1,0:T(8,128)}), f32[8,32,512]{2,1,0:T(8,128)S(1)}, u32[]{:S(2)}, u32[]{:S(2)}) async-start(f32[8,32,512]{2,1,0:T(8,128)} %broadcast_in_dim.277), calls=%async_computation.4 | async-start | bytes 1048576 | tf_op jit(solution)/shard_map/all_to_all | solution.py:188
  110.0 11.9 %all-to-all-start.5 = ((f32[8,32,512]{2,1,0:T(8,128)}), f32[8,32,512]{2,1,0:T(8,128)S(1)}, u32[]{:S(2)}, u32[]{:S(2)}) async-start(f32[8,32,512]{2,1,0:T(8,128)} %copy-done.1), calls=%async_computation.5 | async-start | bytes 1048576 | tf_op jit(solution)/shard_map/all_to_all | solution.py:188
  125.5 11.9 %all-to-all-start.6 = ((f32[8,32,512]{2,1,0:T(8,128)}), f32[8,32,512]{2,1,0:T(8,128)S(1)}, u32[]{:S(2)}, u32[]{:S(2)}) async-start(f32[8,32,512]{2,1,0:T(8,128)} %copy-done.2), calls=%async_computation.6 | async-start | bytes 1048576 | tf_op jit(solution)/shard_map/all_to_all | solution.py:188
  141.0 11.9 %all-to-all-start.7 = ((f32[8,32,512]{2,1,0:T(8,128)}), f32[8,32,512]{2,1,0:T(8,128)S(1)}, u32[]{:S(2)}, u32[]{:S(2)}) async-start(f32[8,32,512]{2,1,0:T(8,128)} %copy-done.3), calls=%async_computation.7 | async-start | bytes 1048576 | tf_op jit(solution)/shard_map/all_to_all | solution.py:188
  155.6 11.1 %copy-start.6 = (f32[8,32,512]{2,1,0:T(8,128)}, f32[8,32,512]{2,1,0:T(8,128)S(1)}, u32[]{:S(2)}) copy-start(f32[8,32,512]{2,1,0:T(8,128)S(1)} %shard_map.79) | copy-start | bytes 1572868
  155.7 4.4 collective-permute-start.4
  160.9 12.0 %all-to-all-start.8 = ((f32[8,32,512]{2,1,0:T(8,128)}), f32[8,32,512]{2,1,0:T(8,128)S(1)}, u32[]{:S(2)}, u32[]{:S(2)}) async-start(f32[8,32,512]{2,1,0:T(8,128)} %broadcast_in_dim.282), calls=%async_computation.8 | async-start | bytes 1048576 | tf_op jit(solution)/shard_map/all_to_all | solution.py:188
  176.5 12.1 %all-to-all-start.9 = ((f32[8,32,512]{2,1,0:T(8,128)}), f32[8,32,512]{2,1,0:T(8,128)S(1)}, u32[]{:S(2)}, u32[]{:S(2)}) async-start(f32[8,32,512]{2,1,0:T(8,128)} %copy-done.4), calls=%async_computation.9 | async-start | bytes 1048576 | tf_op jit(solution)/shard_map/all_to_all | solution.py:188
  192.1 12.0 %all-to-all-start.10 = ((f32[8,32,512]{2,1,0:T(8,128)}), f32[8,32,512]{2,1,0:T(8,128)S(1)}, u32[]{:S(2)}, u32[]{:S(2)}) async-start(f32[8,32,512]{2,1,0:T(8,128)} %shard_map.81), calls=%async_computation.10 | async-start | bytes 1048576 | tf_op jit(solution)/shard_map/all_to_all | solution.py:188
  207.6 12.5 %all-to-all-start.11 = ((f32[8,32,512]{2,1,0:T(8,128)}), f32[8,32,512]{2,1,0:T(8,128)S(1)}, u32[]{:S(2)}, u32[]{:S(2)}) async-start(f32[8,32,512]{2,1,0:T(8,128)} %shard_map.82), calls=%async_computation.11 | async-start | bytes 1048576 | tf_op jit(solution)/shard_map/all_to_all | solution.py:188
  222.9 4.2 collective-permute-start.5
  228.0 12.7 %all-to-all-start.12 = ((f32[8,32,512]{2,1,0:T(8,128)}), f32[8,32,512]{2,1,0:T(8,128)S(1)}, u32[]{:S(2)}, u32[]{:S(2)}) async-start(f32[8,32,512]{2,1,0:T(8,128)} %broadcast_in_dim.287), calls=%async_computation.12 | async-start | bytes 1048576 | tf_op jit(solution)/shard_map/all_to_all | solution.py:188
  244.3 12.0 %all-to-all-start.13 = ((f32[8,32,512]{2,1,0:T(8,128)}), f32[8,32,512]{2,1,0:T(8,128)S(1)}, u32[]{:S(2)}, u32[]{:S(2)}) async-start(f32[8,32,512]{2,1,0:T(8,128)} %shard_map.84), calls=%async_computation.13 | async-start | bytes 1048576 | tf_op jit(solution)/shard_map/all_to_all | solution.py:188
  259.8 12.0 %all-to-all-start.14 = ((f32[8,32,512]{2,1,0:T(8,128)}), f32[8,32,512]{2,1,0:T(8,128)S(1)}, u32[]{:S(2)}, u32[]{:S(2)}) async-start(f32[8,32,512]{2,1,0:T(8,128)} %shard_map.85), calls=%async_computation.14 | async-start | bytes 1048576 | tf_op jit(solution)/shard_map/all_to_all | solution.py:188
  275.3 12.0 %all-to-all-start.15 = ((f32[8,32,512]{2,1,0:T(8,128)}), f32[8,32,512]{2,1,0:T(8,128)S(1)}, u32[]{:S(2)}, u32[]{:S(2)}) async-start(f32[8,32,512]{2,1,0:T(8,128)} %shard_map.86), calls=%async_computation.15 | async-start | bytes 1048576 | tf_op jit(solution)/shard_map/all_to_all | solution.py:188
  290.0 4.4 collective-permute-start.6
  295.3 12.2 %all-to-all-start.16 = ((f32[8,32,512]{2,1,0:T(8,128)}), f32[8,32,512]{2,1,0:T(8,128)S(1)}, u32[]{:S(2)}, u32[]{:S(2)}) async-start(f32[8,32,512]{2,1,0:T(8,128)} %broadcast_in_dim.292), calls=%async_computation.16 | async-start | bytes 1048576 | tf_op jit(solution)/shard_map/all_to_all | solution.py:188
  311.0 12.0 %all-to-all-start.17 = ((f32[8,32,512]{2,1,0:T(8,128)}), f32[8,32,512]{2,1,0:T(8,128)S(1)}, u32[]{:S(2)}, u32[]{:S(2)}) async-start(f32[8,32,512]{2,1,0:T(8,128)} %shard_map.88), calls=%async_computation.17 | async-start | bytes 1048576 | tf_op jit(solution)/shard_map/all_to_all | solution.py:188
  326.5 12.0 %all-to-all-start.18 = ((f32[8,32,512]{2,1,0:T(8,128)}), f32[8,32,512]{2,1,0:T(8,128)S(1)}, u32[]{:S(2)}, u32[]{:S(2)}) async-start(f32[8,32,512]{2,1,0:T(8,128)} %shard_map.89), calls=%async_computation.18 | async-start | bytes 1048576 | tf_op jit(solution)/shard_map/all_to_all | solution.py:188
  342.0 12.0 %all-to-all-start.19 = ((f32[8,32,512]{2,1,0:T(8,128)}), f32[8,32,512]{2,1,0:T(8,128)S(1)}, u32[]{:S(2)}, u32[]{:S(2)}) async-start(f32[8,32,512]{2,1,0:T(8,128)} %shard_map.90), calls=%async_computation.19 | async-start | bytes 1048576 | tf_op jit(solution)/shard_map/all_to_all | solution.py:188
  356.7 4.7 collective-permute-start.7
  362.3 13.4 %all-to-all-start.20 = ((f32[8,32,512]{2,1,0:T(8,128)}), f32[8,32,512]{2,1,0:T(8,128)S(1)}, u32[]{:S(2)}, u32[]{:S(2)}) async-start(f32[8,32,512]{2,1,0:T(8,128)} %broadcast_in_dim.297), calls=%async_computation.20 | async-start | bytes 1048576 | tf_op jit(solution)/shard_map/all_to_all | solution.py:188
  379.2 12.0 %all-to-all-start.21 = ((f32[8,32,512]{2,1,0:T(8,128)}), f32[8,32,512]{2,1,0:T(8,128)S(1)}, u32[]{:S(2)}, u32[]{:S(2)}) async-start(f32[8,32,512]{2,1,0:T(8,128)} %shard_map.92), calls=%async_computation.21 | async-start | bytes 1048576 | tf_op jit(solution)/shard_map/all_to_all | solution.py:188
  394.7 12.0 %all-to-all-start.22 = ((f32[8,32,512]{2,1,0:T(8,128)}), f32[8,32,512]{2,1,0:T(8,128)S(1)}, u32[]{:S(2)}, u32[]{:S(2)}) async-start(f32[8,32,512]{2,1,0:T(8,128)} %shard_map.93), calls=%async_computation.22 | async-start | bytes 1048576 | tf_op jit(solution)/shard_map/all_to_all | solution.py:188
  410.3 12.0 %all-to-all-start.23 = ((f32[8,32,512]{2,1,0:T(8,128)}), f32[8,32,512]{2,1,0:T(8,128)S(1)}, u32[]{:S(2)}, u32[]{:S(2)}) async-start(f32[8,32,512]{2,1,0:T(8,128)} %shard_map.94), calls=%async_computation.23 | async-start | bytes 1048576 | tf_op jit(solution)/shard_map/all_to_all | solution.py:188
  425.0 7.2 %collective-permute-start.8 = (f32[32,512]{1,0:T(8,128)S(1)}, f32[32,512]{1,0:T(8,128)S(1)}, u32[]{:S(2)}, u32[]{:S(2)}) collective-permute-start(f32[32,512]{1,0:T(8,128)S(1)} %slice_bitcast_fusion.34), channel_id=1, source_target_pairs={{0,16},{8,24},{16,32},{24,40},{32,48},{40,56},{48,64},{56,72},{64,... | collective-permute-start | bytes 196616 | tf_op jit(solution)/shard_map/ppermute | solution.py:272
  433.1 13.1 %all-to-all-start.24 = ((f32[8,32,512]{2,1,0:T(8,128)}), f32[8,32,512]{2,1,0:T(8,128)S(1)}, u32[]{:S(2)}, u32[]{:S(2)}) async-start(f32[8,32,512]{2,1,0:T(8,128)} %broadcast_in_dim.302), calls=%async_computation.24 | async-start | bytes 1048576 | tf_op jit(solution)/shard_map/all_to_all | solution.py:188
  449.7 13.8 %all-to-all-start.25 = ((f32[8,32,512]{2,1,0:T(8,128)}), f32[8,32,512]{2,1,0:T(8,128)S(1)}, u32[]{:S(2)}, u32[]{:S(2)}) async-start(f32[8,32,512]{2,1,0:T(8,128)} %shard_map.96), calls=%async_computation.25 | async-start | bytes 1048576 | tf_op jit(solution)/shard_map/all_to_all | solution.py:188
  467.0 13.7 %all-to-all-start.26 = ((f32[8,32,512]{2,1,0:T(8,128)}), f32[8,32,512]{2,1,0:T(8,128)S(1)}, u32[]{:S(2)}, u32[]{:S(2)}) async-start(f32[8,32,512]{2,1,0:T(8,128)} %shard_map.97), calls=%async_computation.26 | async-start | bytes 1048576 | tf_op jit(solution)/shard_map/all_to_all | solution.py:188
  484.3 12.0 %all-to-all-start.27 = ((f32[8,32,512]{2,1,0:T(8,128)}), f32[8,32,512]{2,1,0:T(8,128)S(1)}, u32[]{:S(2)}, u32[]{:S(2)}) async-start(f32[8,32,512]{2,1,0:T(8,128)} %shard_map.98), calls=%async_computation.27 | async-start | bytes 1048576 | tf_op jit(solution)/shard_map/all_to_all | solution.py:188
  499.0 4.4 collective-permute-start.9
  504.2 11.9 %all-to-all-start.28 = ((f32[8,32,512]{2,1,0:T(8,128)}), f32[8,32,512]{2,1,0:T(8,128)S(1)}, u32[]{:S(2)}, u32[]{:S(2)}) async-start(f32[8,32,512]{2,1,0:T(8,128)} %broadcast_in_dim.307), calls=%async_computation.28 | async-start | bytes 1048576 | tf_op jit(solution)/shard_map/all_to_all | solution.py:188
  519.7 12.0 %all-to-all-start.29 = ((f32[8,32,512]{2,1,0:T(8,128)}), f32[8,32,512]{2,1,0:T(8,128)S(1)}, u32[]{:S(2)}, u32[]{:S(2)}) async-start(f32[8,32,512]{2,1,0:T(8,128)} %shard_map.100), calls=%async_computation.29 | async-start | bytes 1048576 | tf_op jit(solution)/shard_map/all_to_all | solution.py:188
  535.2 12.1 %all-to-all-start.30 = ((f32[8,32,512]{2,1,0:T(8,128)}), f32[8,32,512]{2,1,0:T(8,128)S(1)}, u32[]{:S(2)}, u32[]{:S(2)}) async-start(f32[8,32,512]{2,1,0:T(8,128)} %shard_map.101), calls=%async_computation.30 | async-start | bytes 1048576 | tf_op jit(solution)/shard_map/all_to_all | solution.py:188
  550.8 14.2 %all-to-all-start.31 = ((f32[8,32,512]{2,1,0:T(8,128)}), f32[8,32,512]{2,1,0:T(8,128)S(1)}, u32[]{:S(2)}, u32[]{:S(2)}) async-start(f32[8,32,512]{2,1,0:T(8,128)} %shard_map.102), calls=%async_computation.31 | async-start | bytes 1048576 | tf_op jit(solution)/shard_map/all_to_all | solution.py:188
  567.8 4.1 collective-permute-start.10
  572.7 12.5 %all-to-all-start.32 = ((f32[8,32,512]{2,1,0:T(8,128)}), f32[8,32,512]{2,1,0:T(8,128)S(1)}, u32[]{:S(2)}, u32[]{:S(2)}) async-start(f32[8,32,512]{2,1,0:T(8,128)} %broadcast_in_dim.312), calls=%async_computation.32 | async-start | bytes 1048576 | tf_op jit(solution)/shard_map/all_to_all | solution.py:188
  588.7 14.0 %all-to-all-start.33 = ((f32[8,32,512]{2,1,0:T(8,128)}), f32[8,32,512]{2,1,0:T(8,128)S(1)}, u32[]{:S(2)}, u32[]{:S(2)}) async-start(f32[8,32,512]{2,1,0:T(8,128)} %shard_map.104), calls=%async_computation.33 | async-start | bytes 1048576 | tf_op jit(solution)/shard_map/all_to_all | solution.py:188
  606.2 13.7 %all-to-all-start.34 = ((f32[8,32,512]{2,1,0:T(8,128)}), f32[8,32,512]{2,1,0:T(8,128)S(1)}, u32[]{:S(2)}, u32[]{:S(2)}) async-start(f32[8,32,512]{2,1,0:T(8,128)} %shard_map.105), calls=%async_computation.34 | async-start | bytes 1048576 | tf_op jit(solution)/shard_map/all_to_all | solution.py:188
  623.5 65.9 %all-to-all-start.35 = ((f32[8,32,512]{2,1,0:T(8,128)}), f32[8,32,512]{2,1,0:T(8,128)S(1)}, u32[]{:S(2)}, u32[]{:S(2)}) async-start(f32[8,32,512]{2,1,0:T(8,128)} %shard_map.106), calls=%async_computation.35 | async-start | bytes 1048576 | tf_op jit(solution)/shard_map/all_to_all | solution.py:188
  632.1 69.9 %collective-permute-start.12 = (f32[1,2,9,32,512]{4,3,2,1,0:T(8,128)}, f32[1,2,9,32,512]{4,3,2,1,0:T(8,128)S(1)}, u32[]{:S(2)}, u32[]{:S(2)}) collective-permute-start(f32[1,2,9,32,512]{4,3,2,1,0:T(8,128)} %constant_dynamic-slice_fusion), channel_id=1, source_target_pairs={{0,8},{8,0},{16,24},{24,16},{32,40},{40,32},{48,56},{56,48},{64,72... | collective-permute-start | bytes 3538952 | tf_op jit(solution)/shard_map/ppermute | solution.py:237
  696.1 15.3 %collective-permute-start.11 = (f32[1,2,9,32,512]{4,3,2,1,0:T(8,128)}, f32[1,2,9,32,512]{4,3,2,1,0:T(8,128)S(1)}, u32[]{:S(2)}, u32[]{:S(2)}) collective-permute-start(f32[1,2,9,32,512]{4,3,2,1,0:T(8,128)} %constant_dynamic-slice_fusion.1), channel_id=1, source_target_pairs={{0,8},{8,0},{16,24},{24,16},{32,40},{40,32},{48,56},{56,48},{64,72... | collective-permute-start | bytes 3538952 | tf_op jit(solution)/shard_map/ppermute | solution.py:237
  (11 other events, 44.0 us)
where the time goes:
time: 736 us; the launch traced here: 722 us
  waiting for transfers between devices  222 us (30%)
  starting transfers between devices  206 us (28%)
  Pallas kernels  162 us (22%)
  local copies, waits for them, and re-layouts  102 us (14%)
  blocking collectives  24.8 us (3%)
    all_to_all x34, waiting for transfers between devices, to_all(): lax.all_to_all(block, 'tile', split_axis=0, concat_axis=0, tiled=False)  205 us
    all_to_all x34, starting transfers between devices, to_all(): lax.all_to_all(block, 'tile', split_axis=0, concat_axis=0, tiled=False)  131 us
    pallas_call x36, Pallas kernels, layer_step(): pl.pallas_call(functools.partial(step_kernel, half=half, layer=layer, num...  115 us
    ppermute x2, starting transfers between devices, finish(): other = lax.ppermute(send, 'layer', partner)  62 us
    dynamic_update_slice x36, local copies, waits for them, and re-layouts, on_device(): lax.dynamic_update_slice(saved[own], spread[None, None, :1], place)  46.2 us
    dynamic_update_slice x36, local copies, waits for them, and re-layouts, on_device(): saved[own] = lax.dynamic_update_slice(saved[own], full[None, None], place)  31.2 us
    all_to_all x2, blocking collectives, to_all(): lax.all_to_all(block, 'tile', split_axis=0, concat_axis=0, tiled=False)  24.8 us
    ppermute x8, waiting for transfers between devices, on_device(): received = lax.ppermute(spread[0], 'layer', ring)  17.1 us
  transfers between devices with their start and end apart: 47, of which 40 were waited for; matrix products, arithmetic and copies ran while one was open for 13% of the time, Pallas kernels for 5%

commit v1 on v0

v1 whole, which is shorter than its diff:
```python
import functools

import jax
import jax.numpy as jnp
from jax import lax
from jax.experimental import pallas as pl
from jax.experimental.pallas import tpu as pltpu
from jax.sharding import PartitionSpec as P

DEPTHS = 4
CHUNKS = 2
CORES = 2
PARTS = 2
PIECES = 4
GATHERED = 2
SLOTS = 32
NT = (((1,), (1,)), ((), ()))
VMEM = pl.BlockSpec(memory_space=pltpu.VMEM)
SMEM = pl.BlockSpec(memory_space=pltpu.SMEM)
ANYWHERE = pl.BlockSpec(memory_space=pl.ANY)
PARAMS = pltpu.CompilerParams(vmem_limit_bytes=48 * 1024 * 1024)


def widen_kernel(mat_ref, after_ref, out_ref):
    out_ref[...] = mat_ref[0].astype(jnp.float32)


def widen(mats, layer, part, after):
    rows, orders = mats.shape[1:]
    height = rows // PARTS
    piece = height // PIECES
    return pl.pallas_call(
        widen_kernel,
        out_shape=jax.ShapeDtypeStruct((height, orders), jnp.float32),
        grid=(PIECES,),
        in_specs=[
            pl.BlockSpec((1, piece, orders), lambda p: (layer, part * PIECES + p, 0)),
            ANYWHERE,
        ],
        out_specs=pl.BlockSpec((piece, orders), lambda p: (p, 0)),
        compiler_params=PARAMS,
    )(mats, after)


def narrow_kernel(mat_ref, *refs):
    refs[-1][0] = mat_ref[...].astype(jnp.bfloat16)


def narrow(mat, layer, part, layers, before):
    height, orders = mat.shape
    piece = height // PIECES
    return pl.pallas_call(
        narrow_kernel,
        out_shape=jax.ShapeDtypeStruct((layers, height * PARTS, orders), jnp.bfloat16),
        grid=(PIECES,),
        in_specs=[pl.BlockSpec((piece, orders), lambda p: (p, 0))] + [ANYWHERE] * len(before),
        out_specs=pl.BlockSpec((1, piece, orders), lambda p: (layer, part * PIECES + p, 0)),
        input_output_aliases={1: 0} if before else {},
        compiler_params=PARAMS,
    )(mat, *before)


def step_kernel(
    plan_ref, full_ref, phase_ref, own_ref, other_ref, saved_in,
    out_ref, saved_ref, row_buf, mat_buf, sum_buf, row_sem, sems, save_sems,
    *, tick, half, layer, number
):
    blocks, wide, rows = full_ref.shape
    split = wide // 2
    core, valid, slot = plan_ref[tick, 0], plan_ref[tick, 1], plan_ref[tick, 2 + number]
    row_copy = pltpu.make_async_copy(phase_ref.at[number], row_buf, row_sem)
    row_copy.start()

    def copies(mats_ref):
        return [
            pltpu.make_async_copy(
                mats_ref.at[layer, :, pl.ds(b * rows, rows)], mat_buf.at[b], sems.at[b]
            )
            for b in range(blocks)
        ]

    @pl.when(core == half)
    def _():
        for copy in copies(own_ref):
            copy.start()

    @pl.when(core != half)
    def _():
        for copy in copies(other_ref):
            copy.start()

    block_save = pltpu.make_async_copy(
        full_ref, saved_ref.at[slot, pl.ds(0, blocks)], save_sems.at[0]
    )
    sum_save = pltpu.make_async_copy(sum_buf, saved_ref.at[slot, blocks], save_sems.at[1])

    @pl.when(valid == 1)
    def _():
        block_save.start()

    arrivals = copies(own_ref)
    total = jnp.zeros((wide, rows), jnp.float32)
    row_copy.wait()
    for b in range(blocks):
        cosine = row_buf[0, b : b + 1, :]
        sine = row_buf[1, b : b + 1, :]
        real_part = full_ref[b, :split, :]
        imag_part = full_ref[b, split:, :]
        phased = jnp.concatenate(
            [cosine * real_part - sine * imag_part, sine * real_part + cosine * imag_part], axis=0
        ).astype(jnp.bfloat16)
        arrivals[b].wait()
        total += lax.dot_general(phased, mat_buf[b], NT, preferred_element_type=jnp.float32)
    sum_buf[...] = total


    @pl.when(valid == 1)
    def _():
        sum_save.start()

    for b in range(blocks):
        out_ref[b] = total

    @pl.when(valid == 1)
    def _():
        block_save.wait()
        sum_save.wait()


def allocate_kernel(out_ref):
    pass


def allocate(shape):
    return pl.pallas_call(
        allocate_kernel,
        out_shape=jax.ShapeDtypeStruct(shape, jnp.float32),
        in_specs=[],
        out_specs=ANYWHERE,
        compiler_params=PARAMS,
    )()


def layer_step(plan, full, phases, own, other, saved, tick, half, layer, number):
    blocks, wide, rows = full.shape
    return pl.pallas_call(
        functools.partial(
            step_kernel, tick=tick, half=half, layer=layer, number=number
        ),
        out_shape=(
            jax.ShapeDtypeStruct(full.shape, jnp.float32),
            jax.ShapeDtypeStruct(saved.shape, jnp.float32),
        ),
        in_specs=[SMEM, VMEM] + [ANYWHERE] * 4,
        out_specs=(VMEM, ANYWHERE),
        input_output_aliases={5: 1},
        scratch_shapes=[
            pltpu.VMEM(phases.shape[1:], jnp.float32),
            pltpu.VMEM((blocks, rows, rows), jnp.bfloat16),
            pltpu.VMEM((wide, rows), jnp.float32),
            pltpu.SemaphoreType.DMA,
            pltpu.SemaphoreType.DMA((blocks,)),
            pltpu.SemaphoreType.DMA((2,)),
        ],
        compiler_params=PARAMS,
        cost_estimate=pl.CostEstimate(
            flops=2 * wide * rows * rows * blocks,
            bytes_accessed=2 * blocks * rows * rows,
            transcendentals=0,
        ),
    )(plan, full, phases, own, other, saved)


def fields_kernel(
    core_ref, own_ref, other_ref, own_leave_ref, other_leave_ref, cos_ref, sin_ref, mat_ref, *refs
):
    out_ref, leave_ref, total = refs[-3:]
    step = pl.program_id(0)
    chunks, gathered, wide, rows = other_ref.shape
    half = wide // 2
    first = core_ref[0] == 0

    def columns(mine_ref, theirs_ref, b, part):
        mine = mine_ref[:, b, part, :].reshape(chunks * half, rows)
        theirs = theirs_ref[:, b, part, :].reshape(chunks * half, rows)
        low = jnp.where(first, mine, theirs)
        high = jnp.where(first, theirs, mine)
        return jnp.concatenate([low, high], axis=0)

    spans = []
    for b in range(gathered):
        real_part = columns(own_ref, other_ref, b, slice(0, half))
        imag_part = columns(own_ref, other_ref, b, slice(half, wide))
        parts = [real_part.astype(jnp.bfloat16), imag_part.astype(jnp.bfloat16)]
        for depth in range(DEPTHS - 1):
            cosine = cos_ref[b, depth : depth + 1, :]
            sine = sin_ref[b, depth : depth + 1, :]
            parts.append((cosine * real_part - sine * imag_part).astype(jnp.bfloat16))
            parts.append((sine * real_part + cosine * imag_part).astype(jnp.bfloat16))
        spans.append(jnp.concatenate(parts, axis=0))
    depths = jnp.concatenate(spans, axis=1)
    partial = lax.dot_general(mat_ref[0], depths, NT, preferred_element_type=jnp.float32)

    @pl.when(step == 0)
    def _():
        total[...] = partial
        leave = [
            columns(own_leave_ref, other_leave_ref, 0, part)
            for part in (slice(0, half), slice(half, wide))
        ]
        leave_ref[0] = jnp.concatenate(leave, axis=0).T

    @pl.when((step > 0) & (step < pl.num_programs(0) - 1))
    def _():
        total[...] += partial

    @pl.when(step == pl.num_programs(0) - 1)
    def _():
        out_ref[0] = (total[...] + partial).astype(jnp.bfloat16)


def layer_fields(core, own, other, cosines, sines, eigvec, layer, before):
    chunks, blocks, wide, rows = other.shape
    layers, _, orders = eigvec.shape
    blocks -= 1
    width = CORES * chunks * wide
    cols = DEPTHS * width
    entering = pl.BlockSpec((chunks, GATHERED, wide, rows), lambda b, c: (0, b, 0, 0))
    leave = pl.BlockSpec((chunks, 1, wide, rows), lambda b, c: (0, blocks, 0, 0))
    own_entering = pl.BlockSpec(
        (chunks, GATHERED, wide, rows), lambda b, c: (layer * CORES, b, 0, 0)
    )
    own_leave = pl.BlockSpec((chunks, 1, wide, rows), lambda b, c: (layer * CORES, blocks, 0, 0))
    coef = pl.BlockSpec((GATHERED, DEPTHS, rows), lambda b, c: (b, 0, 0))
    return pl.pallas_call(
        fields_kernel,
        out_shape=(
            jax.ShapeDtypeStruct((layers, rows, cols), jnp.bfloat16),
            jax.ShapeDtypeStruct((layers, rows, width), jnp.float32),
        ),
        grid_spec=pltpu.PrefetchScalarGridSpec(
            num_scalar_prefetch=1,
            grid=(blocks // GATHERED,),
            in_specs=[
                own_entering,
                entering,
                own_leave,
                leave,
                coef,
                coef,
                pl.BlockSpec((1, rows, rows * GATHERED), lambda b, c: (layer, 0, b)),
            ]
            + [ANYWHERE] * len(before),
            out_specs=(
                pl.BlockSpec((1, rows, cols), lambda b, c: (layer, 0, 0)),
                pl.BlockSpec((1, rows, width), lambda b, c: (layer, 0, 0)),
            ),
            scratch_shapes=[pltpu.VMEM((rows, cols), jnp.float32)],
        ),
        input_output_aliases={8: 0, 9: 1} if before else {},
        compiler_params=PARAMS,
    )(core, own, other, own, other, cosines, sines, eigvec, *before)


def to_all(block):
    return lax.all_to_all(block, "tile", split_axis=0, concat_axis=0, tiled=False)


def on_device(incident, interface, eigvec, angle, decay):
    groups = lax.axis_size("layer")
    tiles = lax.axis_size("tile")
    member = lax.axis_index("layer")
    core = (member % CORES).astype(jnp.int32)
    stage = (member // CORES).astype(jnp.int32)
    stages = groups // CORES
    layers, rows, orders = interface.shape
    width = incident.shape[1]
    part = width // 2 // CORES // CHUNKS
    wide = 2 * part
    partner = [(i, i ^ 1) for i in range(groups)]
    ring = [(i, (i + CORES) % groups) for i in range(groups)]

    phases = jnp.stack([angle, decay]).reshape(2, layers, tiles, rows)
    other_phases = lax.ppermute(phases, "layer", partner)
    after = incident
    arrived = []
    for layer in range(layers):
        arrived.append([])
        for piece in range(PARTS):
            after = widen(interface, layer, piece, after)
            arrived[layer].append(lax.ppermute(after, "layer", partner))
    others = ()
    early = jnp.where(core == 0, phases, other_phases)
    late = jnp.where(core == 0, other_phases, phases)
    all_phases = jnp.concatenate([early, late], axis=1)
    scale = jnp.exp(-all_phases[1])
    whole = jnp.stack([scale * jnp.cos(all_phases[0]), scale * jnp.sin(all_phases[0])], axis=1)
    fracs = (jnp.arange(1, DEPTHS + 1, dtype=jnp.float32) / DEPTHS).reshape(1, 1, DEPTHS, 1)
    scale = jnp.exp(-fracs * phases[1][:, :, None, :])
    cosines = scale * jnp.cos(fracs * phases[0][:, :, None, :])
    sines = scale * jnp.sin(fracs * phases[0][:, :, None, :])

    whole, cosines, sines = lax.optimization_barrier((whole, cosines, sines))

    start = incident.astype(jnp.float32).T.reshape(2, CORES, CHUNKS, part, rows)
    start = jnp.where(core == 0, start[:, 0], start[:, 1])
    start = start.transpose(1, 0, 2, 3).reshape(CHUNKS, wide, rows)

    ticks = jnp.arange(stages + CHUNKS - 1, dtype=jnp.int32)
    slots = ticks - stage
    valid = (slots >= 0) & (slots < CHUNKS)
    slots = jnp.clip(slots, 0, CHUNKS - 1)
    plan = [jnp.full_like(ticks, core), valid.astype(jnp.int32)]
    for number in range(CORES * layers):
        kind = (core != number // layers).astype(jnp.int32)
        plan.append((number % layers * CORES + kind) * CHUNKS + slots)
    plan = jnp.stack(plan, axis=1)

    saved = allocate((SLOTS, tiles + 1, wide, rows))
    received = None
    for tick in range(stages + CHUNKS - 1):
        inbox = start[min(tick, CHUNKS - 1)]
        if tick > 0:
            inbox = jnp.where(stage == 0, inbox, received)
        spread = jnp.broadcast_to(inbox[None], (tiles, wide, rows))
        for number in range(CORES * layers):
            own, half = number % layers, number // layers
            full = to_all(spread)
            if tick == 0 and number < layers:
                for piece in range(PARTS):
                    tied = others + (spread,) * min(number, 1)
                    others = (narrow(arrived[own][piece], own, piece, layers, tied),)
            spread, saved = layer_step(
                plan, full, whole, interface, others[0], saved, tick, half, own, number
            )
        received = lax.ppermute(spread[0], "layer", ring)

    results = ()
    for layer in range(layers):
        first = (layer * CORES + 1) * CHUNKS
        other = lax.ppermute(saved[first : first + CHUNKS], "layer", partner)
        results = layer_fields(
            core.reshape(1), saved, other, cosines[layer], sines[layer], eigvec, layer,
            results,
        )
    return results


def solution(mesh):
    in_specs = (
        P("tile", None),
        P("layer", "tile", None),
        P("layer", "tile", None),
        P("layer", None),
        P("layer", None),
    )
    out_specs = (P("layer", "tile", None), P("layer", "tile", None))
    return jax.shard_map(
        on_device, mesh=mesh, in_specs=in_specs, out_specs=out_specs, check_vma=False
    )
```

time: 736 us -> 729 us (level)
  the two profiles are of different devices: /device:TPU:25 before, /device:TPU:57 now
where the time goes in v1:
time: 729 us; the launch traced here: 719 us
  blocking collectives  401 us (55%)
  Pallas kernels  179 us (25%)
  starting transfers between devices  112 us (15%)
  waiting for transfers between devices  19 us (3%)
    all_to_all x34, blocking collectives, to_all(): lax.all_to_all(block, 'tile', split_axis=0, concat_axis=0, tiled=False)  401 us
    pallas_call x36, Pallas kernels, layer_step(): pl.pallas_call(functools.partial(step_kernel, tick=tick, half=half, layer...  133 us
    ppermute x2, starting transfers between devices, on_device(): other = lax.ppermute(saved[first:first + CHUNKS], 'layer', partner)  63.5 us
    ppermute x8, starting transfers between devices, on_device(): received = lax.ppermute(spread[0], 'layer', ring)  33.1 us
    pallas_call x4, Pallas kernels, narrow(): pl.pallas_call(narrow_kernel, out_shape=jax.ShapeDtypeStruct((layers, hei...  16.9 us
    pallas_call x4, Pallas kernels, widen(): pl.pallas_call(widen_kernel, out_shape=jax.ShapeDtypeStruct((height, orde...  16.9 us
    ppermute x8, waiting for transfers between devices, on_device(): received = lax.ppermute(spread[0], 'layer', ring)  14.6 us
  transfers between devices with their start and end apart: 17, of which 10 were waited for; matrix products, arithmetic and copies ran while one was open for 0% of the time, Pallas kernels for 6%

profile of v1, /device:TPU:57, one launch (start us, length us, event | category | flops | bytes accessed | tf_op | source)
XLA Modules:
  0.0 719.3 jit_solution(8882731011340442177)
XLA Ops:
  21.4 6.4 all-to-all-start
  42.8 6.7 all-to-all-start.1
  63.4 13.9 %all_to_all.180.full_ref = f32[8,32,512]{2,1,0:T(8,128)S(1)} all-to-all(f32[8,32,512]{2,1,0:T(8,128)S(1)} %get-tuple-element.81), channel_id=1, replica_groups=mesh['layer'=16,'tile'=8] {'tile'}, dimensions={0} | all-to-all | bytes 1048576 | tf_op jit(solution)/shard_map/all_to_all | solution.py:266
  80.8 11.7 %all_to_all.181.full_ref = f32[8,32,512]{2,1,0:T(8,128)S(1)} all-to-all(f32[8,32,512]{2,1,0:T(8,128)S(1)} %get-tuple-element.83), channel_id=1, replica_groups=mesh['layer'=16,'tile'=8] {'tile'}, dimensions={0} | all-to-all | bytes 1048576 | tf_op jit(solution)/shard_map/all_to_all | solution.py:266
  101.0 11.2 %all_to_all.182.full_ref = f32[8,32,512]{2,1,0:T(8,128)S(1)} all-to-all(f32[8,32,512]{2,1,0:T(8,128)S(1)} %broadcast_in_dim.22), channel_id=1, replica_groups=mesh['layer'=16,'tile'=8] {'tile'}, dimensions={0} | all-to-all | bytes 1048576 | tf_op jit(solution)/shard_map/all_to_all | solution.py:266
  115.8 11.3 %all_to_all.183.full_ref = f32[8,32,512]{2,1,0:T(8,128)S(1)} all-to-all(f32[8,32,512]{2,1,0:T(8,128)S(1)} %get-tuple-element.87), channel_id=1, replica_groups=mesh['layer'=16,'tile'=8] {'tile'}, dimensions={0} | all-to-all | bytes 1048576 | tf_op jit(solution)/shard_map/all_to_all | solution.py:266
  130.5 11.3 %all_to_all.184.full_ref = f32[8,32,512]{2,1,0:T(8,128)S(1)} all-to-all(f32[8,32,512]{2,1,0:T(8,128)S(1)} %get-tuple-element.89), channel_id=1, replica_groups=mesh['layer'=16,'tile'=8] {'tile'}, dimensions={0} | all-to-all | bytes 1048576 | tf_op jit(solution)/shard_map/all_to_all | solution.py:266
  145.3 11.3 %all_to_all.185.full_ref = f32[8,32,512]{2,1,0:T(8,128)S(1)} all-to-all(f32[8,32,512]{2,1,0:T(8,128)S(1)} %get-tuple-element.91), channel_id=1, replica_groups=mesh['layer'=16,'tile'=8] {'tile'}, dimensions={0} | all-to-all | bytes 1048576 | tf_op jit(solution)/shard_map/all_to_all | solution.py:266
  160.1 7.4 %collective-permute-start.6 = (f32[32,512]{1,0:T(8,128)S(1)}, f32[32,512]{1,0:T(8,128)S(1)}, u32[]{:S(2)}, u32[]{:S(2)}) collective-permute-start(f32[32,512]{1,0:T(8,128)S(1)} %slice_bitcast_fusion.10), channel_id=1, source_target_pairs={{0,16},{8,24},{16,32},{24,40},{32,48},{40,56},{48,64},{56,72},{64,... | collective-permute-start | bytes 196616 | tf_op jit(solution)/shard_map/ppermute | solution.py:336
  168.8 11.3 %all_to_all.186.full_ref = f32[8,32,512]{2,1,0:T(8,128)S(1)} all-to-all(f32[8,32,512]{2,1,0:T(8,128)S(1)} %broadcast_in_dim.23), channel_id=1, replica_groups=mesh['layer'=16,'tile'=8] {'tile'}, dimensions={0} | all-to-all | bytes 1048576 | tf_op jit(solution)/shard_map/all_to_all | solution.py:266
  183.6 11.8 %all_to_all.187.full_ref = f32[8,32,512]{2,1,0:T(8,128)S(1)} all-to-all(f32[8,32,512]{2,1,0:T(8,128)S(1)} %get-tuple-element.95), channel_id=1, replica_groups=mesh['layer'=16,'tile'=8] {'tile'}, dimensions={0} | all-to-all | bytes 1048576 | tf_op jit(solution)/shard_map/all_to_all | solution.py:266
  198.9 13.4 %all_to_all.188.full_ref = f32[8,32,512]{2,1,0:T(8,128)S(1)} all-to-all(f32[8,32,512]{2,1,0:T(8,128)S(1)} %get-tuple-element.97), channel_id=1, replica_groups=mesh['layer'=16,'tile'=8] {'tile'}, dimensions={0} | all-to-all | bytes 1048576 | tf_op jit(solution)/shard_map/all_to_all | solution.py:266
  215.7 13.6 %all_to_all.189.full_ref = f32[8,32,512]{2,1,0:T(8,128)S(1)} all-to-all(f32[8,32,512]{2,1,0:T(8,128)S(1)} %get-tuple-element.99), channel_id=1, replica_groups=mesh['layer'=16,'tile'=8] {'tile'}, dimensions={0} | all-to-all | bytes 1048576 | tf_op jit(solution)/shard_map/all_to_all | solution.py:266
  232.8 4.3 collective-permute-start.7
  238.5 11.9 %all_to_all.190.full_ref = f32[8,32,512]{2,1,0:T(8,128)S(1)} all-to-all(f32[8,32,512]{2,1,0:T(8,128)S(1)} %broadcast_in_dim.24), channel_id=1, replica_groups=mesh['layer'=16,'tile'=8] {'tile'}, dimensions={0} | all-to-all | bytes 1048576 | tf_op jit(solution)/shard_map/all_to_all | solution.py:266
  253.9 11.1 %all_to_all.191.full_ref = f32[8,32,512]{2,1,0:T(8,128)S(1)} all-to-all(f32[8,32,512]{2,1,0:T(8,128)S(1)} %get-tuple-element.103), channel_id=1, replica_groups=mesh['layer'=16,'tile'=8] {'tile'}, dimensions={0} | all-to-all | bytes 1048576 | tf_op jit(solution)/shard_map/all_to_all | solution.py:266
  268.5 11.6 %all_to_all.192.full_ref = f32[8,32,512]{2,1,0:T(8,128)S(1)} all-to-all(f32[8,32,512]{2,1,0:T(8,128)S(1)} %get-tuple-element.105), channel_id=1, replica_groups=mesh['layer'=16,'tile'=8] {'tile'}, dimensions={0} | all-to-all | bytes 1048576 | tf_op jit(solution)/shard_map/all_to_all | solution.py:266
  283.5 11.3 %all_to_all.193.full_ref = f32[8,32,512]{2,1,0:T(8,128)S(1)} all-to-all(f32[8,32,512]{2,1,0:T(8,128)S(1)} %get-tuple-element.107), channel_id=1, replica_groups=mesh['layer'=16,'tile'=8] {'tile'}, dimensions={0} | all-to-all | bytes 1048576 | tf_op jit(solution)/shard_map/all_to_all | solution.py:266
  303.9 11.1 %all_to_all.194.full_ref = f32[8,32,512]{2,1,0:T(8,128)S(1)} all-to-all(f32[8,32,512]{2,1,0:T(8,128)S(1)} %broadcast_in_dim.25), channel_id=1, replica_groups=mesh['layer'=16,'tile'=8] {'tile'}, dimensions={0} | all-to-all | bytes 1048576 | tf_op jit(solution)/shard_map/all_to_all | solution.py:266
  318.5 11.6 %all_to_all.195.full_ref = f32[8,32,512]{2,1,0:T(8,128)S(1)} all-to-all(f32[8,32,512]{2,1,0:T(8,128)S(1)} %get-tuple-element.111), channel_id=1, replica_groups=mesh['layer'=16,'tile'=8] {'tile'}, dimensions={0} | all-to-all | bytes 1048576 | tf_op jit(solution)/shard_map/all_to_all | solution.py:266
  333.5 11.3 %all_to_all.196.full_ref = f32[8,32,512]{2,1,0:T(8,128)S(1)} all-to-all(f32[8,32,512]{2,1,0:T(8,128)S(1)} %get-tuple-element.113), channel_id=1, replica_groups=mesh['layer'=16,'tile'=8] {'tile'}, dimensions={0} | all-to-all | bytes 1048576 | tf_op jit(solution)/shard_map/all_to_all | solution.py:266
  348.3 11.6 %all_to_all.197.full_ref = f32[8,32,512]{2,1,0:T(8,128)S(1)} all-to-all(f32[8,32,512]{2,1,0:T(8,128)S(1)} %get-tuple-element.115), channel_id=1, replica_groups=mesh['layer'=16,'tile'=8] {'tile'}, dimensions={0} | all-to-all | bytes 1048576 | tf_op jit(solution)/shard_map/all_to_all | solution.py:266
  363.4 5.3 collective-permute-start.9
  370.1 11.3 %all_to_all.198.full_ref = f32[8,32,512]{2,1,0:T(8,128)S(1)} all-to-all(f32[8,32,512]{2,1,0:T(8,128)S(1)} %broadcast_in_dim.26), channel_id=1, replica_groups=mesh['layer'=16,'tile'=8] {'tile'}, dimensions={0} | all-to-all | bytes 1048576 | tf_op jit(solution)/shard_map/all_to_all | solution.py:266
  384.9 11.3 %all_to_all.199.full_ref = f32[8,32,512]{2,1,0:T(8,128)S(1)} all-to-all(f32[8,32,512]{2,1,0:T(8,128)S(1)} %get-tuple-element.119), channel_id=1, replica_groups=mesh['layer'=16,'tile'=8] {'tile'}, dimensions={0} | all-to-all | bytes 1048576 | tf_op jit(solution)/shard_map/all_to_all | solution.py:266
  399.7 11.3 %all_to_all.200.full_ref = f32[8,32,512]{2,1,0:T(8,128)S(1)} all-to-all(f32[8,32,512]{2,1,0:T(8,128)S(1)} %get-tuple-element.121), channel_id=1, replica_groups=mesh['layer'=16,'tile'=8] {'tile'}, dimensions={0} | all-to-all | bytes 1048576 | tf_op jit(solution)/shard_map/all_to_all | solution.py:266
  414.4 11.6 %all_to_all.201.full_ref = f32[8,32,512]{2,1,0:T(8,128)S(1)} all-to-all(f32[8,32,512]{2,1,0:T(8,128)S(1)} %get-tuple-element.123), channel_id=1, replica_groups=mesh['layer'=16,'tile'=8] {'tile'}, dimensions={0} | all-to-all | bytes 1048576 | tf_op jit(solution)/shard_map/all_to_all | solution.py:266
  429.5 4.7 collective-permute-start.10
  435.6 13.7 %all_to_all.202.full_ref = f32[8,32,512]{2,1,0:T(8,128)S(1)} all-to-all(f32[8,32,512]{2,1,0:T(8,128)S(1)} %broadcast_in_dim.27), channel_id=1, replica_groups=mesh['layer'=16,'tile'=8] {'tile'}, dimensions={0} | all-to-all | bytes 1048576 | tf_op jit(solution)/shard_map/all_to_all | solution.py:266
  452.7 12.7 %all_to_all.203.full_ref = f32[8,32,512]{2,1,0:T(8,128)S(1)} all-to-all(f32[8,32,512]{2,1,0:T(8,128)S(1)} %get-tuple-element.127), channel_id=1, replica_groups=mesh['layer'=16,'tile'=8] {'tile'}, dimensions={0} | all-to-all | bytes 1048576 | tf_op jit(solution)/shard_map/all_to_all | solution.py:266
  468.9 12.0 %all_to_all.204.full_ref = f32[8,32,512]{2,1,0:T(8,128)S(1)} all-to-all(f32[8,32,512]{2,1,0:T(8,128)S(1)} %get-tuple-element.129), channel_id=1, replica_groups=mesh['layer'=16,'tile'=8] {'tile'}, dimensions={0} | all-to-all | bytes 1048576 | tf_op jit(solution)/shard_map/all_to_all | solution.py:266
  484.3 11.3 %all_to_all.205.full_ref = f32[8,32,512]{2,1,0:T(8,128)S(1)} all-to-all(f32[8,32,512]{2,1,0:T(8,128)S(1)} %get-tuple-element.131), channel_id=1, replica_groups=mesh['layer'=16,'tile'=8] {'tile'}, dimensions={0} | all-to-all | bytes 1048576 | tf_op jit(solution)/shard_map/all_to_all | solution.py:266
  503.9 12.9 %all_to_all.206.full_ref = f32[8,32,512]{2,1,0:T(8,128)S(1)} all-to-all(f32[8,32,512]{2,1,0:T(8,128)S(1)} %broadcast_in_dim.28), channel_id=1, replica_groups=mesh['layer'=16,'tile'=8] {'tile'}, dimensions={0} | all-to-all | bytes 1048576 | tf_op jit(solution)/shard_map/all_to_all | solution.py:266
  521.0 11.3 %all_to_all.207.full_ref = f32[8,32,512]{2,1,0:T(8,128)S(1)} all-to-all(f32[8,32,512]{2,1,0:T(8,128)S(1)} %get-tuple-element.135), channel_id=1, replica_groups=mesh['layer'=16,'tile'=8] {'tile'}, dimensions={0} | all-to-all | bytes 1048576 | tf_op jit(solution)/shard_map/all_to_all | solution.py:266
  532.3 4.3 shard_map.106
  536.6 11.3 %all_to_all.208.full_ref = f32[8,32,512]{2,1,0:T(8,128)S(1)} all-to-all(f32[8,32,512]{2,1,0:T(8,128)S(1)} %get-tuple-element.137), channel_id=1, replica_groups=mesh['layer'=16,'tile'=8] {'tile'}, dimensions={0} | all-to-all | bytes 1048576 | tf_op jit(solution)/shard_map/all_to_all | solution.py:266
  552.1 12.2 %all_to_all.209.full_ref = f32[8,32,512]{2,1,0:T(8,128)S(1)} all-to-all(f32[8,32,512]{2,1,0:T(8,128)S(1)} %get-tuple-element.139), channel_id=1, replica_groups=mesh['layer'=16,'tile'=8] {'tile'}, dimensions={0} | all-to-all | bytes 1048576 | tf_op jit(solution)/shard_map/all_to_all | solution.py:266
  568.9 5.3 collective-permute-done.12
  574.3 11.9 %all_to_all.210.full_ref = f32[8,32,512]{2,1,0:T(8,128)S(1)} all-to-all(f32[8,32,512]{2,1,0:T(8,128)S(1)} %broadcast_in_dim.29), channel_id=1, replica_groups=mesh['layer'=16,'tile'=8] {'tile'}, dimensions={0} | all-to-all | bytes 1048576 | tf_op jit(solution)/shard_map/all_to_all | solution.py:266
  590.5 11.3 %all_to_all.211.full_ref = f32[8,32,512]{2,1,0:T(8,128)S(1)} all-to-all(f32[8,32,512]{2,1,0:T(8,128)S(1)} %get-tuple-element.143), channel_id=1, replica_groups=mesh['layer'=16,'tile'=8] {'tile'}, dimensions={0} | all-to-all | bytes 1048576 | tf_op jit(solution)/shard_map/all_to_all | solution.py:266
  601.8 4.3 shard_map.110
  606.1 11.3 %all_to_all.212.full_ref = f32[8,32,512]{2,1,0:T(8,128)S(1)} all-to-all(f32[8,32,512]{2,1,0:T(8,128)S(1)} %get-tuple-element.145), channel_id=1, replica_groups=mesh['layer'=16,'tile'=8] {'tile'}, dimensions={0} | all-to-all | bytes 1048576 | tf_op jit(solution)/shard_map/all_to_all | solution.py:266
  617.4 4.3 shard_map.111
  621.6 11.7 %all_to_all.213.full_ref = f32[8,32,512]{2,1,0:T(8,128)S(1)} all-to-all(f32[8,32,512]{2,1,0:T(8,128)S(1)} %get-tuple-element.147), channel_id=1, replica_groups=mesh['layer'=16,'tile'=8] {'tile'}, dimensions={0} | all-to-all | bytes 1048576 | tf_op jit(solution)/shard_map/all_to_all | solution.py:266
  633.3 5.1 shard_map.112
  640.3 63.4 %collective-permute-start.14 = (f32[2,9,32,512]{3,2,1,0:T(8,128)S(1)}, f32[2,9,32,512]{3,2,1,0:T(8,128)S(1)}, u32[]{:S(2)}, u32[]{:S(2)}) collective-permute-start(f32[2,9,32,512]{3,2,1,0:T(8,128)S(1)} %get-tuple-element.154), channel_id=1, source_target_pairs={{0,8},{8,0},{16,24},{24,16},{32,40},{40,32},{48,56},{56,48},{64,72... | collective-permute-start | bytes 3538952 | tf_op jit(solution)/shard_map/ppermute | solution.py:341
  706.2 6.3 shard_map.113
  712.5 6.4 shard_map.114
  (123 shorter events, 182.3 us)
Async XLA Ops:
  0.6 0.9 copy-start
  5.8 24.3 %collective-permute-start.2 = (f32[256,4096]{1,0:T(8,128)}, f32[256,4096]{1,0:T(8,128)}, u32[]{:S(2)}, u32[]{:S(2)}) collective-permute-start(f32[256,4096]{1,0:T(8,128)} %shard_map.68.after_ref), channel_id=1, source_target_pairs={{0,8},{8,0},{16,24},{24,16},{32,40},{40,32},{48,56},{56,48},{64,72... | collective-permute-start | bytes 12582920 | tf_op jit(solution)/shard_map/ppermute | solution.py:291
  10.7 9.0 %copy-start.4 = (f32[2,4096]{1,0:T(2,128)S(1)}, f32[2,4096]{1,0:T(2,128)}, u32[]{:S(2)}) copy-start(f32[2,4096]{1,0:T(2,128)} %param.8) | copy-start | bytes 98308
  10.7 9.1 %copy-start.5 = (f32[2,4096]{1,0:T(2,128)S(1)}, f32[2,4096]{1,0:T(2,128)}, u32[]{:S(2)}) copy-start(f32[2,4096]{1,0:T(2,128)} %param.9) | copy-start | bytes 98308
  10.7 9.7 %copy-start.1 = (bf16[512,128]{1,0:T(8,128)(2,1)S(1)}, bf16[512,128]{1,0:T(8,128)(2,1)}, u32[]{:S(2)}) copy-start(bf16[512,128]{1,0:T(8,128)(2,1)} %after_ref.1) | copy-start | bytes 393220
  10.7 23.6 %collective-permute-start.1 = (f32[256,4096]{1,0:T(8,128)}, f32[256,4096]{1,0:T(8,128)}, u32[]{:S(2)}, u32[]{:S(2)}) collective-permute-start(f32[256,4096]{1,0:T(8,128)} %shard_map.69.after_ref), channel_id=1, source_target_pairs={{0,8},{8,0},{16,24},{24,16},{32,40},{40,32},{48,56},{56,48},{64,72... | collective-permute-start | bytes 12582920 | tf_op jit(solution)/shard_map/ppermute | solution.py:291
  15.0 34.5 %collective-permute-start.4 = (f32[256,4096]{1,0:T(8,128)}, f32[256,4096]{1,0:T(8,128)}, u32[]{:S(2)}, u32[]{:S(2)}) collective-permute-start(f32[256,4096]{1,0:T(8,128)} %shard_map.74.after_ref), channel_id=1, source_target_pairs={{0,8},{8,0},{16,24},{24,16},{32,40},{40,32},{48,56},{56,48},{64,72... | collective-permute-start | bytes 12582920 | tf_op jit(solution)/shard_map/ppermute | solution.py:291
  19.7 34.1 %collective-permute-start.3 = (f32[256,4096]{1,0:T(8,128)}, f32[256,4096]{1,0:T(8,128)}, u32[]{:S(2)}, u32[]{:S(2)}) collective-permute-start(f32[256,4096]{1,0:T(8,128)} %shard_map.75), channel_id=1, source_target_pairs={{0,8},{8,0},{16,24},{24,16},{32,40},{40,32},{48,56},{56,48},{64,72... | collective-permute-start | bytes 12582920 | tf_op jit(solution)/shard_map/ppermute | solution.py:291
  19.8 10.0 %collective-permute-start = (f32[2,2,8,512]{3,2,1,0:T(8,128)S(1)}, f32[2,2,8,512]{3,2,1,0:T(8,128)S(1)}, u32[]{:S(2)}, u32[]{:S(2)}) collective-permute-start(f32[2,2,8,512]{3,2,1,0:T(8,128)S(1)} %get-tuple-element.169), channel_id=1, source_target_pairs={{0,8},{8,0},{16,24},{24,16},{32,40},{40,32},{48,56},{56,48},{64,72... | collective-permute-start | bytes 196616 | tf_op jit(solution)/shard_map/ppermute | solution.py:284
  21.4 17.2 %all-to-all-start = ((f32[8,32,512]{2,1,0:T(8,128)}), f32[8,32,512]{2,1,0:T(8,128)S(1)}, u32[]{:S(2)}, u32[]{:S(2)}) async-start(f32[8,32,512]{2,1,0:T(8,128)} %broadcast_in_dim.21), calls=%async_computation | async-start | bytes 1048576 | tf_op jit(solution)/shard_map/all_to_all | solution.py:266
  42.8 17.1 %all-to-all-start.1 = ((f32[8,32,512]{2,1,0:T(8,128)}), f32[8,32,512]{2,1,0:T(8,128)S(1)}, u32[]{:S(2)}, u32[]{:S(2)}) async-start(f32[8,32,512]{2,1,0:T(8,128)} %get-tuple-element.79.refs_1_), calls=%async_computation.1 | async-start | bytes 1048576 | tf_op jit(solution)/shard_map/all_to_all | solution.py:266
  96.0 5.0 collective-permute-start.5
  160.1 8.7 %collective-permute-start.6 = (f32[32,512]{1,0:T(8,128)S(1)}, f32[32,512]{1,0:T(8,128)S(1)}, u32[]{:S(2)}, u32[]{:S(2)}) collective-permute-start(f32[32,512]{1,0:T(8,128)S(1)} %slice_bitcast_fusion.10), channel_id=1, source_target_pairs={{0,16},{8,24},{16,32},{24,40},{32,48},{40,56},{48,64},{56,72},{64,... | collective-permute-start | bytes 196616 | tf_op jit(solution)/shard_map/ppermute | solution.py:336
  232.8 5.6 collective-permute-start.7
  298.3 5.5 collective-permute-start.8
  363.4 6.6 collective-permute-start.9
  429.5 6.0 collective-permute-start.10
  499.1 4.7 collective-permute-start.11
  568.6 5.6 collective-permute-start.12
  633.3 70.5 %copy-start.3 = (f32[2,8,4,512]{3,2,1,0:T(4,128)S(1)}, f32[2,8,4,512]{3,2,1,0:T(4,128)}, u32[]{:S(2)}) copy-start(f32[2,8,4,512]{3,2,1,0:T(4,128)} %get-tuple-element.151) | copy-start | bytes 393220
  633.3 70.5 %copy-start.2 = (f32[2,8,4,512]{3,2,1,0:T(4,128)S(1)}, f32[2,8,4,512]{3,2,1,0:T(4,128)}, u32[]{:S(2)}) copy-start(f32[2,8,4,512]{3,2,1,0:T(4,128)} %get-tuple-element.150) | copy-start | bytes 393220
  640.3 65.9 %collective-permute-start.14 = (f32[2,9,32,512]{3,2,1,0:T(8,128)S(1)}, f32[2,9,32,512]{3,2,1,0:T(8,128)S(1)}, u32[]{:S(2)}, u32[]{:S(2)}) collective-permute-start(f32[2,9,32,512]{3,2,1,0:T(8,128)S(1)} %get-tuple-element.154), channel_id=1, source_target_pairs={{0,8},{8,0},{16,24},{24,16},{32,40},{40,32},{48,56},{56,48},{64,72... | collective-permute-start | bytes 3538952 | tf_op jit(solution)/shard_map/ppermute | solution.py:341
  703.7 8.8 %collective-permute-start.13 = (f32[2,9,32,512]{3,2,1,0:T(8,128)S(1)}, f32[2,9,32,512]{3,2,1,0:T(8,128)S(1)}, u32[]{:S(2)}, u32[]{:S(2)}) collective-permute-start(f32[2,9,32,512]{3,2,1,0:T(8,128)S(1)} %get-tuple-element.155), channel_id=1, source_target_pairs={{0,8},{8,0},{16,24},{24,16},{32,40},{40,32},{48,56},{56,48},{64,72... | collective-permute-start | bytes 3538952 | tf_op jit(solution)/shard_map/ppermute | solution.py:341

commit v2 on v1

--- a/solution.py
+++ b/solution.py
@@ -11,8 +11,8 @@
 CHUNKS = 2
 CORES = 2
 PARTS = 2
-PIECES = 4
-GATHERED = 2
+PIECES = 2
+GATHERED = 4
 SLOTS = 32
 NT = (((1,), (1,)), ((), ()))
 VMEM = pl.BlockSpec(memory_space=pltpu.VMEM)
@@ -61,13 +61,18 @@
 
 
 def step_kernel(
-    plan_ref, full_ref, phase_ref, own_ref, other_ref, saved_in,
-    out_ref, saved_ref, row_buf, mat_buf, sum_buf, row_sem, sems, save_sems,
-    *, tick, half, layer, number
+    full_ref, phase_ref, own_ref, other_ref, saved_in, *refs, tick, number, layers, ticks
 ):
+    out_ref, saved_ref, row_buf, mat_buf, sum_buf, row_sem, sems, save_sems = refs[-8:]
     blocks, wide, rows = full_ref.shape
     split = wide // 2
-    core, valid, slot = plan_ref[tick, 0], plan_ref[tick, 1], plan_ref[tick, 2 + number]
+    half, layer = number // layers, number % layers
+    member = lax.axis_index("layer")
+    core = lax.rem(member, CORES)
+    stage = lax.div(member, CORES)
+    left = CORES * layers - 1 - number
+    late = tick == ticks - 1 and left < 2
+    behind = (tick or number) and not (late and left == 0)
     row_copy = pltpu.make_async_copy(phase_ref.at[number], row_buf, row_sem)
     row_copy.start()
 
@@ -89,14 +94,33 @@
         for copy in copies(other_ref):
             copy.start()
 
+    def chunk_of(tick):
+        return (tick >= stage) & (tick - stage < CHUNKS), jnp.clip(tick - stage, 0, CHUNKS - 1)
+
+    def entry(number, chunk):
+        kind = jnp.where(core == number // layers, 0, 1)
+        return (number % layers * CORES + kind) * CHUNKS + chunk
+
+    valid, chunk = chunk_of(tick)
     block_save = pltpu.make_async_copy(
-        full_ref, saved_ref.at[slot, pl.ds(0, blocks)], save_sems.at[0]
+        full_ref, saved_ref.at[entry(number, chunk), pl.ds(0, blocks)], save_sems.at[0]
     )
-    sum_save = pltpu.make_async_copy(sum_buf, saved_ref.at[slot, blocks], save_sems.at[1])
-
-    @pl.when(valid == 1)
+    if behind:
+        before = (number - 1) % (CORES * layers)
+        before_valid, before_chunk = chunk_of(tick - (number == 0))
+        before_save = pltpu.make_async_copy(
+            refs[0].at[0], saved_ref.at[entry(before, before_chunk), blocks], save_sems.at[1]
+        )
+
+    @pl.when(valid)
     def _():
         block_save.start()
+
+    if behind:
+
+        @pl.when(before_valid)
+        def _():
+            before_save.start()
 
     arrivals = copies(own_ref)
     total = jnp.zeros((wide, rows), jnp.float32)
@@ -111,20 +135,30 @@
         ).astype(jnp.bfloat16)
         arrivals[b].wait()
         total += lax.dot_general(phased, mat_buf[b], NT, preferred_element_type=jnp.float32)
-    sum_buf[...] = total
-
-
-    @pl.when(valid == 1)
-    def _():
-        sum_save.start()
 
     for b in range(blocks):
         out_ref[b] = total
 
-    @pl.when(valid == 1)
+    if late:
+        sum_buf[...] = total
+        sum_save = pltpu.make_async_copy(
+            sum_buf, saved_ref.at[entry(number, chunk), blocks], save_sems.at[2]
+        )
+
+        @pl.when(valid)
+        def _():
+            sum_save.start()
+            sum_save.wait()
+
+    @pl.when(valid)
     def _():
         block_save.wait()
-        sum_save.wait()
+
+    if behind:
+
+        @pl.when(before_valid)
+        def _():
+            before_save.wait()
 
 
 def allocate_kernel(out_ref):
@@ -141,26 +175,24 @@
     )()
 
 
-def layer_step(plan, full, phases, own, other, saved, tick, half, layer, number):
+def layer_step(full, phases, own, other, saved, extra, **place):
     blocks, wide, rows = full.shape
     return pl.pallas_call(
-        functools.partial(
-            step_kernel, tick=tick, half=half, layer=layer, number=number
-        ),
+        functools.partial(step_kernel, **place),
         out_shape=(
             jax.ShapeDtypeStruct(full.shape, jnp.float32),
             jax.ShapeDtypeStruct(saved.shape, jnp.float32),
         ),
-        in_specs=[SMEM, VMEM] + [ANYWHERE] * 4,
+        in_specs=[VMEM] + [ANYWHERE] * (4 + len(extra)),
         out_specs=(VMEM, ANYWHERE),
-        input_output_aliases={5: 1},
+        input_output_aliases={4: 1},
         scratch_shapes=[
             pltpu.VMEM(phases.shape[1:], jnp.float32),
             pltpu.VMEM((blocks, rows, rows), jnp.bfloat16),
             pltpu.VMEM((wide, rows), jnp.float32),
             pltpu.SemaphoreType.DMA,
             pltpu.SemaphoreType.DMA((blocks,)),
-            pltpu.SemaphoreType.DMA((2,)),
+            pltpu.SemaphoreType.DMA((3,)),
         ],
         compiler_params=PARAMS,
         cost_estimate=pl.CostEstimate(
@@ -168,7 +200,7 @@
             bytes_accessed=2 * blocks * rows * rows,
             transcendentals=0,
         ),
-    )(plan, full, phases, own, other, saved)
+    )(full, phases, own, other, saved, *extra)
 
 
 def fields_kernel(
@@ -282,13 +314,14 @@
 
     phases = jnp.stack([angle, decay]).reshape(2, layers, tiles, rows)
     other_phases = lax.ppermute(phases, "layer", partner)
-    after = incident
-    arrived = []
-    for layer in range(layers):
-        arrived.append([])
+    def swap(layer, after):
+        pieces = []
         for piece in range(PARTS):
             after = widen(interface, layer, piece, after)
-            arrived[layer].append(lax.ppermute(after, "layer", partner))
+            pieces.append(lax.ppermute(after, "layer", partner))
+        return pieces, after
+
+    arrived = [swap(0, incident)[0]]
     others = ()
     early = jnp.where(core == 0, phases, other_phases)
     late = jnp.where(core == 0, other_phases, phases)
@@ -306,43 +339,47 @@
     start = jnp.where(core == 0, start[:, 0], start[:, 1])
     start = start.transpose(1, 0, 2, 3).reshape(CHUNKS, wide, rows)
 
-    ticks = jnp.arange(stages + CHUNKS - 1, dtype=jnp.int32)
-    slots = ticks - stage
-    valid = (slots >= 0) & (slots < CHUNKS)
-    slots = jnp.clip(slots, 0, CHUNKS - 1)
-    plan = [jnp.full_like(ticks, core), valid.astype(jnp.int32)]
-    for number in range(CORES * layers):
-        kind = (core != number // layers).astype(jnp.int32)
-        plan.append((number % layers * CORES + kind) * CHUNKS + slots)
-    plan = jnp.stack(plan, axis=1)
-
+    ticks = stages + CHUNKS - 1
     saved = allocate((SLOTS, tiles + 1, wide, rows))
+    results = ()
+
+    def finish(layer):
+        first = (layer * CORES + 1) * CHUNKS
+        other = lax.ppermute(saved[first : first + CHUNKS], "layer", partner)
+        return layer_fields(
+            core.reshape(1), saved, other, cosines[layer], sines[layer], eigvec, layer, results
+        )
+
     received = None
-    for tick in range(stages + CHUNKS - 1):
+    computed = ()
+    for tick in range(ticks):
         inbox = start[min(tick, CHUNKS - 1)]
         if tick > 0:
             inbox = jnp.where(stage == 0, inbox, received)
         spread = jnp.broadcast_to(inbox[None], (tiles, wide, rows))
         for number in range(CORES * layers):
-            own, half = number % layers, number // layers
             full = to_all(spread)
             if tick == 0 and number < layers:
                 for piece in range(PARTS):
                     tied = others + (spread,) * min(number, 1)
-                    others = (narrow(arrived[own][piece], own, piece, layers, tied),)
+                    if number == 0 and piece == 0:
+                        after = whole
+                        for later in range(1, layers):
+                            pieces, after = swap(later, after)
+                            arrived.append(pieces)
+                    others = (narrow(arrived[number][piece], number, piece, layers, tied),)
+            if tick == ticks - 1 and number == CORES * layers - 1:
+                results = finish(0)
+                computed += tuple(results[1:])
             spread, saved = layer_step(
-                plan, full, whole, interface, others[0], saved, tick, half, own, number
+                full, whole, interface, others[0], saved, computed,
+                tick=tick, number=number, layers=layers, ticks=ticks,
             )
+            computed = (spread,)
         received = lax.ppermute(spread[0], "layer", ring)
 
-    results = ()
-    for layer in range(layers):
-        first = (layer * CORES + 1) * CHUNKS
-        other = lax.ppermute(saved[first : first + CHUNKS], "layer", partner)
-        results = layer_fields(
-            core.reshape(1), saved, other, cosines[layer], sines[layer], eigvec, layer,
-            results,
-        )
+    for layer in range(1, layers):
+        results = finish(layer)
     return results
 
 

time: 729 us -> 689 us (0.945)
  the two profiles are of different devices: /device:TPU:57 before, /device:TPU:0 now
where the time goes in v2:
time: 689 us; the launch traced here: 678 us
  blocking collectives  439 us (64%)
  Pallas kernels  141 us (20%)
  waiting for transfers between devices  69.1 us (10%)
  starting transfers between devices  17.1 us (2%)
  local copies, waits for them, and re-layouts  7.7 us (1%)
    all_to_all x33, blocking collectives, to_all(): lax.all_to_all(block, 'tile', split_axis=0, concat_axis=0, tiled=False)  439 us
    pallas_call x36, Pallas kernels, layer_step(): pl.pallas_call(functools.partial(step_kernel, **place), out_shape=(jax.Sh...  104 us
    ppermute x8, waiting for transfers between devices, on_device(): received = lax.ppermute(spread[0], 'layer', ring)  52 us
    all_to_all x3, starting transfers between devices, to_all(): lax.all_to_all(block, 'tile', split_axis=0, concat_axis=0, tiled=False)  14.9 us
    all_to_all x3, waiting for transfers between devices, to_all(): lax.all_to_all(block, 'tile', split_axis=0, concat_axis=0, tiled=False)  14.2 us
  transfers between devices with their start and end apart: 18, of which 12 were waited for; matrix products, arithmetic and copies ran while one was open for 0% of the time, Pallas kernels for 5%

profile of v2, /device:TPU:0, one launch (start us, length us, event | category | flops | bytes accessed | tf_op | source)
XLA Modules:
  0.0 677.8 jit_solution(9342685372868538342)
XLA Ops:
  20.5 7.7 %all-to-all-start = ((f32[8,32,512]{2,1,0:T(8,128)}), f32[8,32,512]{2,1,0:T(8,128)S(1)}, u32[]{:S(2)}, u32[]{:S(2)}) async-start(f32[8,32,512]{2,1,0:T(8,128)} %broadcast_in_dim.21), calls=%async_computation | async-start | bytes 1048576 | tf_op jit(solution)/shard_map/all_to_all | solution.py:298
  34.9 4.6 all-to-all-done.full_ref
  39.5 3.7 shard_map.73
  53.7 3.8 all-to-all-done.1.full_ref
  60.7 14.0 %all_to_all.180.full_ref = f32[8,32,512]{2,1,0:T(8,128)S(1)} all-to-all(f32[8,32,512]{2,1,0:T(8,128)S(1)} %get-tuple-element.81.refs_0_), channel_id=1, replica_groups=mesh['layer'=16,'tile'=8] {'tile'}, dimensions={0} | all-to-all | bytes 1048576 | tf_op jit(solution)/shard_map/all_to_all | solution.py:298
  77.7 12.8 %all_to_all.181.full_ref = f32[8,32,512]{2,1,0:T(8,128)S(1)} all-to-all(f32[8,32,512]{2,1,0:T(8,128)S(1)} %get-tuple-element.83.refs_0_), channel_id=1, replica_groups=mesh['layer'=16,'tile'=8] {'tile'}, dimensions={0} | all-to-all | bytes 1048576 | tf_op jit(solution)/shard_map/all_to_all | solution.py:298
  93.6 6.5 collective-permute-done.5
  100.2 13.0 %all_to_all.182.full_ref = f32[8,32,512]{2,1,0:T(8,128)S(1)} all-to-all(f32[8,32,512]{2,1,0:T(8,128)S(1)} %broadcast_in_dim.22), channel_id=1, replica_groups=mesh['layer'=16,'tile'=8] {'tile'}, dimensions={0} | all-to-all | bytes 1048576 | tf_op jit(solution)/shard_map/all_to_all | solution.py:298
  116.2 12.7 %all_to_all.183.full_ref = f32[8,32,512]{2,1,0:T(8,128)S(1)} all-to-all(f32[8,32,512]{2,1,0:T(8,128)S(1)} %get-tuple-element.87.refs_0_), channel_id=1, replica_groups=mesh['layer'=16,'tile'=8] {'tile'}, dimensions={0} | all-to-all | bytes 1048576 | tf_op jit(solution)/shard_map/all_to_all | solution.py:298
  131.9 12.7 %all_to_all.184.full_ref = f32[8,32,512]{2,1,0:T(8,128)S(1)} all-to-all(f32[8,32,512]{2,1,0:T(8,128)S(1)} %get-tuple-element.89.refs_0_), channel_id=1, replica_groups=mesh['layer'=16,'tile'=8] {'tile'}, dimensions={0} | all-to-all | bytes 1048576 | tf_op jit(solution)/shard_map/all_to_all | solution.py:298
  147.6 12.7 %all_to_all.185.full_ref = f32[8,32,512]{2,1,0:T(8,128)S(1)} all-to-all(f32[8,32,512]{2,1,0:T(8,128)S(1)} %get-tuple-element.91.refs_0_), channel_id=1, replica_groups=mesh['layer'=16,'tile'=8] {'tile'}, dimensions={0} | all-to-all | bytes 1048576 | tf_op jit(solution)/shard_map/all_to_all | solution.py:298
  163.6 6.4 collective-permute-done.6
  170.0 14.0 %all_to_all.186.full_ref = f32[8,32,512]{2,1,0:T(8,128)S(1)} all-to-all(f32[8,32,512]{2,1,0:T(8,128)S(1)} %broadcast_in_dim.23), channel_id=1, replica_groups=mesh['layer'=16,'tile'=8] {'tile'}, dimensions={0} | all-to-all | bytes 1048576 | tf_op jit(solution)/shard_map/all_to_all | solution.py:298
  186.7 15.8 %all_to_all.187.full_ref = f32[8,32,512]{2,1,0:T(8,128)S(1)} all-to-all(f32[8,32,512]{2,1,0:T(8,128)S(1)} %get-tuple-element.95.refs_0_), channel_id=1, replica_groups=mesh['layer'=16,'tile'=8] {'tile'}, dimensions={0} | all-to-all | bytes 1048576 | tf_op jit(solution)/shard_map/all_to_all | solution.py:298
  205.3 14.5 %all_to_all.188.full_ref = f32[8,32,512]{2,1,0:T(8,128)S(1)} all-to-all(f32[8,32,512]{2,1,0:T(8,128)S(1)} %get-tuple-element.97.refs_0_), channel_id=1, replica_groups=mesh['layer'=16,'tile'=8] {'tile'}, dimensions={0} | all-to-all | bytes 1048576 | tf_op jit(solution)/shard_map/all_to_all | solution.py:298
  222.5 12.7 %all_to_all.189.full_ref = f32[8,32,512]{2,1,0:T(8,128)S(1)} all-to-all(f32[8,32,512]{2,1,0:T(8,128)S(1)} %get-tuple-element.99.refs_0_), channel_id=1, replica_groups=mesh['layer'=16,'tile'=8] {'tile'}, dimensions={0} | all-to-all | bytes 1048576 | tf_op jit(solution)/shard_map/all_to_all | solution.py:298
  238.1 6.6 collective-permute-done.7
  244.8 12.5 %all_to_all.190.full_ref = f32[8,32,512]{2,1,0:T(8,128)S(1)} all-to-all(f32[8,32,512]{2,1,0:T(8,128)S(1)} %broadcast_in_dim.24), channel_id=1, replica_groups=mesh['layer'=16,'tile'=8] {'tile'}, dimensions={0} | all-to-all | bytes 1048576 | tf_op jit(solution)/shard_map/all_to_all | solution.py:298
  260.1 12.7 %all_to_all.191.full_ref = f32[8,32,512]{2,1,0:T(8,128)S(1)} all-to-all(f32[8,32,512]{2,1,0:T(8,128)S(1)} %get-tuple-element.103.refs_0_), channel_id=1, replica_groups=mesh['layer'=16,'tile'=8] {'tile'}, dimensions={0} | all-to-all | bytes 1048576 | tf_op jit(solution)/shard_map/all_to_all | solution.py:298
  275.6 12.7 %all_to_all.192.full_ref = f32[8,32,512]{2,1,0:T(8,128)S(1)} all-to-all(f32[8,32,512]{2,1,0:T(8,128)S(1)} %get-tuple-element.105.refs_0_), channel_id=1, replica_groups=mesh['layer'=16,'tile'=8] {'tile'}, dimensions={0} | all-to-all | bytes 1048576 | tf_op jit(solution)/shard_map/all_to_all | solution.py:298
  291.1 12.7 %all_to_all.193.full_ref = f32[8,32,512]{2,1,0:T(8,128)S(1)} all-to-all(f32[8,32,512]{2,1,0:T(8,128)S(1)} %get-tuple-element.107.refs_0_), channel_id=1, replica_groups=mesh['layer'=16,'tile'=8] {'tile'}, dimensions={0} | all-to-all | bytes 1048576 | tf_op jit(solution)/shard_map/all_to_all | solution.py:298
  306.7 6.7 collective-permute-done.8
  313.5 13.0 %all_to_all.194.full_ref = f32[8,32,512]{2,1,0:T(8,128)S(1)} all-to-all(f32[8,32,512]{2,1,0:T(8,128)S(1)} %broadcast_in_dim.25), channel_id=1, replica_groups=mesh['layer'=16,'tile'=8] {'tile'}, dimensions={0} | all-to-all | bytes 1048576 | tf_op jit(solution)/shard_map/all_to_all | solution.py:298
  329.2 15.4 %all_to_all.195.full_ref = f32[8,32,512]{2,1,0:T(8,128)S(1)} all-to-all(f32[8,32,512]{2,1,0:T(8,128)S(1)} %get-tuple-element.111.refs_0_), channel_id=1, replica_groups=mesh['layer'=16,'tile'=8] {'tile'}, dimensions={0} | all-to-all | bytes 1048576 | tf_op jit(solution)/shard_map/all_to_all | solution.py:298
  347.4 12.7 %all_to_all.196.full_ref = f32[8,32,512]{2,1,0:T(8,128)S(1)} all-to-all(f32[8,32,512]{2,1,0:T(8,128)S(1)} %get-tuple-element.113.refs_0_), channel_id=1, replica_groups=mesh['layer'=16,'tile'=8] {'tile'}, dimensions={0} | all-to-all | bytes 1048576 | tf_op jit(solution)/shard_map/all_to_all | solution.py:298
  362.8 12.8 %all_to_all.197.full_ref = f32[8,32,512]{2,1,0:T(8,128)S(1)} all-to-all(f32[8,32,512]{2,1,0:T(8,128)S(1)} %get-tuple-element.115.refs_0_), channel_id=1, replica_groups=mesh['layer'=16,'tile'=8] {'tile'}, dimensions={0} | all-to-all | bytes 1048576 | tf_op jit(solution)/shard_map/all_to_all | solution.py:298
  378.7 6.7 collective-permute-done.9
  385.5 12.3 %all_to_all.198.full_ref = f32[8,32,512]{2,1,0:T(8,128)S(1)} all-to-all(f32[8,32,512]{2,1,0:T(8,128)S(1)} %broadcast_in_dim.26), channel_id=1, replica_groups=mesh['layer'=16,'tile'=8] {'tile'}, dimensions={0} | all-to-all | bytes 1048576 | tf_op jit(solution)/shard_map/all_to_all | solution.py:298
  400.6 12.8 %all_to_all.199.full_ref = f32[8,32,512]{2,1,0:T(8,128)S(1)} all-to-all(f32[8,32,512]{2,1,0:T(8,128)S(1)} %get-tuple-element.119.refs_0_), channel_id=1, replica_groups=mesh['layer'=16,'tile'=8] {'tile'}, dimensions={0} | all-to-all | bytes 1048576 | tf_op jit(solution)/shard_map/all_to_all | solution.py:298
  416.1 14.2 %all_to_all.200.full_ref = f32[8,32,512]{2,1,0:T(8,128)S(1)} all-to-all(f32[8,32,512]{2,1,0:T(8,128)S(1)} %get-tuple-element.121.refs_0_), channel_id=1, replica_groups=mesh['layer'=16,'tile'=8] {'tile'}, dimensions={0} | all-to-all | bytes 1048576 | tf_op jit(solution)/shard_map/all_to_all | solution.py:298
  433.1 13.6 %all_to_all.201.full_ref = f32[8,32,512]{2,1,0:T(8,128)S(1)} all-to-all(f32[8,32,512]{2,1,0:T(8,128)S(1)} %get-tuple-element.123.refs_0_), channel_id=1, replica_groups=mesh['layer'=16,'tile'=8] {'tile'}, dimensions={0} | all-to-all | bytes 1048576 | tf_op jit(solution)/shard_map/all_to_all | solution.py:298
  449.5 6.4 collective-permute-done.10
  456.0 13.4 %all_to_all.202.full_ref = f32[8,32,512]{2,1,0:T(8,128)S(1)} all-to-all(f32[8,32,512]{2,1,0:T(8,128)S(1)} %broadcast_in_dim.27), channel_id=1, replica_groups=mesh['layer'=16,'tile'=8] {'tile'}, dimensions={0} | all-to-all | bytes 1048576 | tf_op jit(solution)/shard_map/all_to_all | solution.py:298
  472.1 12.6 %all_to_all.203.full_ref = f32[8,32,512]{2,1,0:T(8,128)S(1)} all-to-all(f32[8,32,512]{2,1,0:T(8,128)S(1)} %get-tuple-element.127.refs_0_), channel_id=1, replica_groups=mesh['layer'=16,'tile'=8] {'tile'}, dimensions={0} | all-to-all | bytes 1048576 | tf_op jit(solution)/shard_map/all_to_all | solution.py:298
  487.5 12.7 %all_to_all.204.full_ref = f32[8,32,512]{2,1,0:T(8,128)S(1)} all-to-all(f32[8,32,512]{2,1,0:T(8,128)S(1)} %get-tuple-element.129.refs_0_), channel_id=1, replica_groups=mesh['layer'=16,'tile'=8] {'tile'}, dimensions={0} | all-to-all | bytes 1048576 | tf_op jit(solution)/shard_map/all_to_all | solution.py:298
  503.0 12.7 %all_to_all.205.full_ref = f32[8,32,512]{2,1,0:T(8,128)S(1)} all-to-all(f32[8,32,512]{2,1,0:T(8,128)S(1)} %get-tuple-element.131.refs_0_), channel_id=1, replica_groups=mesh['layer'=16,'tile'=8] {'tile'}, dimensions={0} | all-to-all | bytes 1048576 | tf_op jit(solution)/shard_map/all_to_all | solution.py:298
  518.6 6.4 collective-permute-done.11
  525.0 13.4 %all_to_all.206.full_ref = f32[8,32,512]{2,1,0:T(8,128)S(1)} all-to-all(f32[8,32,512]{2,1,0:T(8,128)S(1)} %broadcast_in_dim.28), channel_id=1, replica_groups=mesh['layer'=16,'tile'=8] {'tile'}, dimensions={0} | all-to-all | bytes 1048576 | tf_op jit(solution)/shard_map/all_to_all | solution.py:298
  541.2 13.5 %all_to_all.207.full_ref = f32[8,32,512]{2,1,0:T(8,128)S(1)} all-to-all(f32[8,32,512]{2,1,0:T(8,128)S(1)} %get-tuple-element.135.refs_0_), channel_id=1, replica_groups=mesh['layer'=16,'tile'=8] {'tile'}, dimensions={0} | all-to-all | bytes 1048576 | tf_op jit(solution)/shard_map/all_to_all | solution.py:298
  557.4 14.9 %all_to_all.208.full_ref = f32[8,32,512]{2,1,0:T(8,128)S(1)} all-to-all(f32[8,32,512]{2,1,0:T(8,128)S(1)} %get-tuple-element.137.refs_0_), channel_id=1, replica_groups=mesh['layer'=16,'tile'=8] {'tile'}, dimensions={0} | all-to-all | bytes 1048576 | tf_op jit(solution)/shard_map/all_to_all | solution.py:298
  575.0 14.8 %all_to_all.209.full_ref = f32[8,32,512]{2,1,0:T(8,128)S(1)} all-to-all(f32[8,32,512]{2,1,0:T(8,128)S(1)} %get-tuple-element.139.refs_0_), channel_id=1, replica_groups=mesh['layer'=16,'tile'=8] {'tile'}, dimensions={0} | all-to-all | bytes 1048576 | tf_op jit(solution)/shard_map/all_to_all | solution.py:298
  592.7 6.4 collective-permute-done.12
  599.1 12.7 %all_to_all.210.full_ref = f32[8,32,512]{2,1,0:T(8,128)S(1)} all-to-all(f32[8,32,512]{2,1,0:T(8,128)S(1)} %broadcast_in_dim.29), channel_id=1, replica_groups=mesh['layer'=16,'tile'=8] {'tile'}, dimensions={0} | all-to-all | bytes 1048576 | tf_op jit(solution)/shard_map/all_to_all | solution.py:298
  614.6 12.7 %all_to_all.211.full_ref = f32[8,32,512]{2,1,0:T(8,128)S(1)} all-to-all(f32[8,32,512]{2,1,0:T(8,128)S(1)} %get-tuple-element.143.refs_0_), channel_id=1, replica_groups=mesh['layer'=16,'tile'=8] {'tile'}, dimensions={0} | all-to-all | bytes 1048576 | tf_op jit(solution)/shard_map/all_to_all | solution.py:298
  630.1 12.7 %all_to_all.212.full_ref = f32[8,32,512]{2,1,0:T(8,128)S(1)} all-to-all(f32[8,32,512]{2,1,0:T(8,128)S(1)} %get-tuple-element.145.refs_0_), channel_id=1, replica_groups=mesh['layer'=16,'tile'=8] {'tile'}, dimensions={0} | all-to-all | bytes 1048576 | tf_op jit(solution)/shard_map/all_to_all | solution.py:298
  651.5 5.6 shard_map.112
  657.1 5.8 all-to-all-done.35.full_ref
  671.8 5.6 shard_map.114
  (118 shorter events, 148.7 us)
Async XLA Ops:
  2.2 9.9 %collective-permute-start = (f32[2,2,8,512]{3,2,1,0:T(8,128)S(1)}, f32[2,2,8,512]{3,2,1,0:T(8,128)S(1)}, u32[]{:S(2)}, u32[]{:S(2)}) collective-permute-start(f32[2,2,8,512]{3,2,1,0:T(8,128)S(1)} %get-tuple-element.167), channel_id=1, source_target_pairs={{0,8},{8,0},{16,24},{24,16},{32,40},{40,32},{48,56},{56,48},{64,72... | collective-permute-start | bytes 196616 | tf_op jit(solution)/shard_map/ppermute | solution.py:316
  2.2 0.9 copy-start.1
  6.4 21.8 %collective-permute-start.2 = (f32[256,4096]{1,0:T(8,128)}, f32[256,4096]{1,0:T(8,128)}, u32[]{:S(2)}, u32[]{:S(2)}) collective-permute-start(f32[256,4096]{1,0:T(8,128)} %shard_map.68.after_ref), channel_id=1, source_target_pairs={{0,8},{8,0},{16,24},{24,16},{32,40},{40,32},{48,56},{56,48},{64,72... | collective-permute-start | bytes 12582920 | tf_op jit(solution)/shard_map/ppermute | solution.py:321
  10.2 9.3 %copy-start.2 = (bf16[512,128]{1,0:T(8,128)(2,1)S(1)}, bf16[512,128]{1,0:T(8,128)(2,1)}, u32[]{:S(2)}) copy-start(bf16[512,128]{1,0:T(8,128)(2,1)} %after_ref.1) | copy-start | bytes 393220
  10.2 21.3 %collective-permute-start.1 = (f32[256,4096]{1,0:T(8,128)}, f32[256,4096]{1,0:T(8,128)}, u32[]{:S(2)}, u32[]{:S(2)}) collective-permute-start(f32[256,4096]{1,0:T(8,128)} %shard_map.69), channel_id=1, source_target_pairs={{0,8},{8,0},{16,24},{24,16},{32,40},{40,32},{48,56},{56,48},{64,72... | collective-permute-start | bytes 12582920 | tf_op jit(solution)/shard_map/ppermute | solution.py:321
  15.7 31.3 %collective-permute-start.4 = (f32[256,4096]{1,0:T(8,128)}, f32[256,4096]{1,0:T(8,128)}, u32[]{:S(2)}, u32[]{:S(2)}) collective-permute-start(f32[256,4096]{1,0:T(8,128)} %shard_map.74.after_ref), channel_id=1, source_target_pairs={{0,8},{8,0},{16,24},{24,16},{32,40},{40,32},{48,56},{56,48},{64,72... | collective-permute-start | bytes 12582920 | tf_op jit(solution)/shard_map/ppermute | solution.py:321
  19.5 30.9 %collective-permute-start.3 = (f32[256,4096]{1,0:T(8,128)}, f32[256,4096]{1,0:T(8,128)}, u32[]{:S(2)}, u32[]{:S(2)}) collective-permute-start(f32[256,4096]{1,0:T(8,128)} %shard_map.75), channel_id=1, source_target_pairs={{0,8},{8,0},{16,24},{24,16},{32,40},{40,32},{48,56},{56,48},{64,72... | collective-permute-start | bytes 12582920 | tf_op jit(solution)/shard_map/ppermute | solution.py:321
  20.5 19.0 %all-to-all-start = ((f32[8,32,512]{2,1,0:T(8,128)}), f32[8,32,512]{2,1,0:T(8,128)S(1)}, u32[]{:S(2)}, u32[]{:S(2)}) async-start(f32[8,32,512]{2,1,0:T(8,128)} %broadcast_in_dim.21), calls=%async_computation | async-start | bytes 1048576 | tf_op jit(solution)/shard_map/all_to_all | solution.py:298
  43.2 14.2 %all-to-all-start.1 = ((f32[8,32,512]{2,1,0:T(8,128)}), f32[8,32,512]{2,1,0:T(8,128)S(1)}, u32[]{:S(2)}, u32[]{:S(2)}) async-start(f32[8,32,512]{2,1,0:T(8,128)} %get-tuple-element.79.refs_1_.refs_0_), calls=%async_computation.1 | async-start | bytes 1048576 | tf_op jit(solution)/shard_map/all_to_all | solution.py:298
  93.5 6.6 collective-permute-start.5
  163.3 6.6 collective-permute-start.6
  238.1 6.7 collective-permute-start.7
  306.6 6.8 %collective-permute-start.8 = (f32[32,512]{1,0:T(8,128)S(1)}, f32[32,512]{1,0:T(8,128)S(1)}, u32[]{:S(2)}, u32[]{:S(2)}) collective-permute-start(f32[32,512]{1,0:T(8,128)S(1)} %slice_bitcast_fusion.8), channel_id=1, source_target_pairs={{0,16},{8,24},{16,32},{24,40},{32,48},{40,56},{48,64},{56,72},{64,... | collective-permute-start | bytes 196616 | tf_op jit(solution)/shard_map/ppermute | solution.py:379
  378.4 7.0 %collective-permute-start.9 = (f32[32,512]{1,0:T(8,128)S(1)}, f32[32,512]{1,0:T(8,128)S(1)}, u32[]{:S(2)}, u32[]{:S(2)}) collective-permute-start(f32[32,512]{1,0:T(8,128)S(1)} %slice_bitcast_fusion.7), channel_id=1, source_target_pairs={{0,16},{8,24},{16,32},{24,40},{32,48},{40,56},{48,64},{56,72},{64,... | collective-permute-start | bytes 196616 | tf_op jit(solution)/shard_map/ppermute | solution.py:379
  449.4 6.4 collective-permute-start.10
  518.5 6.4 collective-permute-start.11
  592.6 6.4 collective-permute-start.12
  642.8 8.6 %copy-start.4 = (f32[2,8,4,512]{3,2,1,0:T(4,128)S(1)}, f32[2,8,4,512]{3,2,1,0:T(4,128)}, u32[]{:S(2)}) copy-start(f32[2,8,4,512]{3,2,1,0:T(4,128)} %get-tuple-element.150) | copy-start | bytes 393220
  642.8 8.7 %copy-start.3 = (f32[2,8,4,512]{3,2,1,0:T(4,128)S(1)}, f32[2,8,4,512]{3,2,1,0:T(4,128)}, u32[]{:S(2)}) copy-start(f32[2,8,4,512]{3,2,1,0:T(4,128)} %get-tuple-element.149) | copy-start | bytes 393220
  647.8 3.7 collective-permute-start.13
  647.9 14.9 %all-to-all-start.35 = ((f32[8,32,512]{2,1,0:T(8,128)}), f32[8,32,512]{2,1,0:T(8,128)S(1)}, u32[]{:S(2)}, u32[]{:S(2)}) async-start(f32[8,32,512]{2,1,0:T(8,128)} %get-tuple-element.147.refs_0_), calls=%async_computation.35 | async-start | bytes 1048576 | tf_op jit(solution)/shard_map/all_to_all | solution.py:298
  662.9 1.0 copy-start
  668.9 2.9 collective-permute-start.14

commit v3 on v2

--- a/solution.py
+++ b/solution.py
@@ -13,11 +13,12 @@
 PARTS = 2
 PIECES = 2
 GATHERED = 4
-SLOTS = 32
+SLOTS = 48
 NT = (((1,), (1,)), ((), ()))
 VMEM = pl.BlockSpec(memory_space=pltpu.VMEM)
 SMEM = pl.BlockSpec(memory_space=pltpu.SMEM)
 ANYWHERE = pl.BlockSpec(memory_space=pl.ANY)
+STEP_PARAMS = pltpu.CompilerParams(vmem_limit_bytes=36 * 1024 * 1024)
 PARAMS = pltpu.CompilerParams(vmem_limit_bytes=48 * 1024 * 1024)
 
 
@@ -42,58 +43,42 @@
     )(mats, after)
 
 
-def narrow_kernel(mat_ref, *refs):
-    refs[-1][0] = mat_ref[...].astype(jnp.bfloat16)
-
-
-def narrow(mat, layer, part, layers, before):
-    height, orders = mat.shape
+def place_kernel(own_ref, other_ref, *refs, half):
+    core = lax.rem(lax.axis_index("layer"), CORES)
+    refs[-1][...] = jnp.where(core == half, own_ref[0], other_ref[...].astype(jnp.bfloat16))
+
+
+def place(mats, other, layer, part, half, before):
+    height, orders = other.shape
     piece = height // PIECES
-    return pl.pallas_call(
-        narrow_kernel,
-        out_shape=jax.ShapeDtypeStruct((layers, height * PARTS, orders), jnp.bfloat16),
+    aliased = part > 0
+    return pl.pallas_call(
+        functools.partial(place_kernel, half=half),
+        out_shape=jax.ShapeDtypeStruct((height * PARTS, orders), jnp.bfloat16),
         grid=(PIECES,),
-        in_specs=[pl.BlockSpec((piece, orders), lambda p: (p, 0))] + [ANYWHERE] * len(before),
-        out_specs=pl.BlockSpec((1, piece, orders), lambda p: (layer, part * PIECES + p, 0)),
-        input_output_aliases={1: 0} if before else {},
+        in_specs=[
+            pl.BlockSpec((1, piece, orders), lambda p: (layer, part * PIECES + p, 0)),
+            pl.BlockSpec((piece, orders), lambda p: (p, 0)),
+        ]
+        + [ANYWHERE] * len(before),
+        out_specs=pl.BlockSpec((piece, orders), lambda p: (part * PIECES + p, 0)),
+        input_output_aliases={2: 0} if aliased else {},
         compiler_params=PARAMS,
-    )(mat, *before)
+    )(mats, other, *before)
 
 
 def step_kernel(
-    full_ref, phase_ref, own_ref, other_ref, saved_in, *refs, tick, number, layers, ticks
+    full_ref, phase_ref, mat_ref, saved_in, *refs, tick, number, layers, ticks
 ):
-    out_ref, saved_ref, row_buf, mat_buf, sum_buf, row_sem, sems, save_sems = refs[-8:]
+    out_ref, saved_ref, sum_buf, save_sems = refs[-4:]
     blocks, wide, rows = full_ref.shape
     split = wide // 2
-    half, layer = number // layers, number % layers
     member = lax.axis_index("layer")
     core = lax.rem(member, CORES)
     stage = lax.div(member, CORES)
     left = CORES * layers - 1 - number
     late = tick == ticks - 1 and left < 2
     behind = (tick or number) and not (late and left == 0)
-    row_copy = pltpu.make_async_copy(phase_ref.at[number], row_buf, row_sem)
-    row_copy.start()
-
-    def copies(mats_ref):
-        return [
-            pltpu.make_async_copy(
-                mats_ref.at[layer, :, pl.ds(b * rows, rows)], mat_buf.at[b], sems.at[b]
-            )
-            for b in range(blocks)
-        ]
-
-    @pl.when(core == half)
-    def _():
-        for copy in copies(own_ref):
-            copy.start()
-
-    @pl.when(core != half)
-    def _():
-        for copy in copies(other_ref):
-            copy.start()
-
     def chunk_of(tick):
         return (tick >= stage) & (tick - stage < CHUNKS), jnp.clip(tick - stage, 0, CHUNKS - 1)
 
@@ -122,19 +107,17 @@
         def _():
             before_save.start()
 
-    arrivals = copies(own_ref)
     total = jnp.zeros((wide, rows), jnp.float32)
-    row_copy.wait()
     for b in range(blocks):
-        cosine = row_buf[0, b : b + 1, :]
-        sine = row_buf[1, b : b + 1, :]
+        cosine = phase_ref[number, 0, b : b + 1, :]
+        sine = phase_ref[number, 1, b : b + 1, :]
         real_part = full_ref[b, :split, :]
         imag_part = full_ref[b, split:, :]
         phased = jnp.concatenate(
             [cosine * real_part - sine * imag_part, sine * real_part + cosine * imag_part], axis=0
         ).astype(jnp.bfloat16)
-        arrivals[b].wait()
-        total += lax.dot_general(phased, mat_buf[b], NT, preferred_element_type=jnp.float32)
+        mat = mat_ref[:, b * rows : (b + 1) * rows]
+        total += lax.dot_general(phased, mat, NT, preferred_element_type=jnp.float32)
 
     for b in range(blocks):
         out_ref[b] = total
@@ -175,32 +158,28 @@
     )()
 
 
-def layer_step(full, phases, own, other, saved, extra, **place):
+def layer_step(full, phases, mat, saved, extra, **position):
     blocks, wide, rows = full.shape
     return pl.pallas_call(
-        functools.partial(step_kernel, **place),
+        functools.partial(step_kernel, **position),
         out_shape=(
             jax.ShapeDtypeStruct(full.shape, jnp.float32),
             jax.ShapeDtypeStruct(saved.shape, jnp.float32),
         ),
-        in_specs=[VMEM] + [ANYWHERE] * (4 + len(extra)),
+        in_specs=[VMEM] * 3 + [ANYWHERE] * (1 + len(extra)),
         out_specs=(VMEM, ANYWHERE),
-        input_output_aliases={4: 1},
+        input_output_aliases={3: 1},
         scratch_shapes=[
-            pltpu.VMEM(phases.shape[1:], jnp.float32),
-            pltpu.VMEM((blocks, rows, rows), jnp.bfloat16),
             pltpu.VMEM((wide, rows), jnp.float32),
-            pltpu.SemaphoreType.DMA,
-            pltpu.SemaphoreType.DMA((blocks,)),
             pltpu.SemaphoreType.DMA((3,)),
         ],
-        compiler_params=PARAMS,
+        compiler_params=STEP_PARAMS,
         cost_estimate=pl.CostEstimate(
             flops=2 * wide * rows * rows * blocks,
             bytes_accessed=2 * blocks * rows * rows,
             transcendentals=0,
         ),
-    )(full, phases, own, other, saved, *extra)
+    )(full, phases, mat, saved, *extra)
 
 
 def fields_kernel(
@@ -322,7 +301,7 @@
         return pieces, after
 
     arrived = [swap(0, incident)[0]]
-    others = ()
+    mats = {}
     early = jnp.where(core == 0, phases, other_phases)
     late = jnp.where(core == 0, other_phases, phases)
     all_phases = jnp.concatenate([early, late], axis=1)
@@ -359,20 +338,20 @@
         spread = jnp.broadcast_to(inbox[None], (tiles, wide, rows))
         for number in range(CORES * layers):
             full = to_all(spread)
-            if tick == 0 and number < layers:
+            if tick == 0:
+                own, half = number % layers, number // layers
+                mat = ()
                 for piece in range(PARTS):
-                    tied = others + (spread,) * min(number, 1)
                     if number == 0 and piece == 0:
-                        after = whole
-                        for later in range(1, layers):
-                            pieces, after = swap(later, after)
-                            arrived.append(pieces)
-                    others = (narrow(arrived[number][piece], number, piece, layers, tied),)
+                        arrived += [swap(layer, whole)[0] for layer in range(1, layers)]
+                    tied = mat + (spread,) * min(number, 1)
+                    mat = (place(interface, arrived[own][piece], own, piece, half, tied),)
+                mats[number] = mat[0]
             if tick == ticks - 1 and number == CORES * layers - 1:
                 results = finish(0)
                 computed += tuple(results[1:])
             spread, saved = layer_step(
-                full, whole, interface, others[0], saved, computed,
+                full, whole, mats[number], saved, computed,
                 tick=tick, number=number, layers=layers, ticks=ticks,
             )
             computed = (spread,)

time: 689 us -> 669 us (0.971)
  Pallas kernels: 141 us -> 112 us
  blocking collectives: 439 us -> 415 us
  local copies, waits for them, and re-layouts: 7.7 us -> 28.9 us
  starting transfers between devices: 17.1 us -> 26.8 us
    pallas_call x40 -> x44, Pallas kernels: 117 us -> 87.6 us  [the longest x36 63.2 us: layer_step(): pl.pallas_call(functools.partial(step_kernel, **position), out_shape=(jax...]
    all_to_all x33 -> x31, blocking collectives: 439 us -> 415 us  [to_all(): lax.all_to_all(block, 'tile', split_axis=0, concat_axis=0, tiled=False)]
    unnamed x11 -> x39, local copies, waits for them, and re-layouts: 2.07 us -> 23.3 us
    all_to_all x3 -> x5, starting transfers between devices: 14.9 us -> 25 us  [to_all(): lax.all_to_all(block, 'tile', split_axis=0, concat_axis=0, tiled=False)]
    all_to_all x3 -> x5, waiting for transfers between devices: 14.2 us -> 16 us  [to_all(): lax.all_to_all(block, 'tile', split_axis=0, concat_axis=0, tiled=False)]
  transfers between devices with their start and end apart: 18 -> 20, of which waited for: 12 -> 14; matrix products, arithmetic and copies ran while one was open for 0% -> 0% of each run, Pallas kernels for 5% -> 7%
where the time goes in v3:
time: 669 us; the launch traced here: 657 us
  blocking collectives  415 us (62%)
  Pallas kernels  112 us (17%)
  waiting for transfers between devices  70.6 us (11%)
  local copies, waits for them, and re-layouts  28.9 us (4%)
  starting transfers between devices  26.8 us (4%)
    all_to_all x31, blocking collectives, to_all(): lax.all_to_all(block, 'tile', split_axis=0, concat_axis=0, tiled=False)  415 us
    pallas_call x36, Pallas kernels, layer_step(): pl.pallas_call(functools.partial(step_kernel, **position), out_shape=(jax...  63.2 us
    ppermute x8, waiting for transfers between devices, on_device(): received = lax.ppermute(spread[0], 'layer', ring)  51.8 us
    all_to_all x5, starting transfers between devices, to_all(): lax.all_to_all(block, 'tile', split_axis=0, concat_axis=0, tiled=False)  25 us
    pallas_call x8, Pallas kernels, place(): pl.pallas_call(functools.partial(place_kernel, half=half), out_shape=jax....  24.4 us
    unnamed x39, local copies, waits for them, and re-layouts  23.3 us
    all_to_all x5, waiting for transfers between devices, to_all(): lax.all_to_all(block, 'tile', split_axis=0, concat_axis=0, tiled=False)  16 us
    pallas_call x4, Pallas kernels, widen(): pl.pallas_call(widen_kernel, out_shape=jax.ShapeDtypeStruct((height, orde...  13.6 us
  transfers between devices with their start and end apart: 20, of which 14 were waited for; matrix products, arithmetic and copies ran while one was open for 0% of the time, Pallas kernels for 7%

profile of v3, /device:TPU:0, one launch (start us, length us, event | category | flops | bytes accessed | tf_op | source)
XLA Modules:
  0.0 657.4 jit_solution(9274045675561874959)
XLA Ops:
  20.8 7.7 %all-to-all-start = ((f32[8,32,512]{2,1,0:T(8,128)}), f32[8,32,512]{2,1,0:T(8,128)S(1)}, u32[]{:S(2)}, u32[]{:S(2)}) async-start(f32[8,32,512]{2,1,0:T(8,128)} %broadcast_in_dim.21), calls=%async_computation | async-start | bytes 1048576 | tf_op jit(solution)/shard_map/all_to_all | solution.py:277
  44.8 4.2 all-to-all-start.1
  62.1 3.9 shard_map.78
  66.0 4.5 all-to-all-start.2
  83.1 3.9 shard_map.81
  87.0 4.9 all-to-all-start.3
  107.5 6.3 collective-permute-done.5
  113.9 14.8 %all_to_all.180.full_ref = f32[8,32,512]{2,1,0:T(8,128)S(1)} all-to-all(f32[8,32,512]{2,1,0:T(8,128)S(1)} %broadcast_in_dim.22), channel_id=1, replica_groups=mesh['layer'=16,'tile'=8] {'tile'}, dimensions={0} | all-to-all | bytes 1048576 | tf_op jit(solution)/shard_map/all_to_all | solution.py:277
  132.9 12.9 %all_to_all.181.full_ref = f32[8,32,512]{2,1,0:T(8,128)S(1)} all-to-all(f32[8,32,512]{2,1,0:T(8,128)S(1)} %get-tuple-element.87.refs_0_), channel_id=1, replica_groups=mesh['layer'=16,'tile'=8] {'tile'}, dimensions={0} | all-to-all | bytes 1048576 | tf_op jit(solution)/shard_map/all_to_all | solution.py:277
  147.8 13.2 %all_to_all.182.full_ref = f32[8,32,512]{2,1,0:T(8,128)S(1)} all-to-all(f32[8,32,512]{2,1,0:T(8,128)S(1)} %get-tuple-element.89.refs_0_), channel_id=1, replica_groups=mesh['layer'=16,'tile'=8] {'tile'}, dimensions={0} | all-to-all | bytes 1048576 | tf_op jit(solution)/shard_map/all_to_all | solution.py:277
  163.1 12.7 %all_to_all.183.full_ref = f32[8,32,512]{2,1,0:T(8,128)S(1)} all-to-all(f32[8,32,512]{2,1,0:T(8,128)S(1)} %get-tuple-element.91.refs_0_), channel_id=1, replica_groups=mesh['layer'=16,'tile'=8] {'tile'}, dimensions={0} | all-to-all | bytes 1048576 | tf_op jit(solution)/shard_map/all_to_all | solution.py:277
  178.0 6.4 collective-permute-done.6
  184.4 14.5 %all_to_all.184.full_ref = f32[8,32,512]{2,1,0:T(8,128)S(1)} all-to-all(f32[8,32,512]{2,1,0:T(8,128)S(1)} %broadcast_in_dim.23), channel_id=1, replica_groups=mesh['layer'=16,'tile'=8] {'tile'}, dimensions={0} | all-to-all | bytes 1048576 | tf_op jit(solution)/shard_map/all_to_all | solution.py:277
  200.7 15.6 %all_to_all.185.full_ref = f32[8,32,512]{2,1,0:T(8,128)S(1)} all-to-all(f32[8,32,512]{2,1,0:T(8,128)S(1)} %get-tuple-element.95.refs_0_), channel_id=1, replica_groups=mesh['layer'=16,'tile'=8] {'tile'}, dimensions={0} | all-to-all | bytes 1048576 | tf_op jit(solution)/shard_map/all_to_all | solution.py:277
  217.7 14.5 %all_to_all.186.full_ref = f32[8,32,512]{2,1,0:T(8,128)S(1)} all-to-all(f32[8,32,512]{2,1,0:T(8,128)S(1)} %get-tuple-element.97.refs_0_), channel_id=1, replica_groups=mesh['layer'=16,'tile'=8] {'tile'}, dimensions={0} | all-to-all | bytes 1048576 | tf_op jit(solution)/shard_map/all_to_all | solution.py:277
  233.6 12.8 %all_to_all.187.full_ref = f32[8,32,512]{2,1,0:T(8,128)S(1)} all-to-all(f32[8,32,512]{2,1,0:T(8,128)S(1)} %get-tuple-element.99.refs_0_), channel_id=1, replica_groups=mesh['layer'=16,'tile'=8] {'tile'}, dimensions={0} | all-to-all | bytes 1048576 | tf_op jit(solution)/shard_map/all_to_all | solution.py:277
  247.9 6.5 collective-permute-done.7
  254.5 12.5 %all_to_all.188.full_ref = f32[8,32,512]{2,1,0:T(8,128)S(1)} all-to-all(f32[8,32,512]{2,1,0:T(8,128)S(1)} %broadcast_in_dim.24), channel_id=1, replica_groups=mesh['layer'=16,'tile'=8] {'tile'}, dimensions={0} | all-to-all | bytes 1048576 | tf_op jit(solution)/shard_map/all_to_all | solution.py:277
  268.4 12.7 %all_to_all.189.full_ref = f32[8,32,512]{2,1,0:T(8,128)S(1)} all-to-all(f32[8,32,512]{2,1,0:T(8,128)S(1)} %get-tuple-element.103.refs_0_), channel_id=1, replica_groups=mesh['layer'=16,'tile'=8] {'tile'}, dimensions={0} | all-to-all | bytes 1048576 | tf_op jit(solution)/shard_map/all_to_all | solution.py:277
  282.6 12.7 %all_to_all.190.full_ref = f32[8,32,512]{2,1,0:T(8,128)S(1)} all-to-all(f32[8,32,512]{2,1,0:T(8,128)S(1)} %get-tuple-element.105.refs_0_), channel_id=1, replica_groups=mesh['layer'=16,'tile'=8] {'tile'}, dimensions={0} | all-to-all | bytes 1048576 | tf_op jit(solution)/shard_map/all_to_all | solution.py:277
  296.7 13.3 %all_to_all.191.full_ref = f32[8,32,512]{2,1,0:T(8,128)S(1)} all-to-all(f32[8,32,512]{2,1,0:T(8,128)S(1)} %get-tuple-element.107.refs_0_), channel_id=1, replica_groups=mesh['layer'=16,'tile'=8] {'tile'}, dimensions={0} | all-to-all | bytes 1048576 | tf_op jit(solution)/shard_map/all_to_all | solution.py:277
  311.5 6.4 collective-permute-done.8
  318.0 13.4 %all_to_all.192.full_ref = f32[8,32,512]{2,1,0:T(8,128)S(1)} all-to-all(f32[8,32,512]{2,1,0:T(8,128)S(1)} %broadcast_in_dim.25), channel_id=1, replica_groups=mesh['layer'=16,'tile'=8] {'tile'}, dimensions={0} | all-to-all | bytes 1048576 | tf_op jit(solution)/shard_map/all_to_all | solution.py:277
  332.8 15.3 %all_to_all.193.full_ref = f32[8,32,512]{2,1,0:T(8,128)S(1)} all-to-all(f32[8,32,512]{2,1,0:T(8,128)S(1)} %get-tuple-element.111.refs_0_), channel_id=1, replica_groups=mesh['layer'=16,'tile'=8] {'tile'}, dimensions={0} | all-to-all | bytes 1048576 | tf_op jit(solution)/shard_map/all_to_all | solution.py:277
  349.5 12.8 %all_to_all.194.full_ref = f32[8,32,512]{2,1,0:T(8,128)S(1)} all-to-all(f32[8,32,512]{2,1,0:T(8,128)S(1)} %get-tuple-element.113.refs_0_), channel_id=1, replica_groups=mesh['layer'=16,'tile'=8] {'tile'}, dimensions={0} | all-to-all | bytes 1048576 | tf_op jit(solution)/shard_map/all_to_all | solution.py:277
  363.7 12.8 %all_to_all.195.full_ref = f32[8,32,512]{2,1,0:T(8,128)S(1)} all-to-all(f32[8,32,512]{2,1,0:T(8,128)S(1)} %get-tuple-element.115.refs_0_), channel_id=1, replica_groups=mesh['layer'=16,'tile'=8] {'tile'}, dimensions={0} | all-to-all | bytes 1048576 | tf_op jit(solution)/shard_map/all_to_all | solution.py:277
  378.0 6.7 %collective-permute-done.9 = f32[32,512]{1,0:T(8,128)S(1)} collective-permute-done((f32[32,512]{1,0:T(8,128)S(1)}, f32[32,512]{1,0:T(8,128)S(1)}, u32[]{:S(2)}, u32[]{:S(2)}) %collective-permute-start.9) | collective-permute-done | bytes 65568 | tf_op jit(solution)/shard_map/ppermute | solution.py:358
  384.7 12.3 %all_to_all.196.full_ref = f32[8,32,512]{2,1,0:T(8,128)S(1)} all-to-all(f32[8,32,512]{2,1,0:T(8,128)S(1)} %broadcast_in_dim.26), channel_id=1, replica_groups=mesh['layer'=16,'tile'=8] {'tile'}, dimensions={0} | all-to-all | bytes 1048576 | tf_op jit(solution)/shard_map/all_to_all | solution.py:277
  398.5 12.8 %all_to_all.197.full_ref = f32[8,32,512]{2,1,0:T(8,128)S(1)} all-to-all(f32[8,32,512]{2,1,0:T(8,128)S(1)} %get-tuple-element.119.refs_0_), channel_id=1, replica_groups=mesh['layer'=16,'tile'=8] {'tile'}, dimensions={0} | all-to-all | bytes 1048576 | tf_op jit(solution)/shard_map/all_to_all | solution.py:277
  412.7 14.4 %all_to_all.198.full_ref = f32[8,32,512]{2,1,0:T(8,128)S(1)} all-to-all(f32[8,32,512]{2,1,0:T(8,128)S(1)} %get-tuple-element.121.refs_0_), channel_id=1, replica_groups=mesh['layer'=16,'tile'=8] {'tile'}, dimensions={0} | all-to-all | bytes 1048576 | tf_op jit(solution)/shard_map/all_to_all | solution.py:277
  428.5 13.6 %all_to_all.199.full_ref = f32[8,32,512]{2,1,0:T(8,128)S(1)} all-to-all(f32[8,32,512]{2,1,0:T(8,128)S(1)} %get-tuple-element.123.refs_0_), channel_id=1, replica_groups=mesh['layer'=16,'tile'=8] {'tile'}, dimensions={0} | all-to-all | bytes 1048576 | tf_op jit(solution)/shard_map/all_to_all | solution.py:277
  443.6 6.7 %collective-permute-done.10 = f32[32,512]{1,0:T(8,128)S(1)} collective-permute-done((f32[32,512]{1,0:T(8,128)S(1)}, f32[32,512]{1,0:T(8,128)S(1)}, u32[]{:S(2)}, u32[]{:S(2)}) %collective-permute-start.10) | collective-permute-done | bytes 65568 | tf_op jit(solution)/shard_map/ppermute | solution.py:358
  450.4 13.0 %all_to_all.200.full_ref = f32[8,32,512]{2,1,0:T(8,128)S(1)} all-to-all(f32[8,32,512]{2,1,0:T(8,128)S(1)} %broadcast_in_dim.27), channel_id=1, replica_groups=mesh['layer'=16,'tile'=8] {'tile'}, dimensions={0} | all-to-all | bytes 1048576 | tf_op jit(solution)/shard_map/all_to_all | solution.py:277
  464.8 12.6 %all_to_all.201.full_ref = f32[8,32,512]{2,1,0:T(8,128)S(1)} all-to-all(f32[8,32,512]{2,1,0:T(8,128)S(1)} %get-tuple-element.127.refs_0_), channel_id=1, replica_groups=mesh['layer'=16,'tile'=8] {'tile'}, dimensions={0} | all-to-all | bytes 1048576 | tf_op jit(solution)/shard_map/all_to_all | solution.py:277
  478.8 13.0 %all_to_all.202.full_ref = f32[8,32,512]{2,1,0:T(8,128)S(1)} all-to-all(f32[8,32,512]{2,1,0:T(8,128)S(1)} %get-tuple-element.129.refs_0_), channel_id=1, replica_groups=mesh['layer'=16,'tile'=8] {'tile'}, dimensions={0} | all-to-all | bytes 1048576 | tf_op jit(solution)/shard_map/all_to_all | solution.py:277
  493.1 12.7 %all_to_all.203.full_ref = f32[8,32,512]{2,1,0:T(8,128)S(1)} all-to-all(f32[8,32,512]{2,1,0:T(8,128)S(1)} %get-tuple-element.131.refs_0_), channel_id=1, replica_groups=mesh['layer'=16,'tile'=8] {'tile'}, dimensions={0} | all-to-all | bytes 1048576 | tf_op jit(solution)/shard_map/all_to_all | solution.py:277
  507.3 6.5 collective-permute-done.11
  513.9 12.6 %all_to_all.204.full_ref = f32[8,32,512]{2,1,0:T(8,128)S(1)} all-to-all(f32[8,32,512]{2,1,0:T(8,128)S(1)} %broadcast_in_dim.28), channel_id=1, replica_groups=mesh['layer'=16,'tile'=8] {'tile'}, dimensions={0} | all-to-all | bytes 1048576 | tf_op jit(solution)/shard_map/all_to_all | solution.py:277
  527.9 13.3 %all_to_all.205.full_ref = f32[8,32,512]{2,1,0:T(8,128)S(1)} all-to-all(f32[8,32,512]{2,1,0:T(8,128)S(1)} %get-tuple-element.135.refs_0_), channel_id=1, replica_groups=mesh['layer'=16,'tile'=8] {'tile'}, dimensions={0} | all-to-all | bytes 1048576 | tf_op jit(solution)/shard_map/all_to_all | solution.py:277
  542.6 15.1 %all_to_all.206.full_ref = f32[8,32,512]{2,1,0:T(8,128)S(1)} all-to-all(f32[8,32,512]{2,1,0:T(8,128)S(1)} %get-tuple-element.137.refs_0_), channel_id=1, replica_groups=mesh['layer'=16,'tile'=8] {'tile'}, dimensions={0} | all-to-all | bytes 1048576 | tf_op jit(solution)/shard_map/all_to_all | solution.py:277
  559.1 14.8 %all_to_all.207.full_ref = f32[8,32,512]{2,1,0:T(8,128)S(1)} all-to-all(f32[8,32,512]{2,1,0:T(8,128)S(1)} %get-tuple-element.139.refs_0_), channel_id=1, replica_groups=mesh['layer'=16,'tile'=8] {'tile'}, dimensions={0} | all-to-all | bytes 1048576 | tf_op jit(solution)/shard_map/all_to_all | solution.py:277
  575.3 6.4 collective-permute-done.12
  581.8 12.7 %all_to_all.208.full_ref = f32[8,32,512]{2,1,0:T(8,128)S(1)} all-to-all(f32[8,32,512]{2,1,0:T(8,128)S(1)} %broadcast_in_dim.29), channel_id=1, replica_groups=mesh['layer'=16,'tile'=8] {'tile'}, dimensions={0} | all-to-all | bytes 1048576 | tf_op jit(solution)/shard_map/all_to_all | solution.py:277
  595.9 12.7 %all_to_all.209.full_ref = f32[8,32,512]{2,1,0:T(8,128)S(1)} all-to-all(f32[8,32,512]{2,1,0:T(8,128)S(1)} %get-tuple-element.143.refs_0_), channel_id=1, replica_groups=mesh['layer'=16,'tile'=8] {'tile'}, dimensions={0} | all-to-all | bytes 1048576 | tf_op jit(solution)/shard_map/all_to_all | solution.py:277
  610.0 12.7 %all_to_all.210.full_ref = f32[8,32,512]{2,1,0:T(8,128)S(1)} all-to-all(f32[8,32,512]{2,1,0:T(8,128)S(1)} %get-tuple-element.145.refs_0_), channel_id=1, replica_groups=mesh['layer'=16,'tile'=8] {'tile'}, dimensions={0} | all-to-all | bytes 1048576 | tf_op jit(solution)/shard_map/all_to_all | solution.py:277
  630.3 5.6 shard_map.116
  635.8 5.8 all-to-all-done.35.full_ref
  651.5 5.5 shard_map.118
  (152 shorter events, 143.1 us)
Async XLA Ops:
  2.2 10.1 %collective-permute-start = (f32[2,2,8,512]{3,2,1,0:T(8,128)S(1)}, f32[2,2,8,512]{3,2,1,0:T(8,128)S(1)}, u32[]{:S(2)}, u32[]{:S(2)}) collective-permute-start(f32[2,2,8,512]{3,2,1,0:T(8,128)S(1)} %get-tuple-element.167), channel_id=1, source_target_pairs={{0,8},{8,0},{16,24},{24,16},{32,40},{40,32},{48,56},{56,48},{64,72... | collective-permute-start | bytes 196616 | tf_op jit(solution)/shard_map/ppermute | solution.py:295
  2.2 0.9 copy-start.15
  3.1 16.7 %copy-start.16 = (bf16[512,128]{1,0:T(8,128)(2,1)S(1)}, bf16[512,128]{1,0:T(8,128)(2,1)}, u32[]{:S(2)}) copy-start(bf16[512,128]{1,0:T(8,128)(2,1)} %after_ref.1) | copy-start | bytes 393220
  6.6 22.0 %collective-permute-start.2 = (f32[256,4096]{1,0:T(8,128)}, f32[256,4096]{1,0:T(8,128)}, u32[]{:S(2)}, u32[]{:S(2)}) collective-permute-start(f32[256,4096]{1,0:T(8,128)} %shard_map.68.after_ref), channel_id=1, source_target_pairs={{0,8},{8,0},{16,24},{24,16},{32,40},{40,32},{48,56},{56,48},{64,72... | collective-permute-start | bytes 12582920 | tf_op jit(solution)/shard_map/ppermute | solution.py:300
  10.5 21.1 %collective-permute-start.1 = (f32[256,4096]{1,0:T(8,128)}, f32[256,4096]{1,0:T(8,128)}, u32[]{:S(2)}, u32[]{:S(2)}) collective-permute-start(f32[256,4096]{1,0:T(8,128)} %shard_map.69), channel_id=1, source_target_pairs={{0,8},{8,0},{16,24},{24,16},{32,40},{40,32},{48,56},{56,48},{64,72... | collective-permute-start | bytes 12582920 | tf_op jit(solution)/shard_map/ppermute | solution.py:300
  16.0 33.0 %collective-permute-start.4 = (f32[256,4096]{1,0:T(8,128)}, f32[256,4096]{1,0:T(8,128)}, u32[]{:S(2)}, u32[]{:S(2)}) collective-permute-start(f32[256,4096]{1,0:T(8,128)} %shard_map.74.after_ref), channel_id=1, source_target_pairs={{0,8},{8,0},{16,24},{24,16},{32,40},{40,32},{48,56},{56,48},{64,72... | collective-permute-start | bytes 12582920 | tf_op jit(solution)/shard_map/ppermute | solution.py:300
  19.7 32.3 %collective-permute-start.3 = (f32[256,4096]{1,0:T(8,128)}, f32[256,4096]{1,0:T(8,128)}, u32[]{:S(2)}, u32[]{:S(2)}) collective-permute-start(f32[256,4096]{1,0:T(8,128)} %shard_map.75), channel_id=1, source_target_pairs={{0,8},{8,0},{16,24},{24,16},{32,40},{40,32},{48,56},{56,48},{64,72... | collective-permute-start | bytes 12582920 | tf_op jit(solution)/shard_map/ppermute | solution.py:300
  20.8 19.0 %all-to-all-start = ((f32[8,32,512]{2,1,0:T(8,128)}), f32[8,32,512]{2,1,0:T(8,128)S(1)}, u32[]{:S(2)}, u32[]{:S(2)}) async-start(f32[8,32,512]{2,1,0:T(8,128)} %broadcast_in_dim.21), calls=%async_computation | async-start | bytes 1048576 | tf_op jit(solution)/shard_map/all_to_all | solution.py:277
  34.7 2.1 copy-start
  39.8 2.2 copy-start.1
  44.8 15.2 %all-to-all-start.1 = ((f32[8,32,512]{2,1,0:T(8,128)}), f32[8,32,512]{2,1,0:T(8,128)S(1)}, u32[]{:S(2)}, u32[]{:S(2)}) async-start(f32[8,32,512]{2,1,0:T(8,128)} %get-tuple-element.79.refs_0_.refs_1_), calls=%async_computation.1 | async-start | bytes 1048576 | tf_op jit(solution)/shard_map/all_to_all | solution.py:277
  55.1 2.1 copy-start.4
  59.9 2.2 copy-start.5
  66.0 14.9 %all-to-all-start.2 = ((f32[8,32,512]{2,1,0:T(8,128)}), f32[8,32,512]{2,1,0:T(8,128)S(1)}, u32[]{:S(2)}, u32[]{:S(2)}) async-start(f32[8,32,512]{2,1,0:T(8,128)} %get-tuple-element.81.refs_0_.refs_1_), calls=%async_computation.2 | async-start | bytes 1048576 | tf_op jit(solution)/shard_map/all_to_all | solution.py:277
  76.6 2.0 copy-start.7
  80.9 2.2 copy-start.8
  87.0 15.1 %all-to-all-start.3 = ((f32[8,32,512]{2,1,0:T(8,128)}), f32[8,32,512]{2,1,0:T(8,128)S(1)}, u32[]{:S(2)}, u32[]{:S(2)}) async-start(f32[8,32,512]{2,1,0:T(8,128)} %get-tuple-element.83.refs_0_.refs_1_), calls=%async_computation.3 | async-start | bytes 1048576 | tf_op jit(solution)/shard_map/all_to_all | solution.py:277
  98.0 2.0 copy-start.10
  102.1 2.2 copy-start.11
  107.4 6.4 collective-permute-start.5
  128.7 2.2 copy-start.2
  130.9 14.9 %copy-start.6 = (bf16[512,4096]{1,0:T(8,128)(2,1)S(1)}, bf16[512,4096]{1,0:T(8,128)(2,1)}, u32[]{:S(2)}) copy-start(bf16[512,4096]{1,0:T(8,128)(2,1)} %copy-done.4) | copy-start | bytes 12582916
  130.9 30.2 %copy-start.9 = (bf16[512,4096]{1,0:T(8,128)(2,1)S(1)}, bf16[512,4096]{1,0:T(8,128)(2,1)}, u32[]{:S(2)}) copy-start(bf16[512,4096]{1,0:T(8,128)(2,1)} %copy-done.7) | copy-start | bytes 12582916
  145.8 30.0 %copy-start.12 = (bf16[512,4096]{1,0:T(8,128)(2,1)S(1)}, bf16[512,4096]{1,0:T(8,128)(2,1)}, u32[]{:S(2)}) copy-start(bf16[512,4096]{1,0:T(8,128)(2,1)} %copy-done.10) | copy-start | bytes 12582916
  161.1 37.8 %copy-start.3 = (bf16[512,4096]{1,0:T(8,128)(2,1)S(1)}, bf16[512,4096]{1,0:T(8,128)(2,1)}, u32[]{:S(2)}) copy-start(bf16[512,4096]{1,0:T(8,128)(2,1)} %copy-done) | copy-start | bytes 12582916
  177.9 6.4 collective-permute-start.6
  247.8 6.6 %collective-permute-start.7 = (f32[32,512]{1,0:T(8,128)S(1)}, f32[32,512]{1,0:T(8,128)S(1)}, u32[]{:S(2)}, u32[]{:S(2)}) collective-permute-start(f32[32,512]{1,0:T(8,128)S(1)} %slice_bitcast_fusion.9), channel_id=1, source_target_pairs={{0,16},{8,24},{16,32},{24,40},{32,48},{40,56},{48,64},{56,72},{64,... | collective-permute-start | bytes 196616 | tf_op jit(solution)/shard_map/ppermute | solution.py:358
  311.4 6.5 collective-permute-start.8
  377.9 6.8 %collective-permute-start.9 = (f32[32,512]{1,0:T(8,128)S(1)}, f32[32,512]{1,0:T(8,128)S(1)}, u32[]{:S(2)}, u32[]{:S(2)}) collective-permute-start(f32[32,512]{1,0:T(8,128)S(1)} %slice_bitcast_fusion.7), channel_id=1, source_target_pairs={{0,16},{8,24},{16,32},{24,40},{32,48},{40,56},{48,64},{56,72},{64,... | collective-permute-start | bytes 196616 | tf_op jit(solution)/shard_map/ppermute | solution.py:358
  443.5 6.8 %collective-permute-start.10 = (f32[32,512]{1,0:T(8,128)S(1)}, f32[32,512]{1,0:T(8,128)S(1)}, u32[]{:S(2)}, u32[]{:S(2)}) collective-permute-start(f32[32,512]{1,0:T(8,128)S(1)} %slice_bitcast_fusion.6), channel_id=1, source_target_pairs={{0,16},{8,24},{16,32},{24,40},{32,48},{40,56},{48,64},{56,72},{64,... | collective-permute-start | bytes 196616 | tf_op jit(solution)/shard_map/ppermute | solution.py:358
  507.3 6.5 collective-permute-start.11
  575.2 6.4 collective-permute-start.12
  608.6 21.6 %copy-start.18 = (f32[2,8,4,512]{3,2,1,0:T(4,128)S(1)}, f32[2,8,4,512]{3,2,1,0:T(4,128)}, u32[]{:S(2)}) copy-start(f32[2,8,4,512]{3,2,1,0:T(4,128)} %get-tuple-element.149) | copy-start | bytes 393220
  608.6 21.6 %copy-start.17 = (f32[2,8,4,512]{3,2,1,0:T(4,128)S(1)}, f32[2,8,4,512]{3,2,1,0:T(4,128)}, u32[]{:S(2)}) copy-start(f32[2,8,4,512]{3,2,1,0:T(4,128)} %get-tuple-element.150) | copy-start | bytes 393220
  626.3 3.9 collective-permute-start.13
  626.4 15.2 %all-to-all-start.35 = ((f32[8,32,512]{2,1,0:T(8,128)}), f32[8,32,512]{2,1,0:T(8,128)S(1)}, u32[]{:S(2)}, u32[]{:S(2)}) async-start(f32[8,32,512]{2,1,0:T(8,128)} %get-tuple-element.147.refs_0_), calls=%async_computation.35 | async-start | bytes 1048576 | tf_op jit(solution)/shard_map/all_to_all | solution.py:277
  641.6 2.2 copy-start.13
  643.8 1.0 copy-start.14
  648.5 2.9 collective-permute-start.14

commit v4 on v3

--- a/solution.py
+++ b/solution.py
@@ -18,12 +18,13 @@
 VMEM = pl.BlockSpec(memory_space=pltpu.VMEM)
 SMEM = pl.BlockSpec(memory_space=pltpu.SMEM)
 ANYWHERE = pl.BlockSpec(memory_space=pl.ANY)
+PLACE_PARAMS = pltpu.CompilerParams(vmem_limit_bytes=58 * 1024 * 1024)
 STEP_PARAMS = pltpu.CompilerParams(vmem_limit_bytes=36 * 1024 * 1024)
 PARAMS = pltpu.CompilerParams(vmem_limit_bytes=48 * 1024 * 1024)
 
 
-def widen_kernel(mat_ref, after_ref, out_ref):
-    out_ref[...] = mat_ref[0].astype(jnp.float32)
+def widen_kernel(mat_ref, *refs):
+    refs[-1][...] = mat_ref[0].astype(jnp.float32)
 
 
 def widen(mats, layer, part, after):
@@ -36,34 +37,47 @@
         grid=(PIECES,),
         in_specs=[
             pl.BlockSpec((1, piece, orders), lambda p: (layer, part * PIECES + p, 0)),
-            ANYWHERE,
-        ],
+        ]
+        + [ANYWHERE] * len(after),
         out_specs=pl.BlockSpec((piece, orders), lambda p: (p, 0)),
         compiler_params=PARAMS,
-    )(mats, after)
-
-
-def place_kernel(own_ref, other_ref, *refs, half):
+    )(mats, *after)
+
+
+def place_kernel(own_ref, other_ref, *refs):
+    early_ref, late_ref = refs[-2:]
     core = lax.rem(lax.axis_index("layer"), CORES)
-    refs[-1][...] = jnp.where(core == half, own_ref[0], other_ref[...].astype(jnp.bfloat16))
-
-
-def place(mats, other, layer, part, half, before):
+    own = own_ref[0]
+    other = other_ref[...].astype(jnp.bfloat16)
+
+    @pl.when(core == 0)
+    def _():
+        early_ref[...] = own
+        late_ref[...] = other
+
+    @pl.when(core != 0)
+    def _():
+        early_ref[...] = other
+        late_ref[...] = own
+
+
+def place(mats, other, layer, part, before):
     height, orders = other.shape
     piece = height // PIECES
-    aliased = part > 0
-    return pl.pallas_call(
-        functools.partial(place_kernel, half=half),
-        out_shape=jax.ShapeDtypeStruct((height * PARTS, orders), jnp.bfloat16),
+    out = jax.ShapeDtypeStruct((height * PARTS, orders), jnp.bfloat16)
+    spec = pl.BlockSpec((piece, orders), lambda p: (part * PIECES + p, 0))
+    return pl.pallas_call(
+        place_kernel,
+        out_shape=(out, out),
         grid=(PIECES,),
         in_specs=[
             pl.BlockSpec((1, piece, orders), lambda p: (layer, part * PIECES + p, 0)),
             pl.BlockSpec((piece, orders), lambda p: (p, 0)),
         ]
         + [ANYWHERE] * len(before),
-        out_specs=pl.BlockSpec((piece, orders), lambda p: (part * PIECES + p, 0)),
-        input_output_aliases={2: 0} if aliased else {},
-        compiler_params=PARAMS,
+        out_specs=(spec, spec),
+        input_output_aliases={2: 0, 3: 1} if part > 0 else {},
+        compiler_params=PLACE_PARAMS,
     )(mats, other, *before)
 
 
@@ -87,19 +101,22 @@
         return (number % layers * CORES + kind) * CHUNKS + chunk
 
     valid, chunk = chunk_of(tick)
-    block_save = pltpu.make_async_copy(
-        full_ref, saved_ref.at[entry(number, chunk), pl.ds(0, blocks)], save_sems.at[0]
-    )
+    place = entry(number, chunk)
+    block_saves = [
+        pltpu.make_async_copy(full_ref.at[b], saved_ref.at[place, b], save_sems.at[b])
+        for b in range(blocks)
+    ]
     if behind:
         before = (number - 1) % (CORES * layers)
         before_valid, before_chunk = chunk_of(tick - (number == 0))
         before_save = pltpu.make_async_copy(
-            refs[0].at[0], saved_ref.at[entry(before, before_chunk), blocks], save_sems.at[1]
+            refs[0].at[0], saved_ref.at[entry(before, before_chunk), blocks], save_sems.at[blocks]
         )
 
     @pl.when(valid)
     def _():
-        block_save.start()
+        for copy in block_saves:
+            copy.start()
 
     if behind:
 
@@ -125,7 +142,7 @@
     if late:
         sum_buf[...] = total
         sum_save = pltpu.make_async_copy(
-            sum_buf, saved_ref.at[entry(number, chunk), blocks], save_sems.at[2]
+            sum_buf, saved_ref.at[place, blocks], save_sems.at[blocks + 1]
         )
 
         @pl.when(valid)
@@ -135,7 +152,8 @@
 
     @pl.when(valid)
     def _():
-        block_save.wait()
+        for copy in block_saves:
+            copy.wait()
 
     if behind:
 
@@ -171,7 +189,7 @@
         input_output_aliases={3: 1},
         scratch_shapes=[
             pltpu.VMEM((wide, rows), jnp.float32),
-            pltpu.SemaphoreType.DMA((3,)),
+            pltpu.SemaphoreType.DMA((blocks + 2,)),
         ],
         compiler_params=STEP_PARAMS,
         cost_estimate=pl.CostEstimate(
@@ -185,7 +203,7 @@
 def fields_kernel(
     core_ref, own_ref, other_ref, own_leave_ref, other_leave_ref, cos_ref, sin_ref, mat_ref, *refs
 ):
-    out_ref, leave_ref, total = refs[-3:]
+    out_ref, leave_ref, token_ref, total = refs[-4:]
     step = pl.program_id(0)
     chunks, gathered, wide, rows = other_ref.shape
     half = wide // 2
@@ -215,6 +233,7 @@
     @pl.when(step == 0)
     def _():
         total[...] = partial
+        token_ref[...] = jnp.zeros_like(token_ref)
         leave = [
             columns(own_leave_ref, other_leave_ref, 0, part)
             for part in (slice(0, half), slice(half, wide))
@@ -248,6 +267,7 @@
         out_shape=(
             jax.ShapeDtypeStruct((layers, rows, cols), jnp.bfloat16),
             jax.ShapeDtypeStruct((layers, rows, width), jnp.float32),
+            jax.ShapeDtypeStruct((8, 128), jnp.float32),
         ),
         grid_spec=pltpu.PrefetchScalarGridSpec(
             num_scalar_prefetch=1,
@@ -265,6 +285,7 @@
             out_specs=(
                 pl.BlockSpec((1, rows, cols), lambda b, c: (layer, 0, 0)),
                 pl.BlockSpec((1, rows, width), lambda b, c: (layer, 0, 0)),
+                pl.BlockSpec((8, 128), lambda b, c: (0, 0)),
             ),
             scratch_shapes=[pltpu.VMEM((rows, cols), jnp.float32)],
         ),
@@ -296,11 +317,11 @@
     def swap(layer, after):
         pieces = []
         for piece in range(PARTS):
-            after = widen(interface, layer, piece, after)
-            pieces.append(lax.ppermute(after, "layer", partner))
+            after = (widen(interface, layer, piece, after),)
+            pieces.append(lax.ppermute(after[0], "layer", partner))
         return pieces, after
 
-    arrived = [swap(0, incident)[0]]
+    arrived = [swap(0, ())[0]]
     mats = {}
     early = jnp.where(core == 0, phases, other_phases)
     late = jnp.where(core == 0, other_phases, phases)
@@ -326,7 +347,7 @@
         first = (layer * CORES + 1) * CHUNKS
         other = lax.ppermute(saved[first : first + CHUNKS], "layer", partner)
         return layer_fields(
-            core.reshape(1), saved, other, cosines[layer], sines[layer], eigvec, layer, results
+            core.reshape(1), saved, other, cosines[layer], sines[layer], eigvec, layer, results[:2]
         )
 
     received = None
@@ -338,18 +359,18 @@
         spread = jnp.broadcast_to(inbox[None], (tiles, wide, rows))
         for number in range(CORES * layers):
             full = to_all(spread)
-            if tick == 0:
-                own, half = number % layers, number // layers
-                mat = ()
+            if tick == 0 and number < layers:
+                pair = ()
                 for piece in range(PARTS):
                     if number == 0 and piece == 0:
-                        arrived += [swap(layer, whole)[0] for layer in range(1, layers)]
-                    tied = mat + (spread,) * min(number, 1)
-                    mat = (place(interface, arrived[own][piece], own, piece, half, tied),)
-                mats[number] = mat[0]
+                        arrived += [swap(layer, (whole,))[0] for layer in range(1, layers)]
+                    tied = pair + (spread,) * min(number, 1)
+                    pair = tuple(place(interface, arrived[number][piece], number, piece, tied))
+                for half in range(CORES):
+                    mats[half * layers + number] = pair[half]
             if tick == ticks - 1 and number == CORES * layers - 1:
                 results = finish(0)
-                computed += tuple(results[1:])
+                computed += tuple(results[2:])
             spread, saved = layer_step(
                 full, whole, mats[number], saved, computed,
                 tick=tick, number=number, layers=layers, ticks=ticks,
@@ -359,7 +380,7 @@
 
     for layer in range(1, layers):
         results = finish(layer)
-    return results
+    return results[:2]
 
 
 def solution(mesh):

time: 669 us -> 658 us (0.984)
  blocking collectives: 415 us -> 441 us
  waiting for transfers between devices: 70.6 us -> 51.8 us
  local copies, waits for them, and re-layouts: 28.9 us -> 14.7 us
  Pallas kernels: 112 us -> 105 us
    all_to_all x31 -> x33, blocking collectives: 415 us -> 441 us  [to_all(): lax.all_to_all(block, 'tile', split_axis=0, concat_axis=0, tiled=False)]
    unnamed x39 -> x27, local copies, waits for them, and re-layouts: 23.3 us -> 9.05 us
    ppermute x8, waiting for transfers between devices: 51.8 us -> 39.3 us  [on_device(): received = lax.ppermute(spread[0], 'layer', ring)]
    ppermute x8, starting transfers between devices: 0.65 us -> 12.5 us  [on_device(): received = lax.ppermute(spread[0], 'layer', ring)]
    all_to_all x5 -> x3, starting transfers between devices: 25 us -> 16.6 us  [to_all(): lax.all_to_all(block, 'tile', split_axis=0, concat_axis=0, tiled=False)]
    all_to_all x5 -> x3, waiting for transfers between devices: 16 us -> 9.6 us  [to_all(): lax.all_to_all(block, 'tile', split_axis=0, concat_axis=0, tiled=False)]
    pallas_call x8 -> x4, Pallas kernels: 24.4 us -> 18.4 us  [place(): pl.pallas_call(place_kernel, out_shape=(out, out), grid=(PIECES,), in_spe...]
  transfers between devices with their start and end apart: 20 -> 18, of which waited for: 14 -> 12; matrix products, arithmetic and copies ran while one was open for 0% -> 0% of each run, Pallas kernels for 7% -> 6%
where the time goes in v4:
time: 658 us; the launch traced here: 647 us
  blocking collectives  441 us (67%)
  Pallas kernels  105 us (16%)
  waiting for transfers between devices  51.8 us (8%)
  starting transfers between devices  30.4 us (5%)
  local copies, waits for them, and re-layouts  14.7 us (2%)
    all_to_all x33, blocking collectives, to_all(): lax.all_to_all(block, 'tile', split_axis=0, concat_axis=0, tiled=False)  441 us
    pallas_call x36, Pallas kernels, layer_step(): pl.pallas_call(functools.partial(step_kernel, **position), out_shape=(jax...  62 us
    ppermute x8, waiting for transfers between devices, on_device(): received = lax.ppermute(spread[0], 'layer', ring)  39.3 us
    pallas_call x4, Pallas kernels, place(): pl.pallas_call(place_kernel, out_shape=(out, out), grid=(PIECES,), in_spe...  18.4 us
    all_to_all x3, starting transfers between devices, to_all(): lax.all_to_all(block, 'tile', split_axis=0, concat_axis=0, tiled=False)  16.6 us
    pallas_call x4, Pallas kernels, widen(): pl.pallas_call(widen_kernel, out_shape=jax.ShapeDtypeStruct((height, orde...  13.5 us
  transfers between devices with their start and end apart: 18, of which 12 were waited for; matrix products, arithmetic and copies ran while one was open for 0% of the time, Pallas kernels for 6%

profile of v4, /device:TPU:0, one launch (start us, length us, event | category | flops | bytes accessed | tf_op | source)
XLA Modules:
  0.0 646.5 jit_solution(1515501828141637844)
XLA Ops:
  19.9 7.7 %all-to-all-start = ((f32[8,32,512]{2,1,0:T(8,128)}), f32[8,32,512]{2,1,0:T(8,128)S(1)}, u32[]{:S(2)}, u32[]{:S(2)}) async-start(f32[8,32,512]{2,1,0:T(8,128)} %broadcast_in_dim.21), calls=%async_computation | async-start | bytes 1048576 | tf_op jit(solution)/shard_map/all_to_all | solution.py:298
  27.6 4.6 shard_map.70
  32.2 4.6 shard_map.71
  43.9 5.1 all-to-all-start.1
  49.1 4.6 shard_map.76
  53.7 4.6 shard_map.77
  65.5 16.0 %all_to_all.180.full_ref = f32[8,32,512]{2,1,0:T(8,128)S(1)} all-to-all(f32[8,32,512]{2,1,0:T(8,128)S(1)} %get-tuple-element.98.refs_0_), channel_id=1, replica_groups=mesh['layer'=16,'tile'=8] {'tile'}, dimensions={0} | all-to-all | bytes 1048576 | tf_op jit(solution)/shard_map/all_to_all | solution.py:298
  83.7 12.7 %all_to_all.181.full_ref = f32[8,32,512]{2,1,0:T(8,128)S(1)} all-to-all(f32[8,32,512]{2,1,0:T(8,128)S(1)} %get-tuple-element.101.refs_0_), channel_id=1, replica_groups=mesh['layer'=16,'tile'=8] {'tile'}, dimensions={0} | all-to-all | bytes 1048576 | tf_op jit(solution)/shard_map/all_to_all | solution.py:298
  98.7 6.6 %collective-permute-done.5 = f32[32,512]{1,0:T(8,128)S(1)} collective-permute-done((f32[32,512]{1,0:T(8,128)S(1)}, f32[32,512]{1,0:T(8,128)S(1)}, u32[]{:S(2)}, u32[]{:S(2)}) %collective-permute-start.5) | collective-permute-done | bytes 65568 | tf_op jit(solution)/shard_map/ppermute | solution.py:379
  105.3 13.0 %all_to_all.182.full_ref = f32[8,32,512]{2,1,0:T(8,128)S(1)} all-to-all(f32[8,32,512]{2,1,0:T(8,128)S(1)} %broadcast_in_dim.22), channel_id=1, replica_groups=mesh['layer'=16,'tile'=8] {'tile'}, dimensions={0} | all-to-all | bytes 1048576 | tf_op jit(solution)/shard_map/all_to_all | solution.py:298
  122.7 13.3 %all_to_all.183.full_ref = f32[8,32,512]{2,1,0:T(8,128)S(1)} all-to-all(f32[8,32,512]{2,1,0:T(8,128)S(1)} %get-tuple-element.106.refs_0_), channel_id=1, replica_groups=mesh['layer'=16,'tile'=8] {'tile'}, dimensions={0} | all-to-all | bytes 1048576 | tf_op jit(solution)/shard_map/all_to_all | solution.py:298
  138.2 12.7 %all_to_all.184.full_ref = f32[8,32,512]{2,1,0:T(8,128)S(1)} all-to-all(f32[8,32,512]{2,1,0:T(8,128)S(1)} %get-tuple-element.108.refs_0_), channel_id=1, replica_groups=mesh['layer'=16,'tile'=8] {'tile'}, dimensions={0} | all-to-all | bytes 1048576 | tf_op jit(solution)/shard_map/all_to_all | solution.py:298
  153.0 12.7 %all_to_all.185.full_ref = f32[8,32,512]{2,1,0:T(8,128)S(1)} all-to-all(f32[8,32,512]{2,1,0:T(8,128)S(1)} %get-tuple-element.110.refs_0_), channel_id=1, replica_groups=mesh['layer'=16,'tile'=8] {'tile'}, dimensions={0} | all-to-all | bytes 1048576 | tf_op jit(solution)/shard_map/all_to_all | solution.py:298
  168.0 6.4 collective-permute-done.6
  174.4 14.9 %all_to_all.186.full_ref = f32[8,32,512]{2,1,0:T(8,128)S(1)} all-to-all(f32[8,32,512]{2,1,0:T(8,128)S(1)} %broadcast_in_dim.23), channel_id=1, replica_groups=mesh['layer'=16,'tile'=8] {'tile'}, dimensions={0} | all-to-all | bytes 1048576 | tf_op jit(solution)/shard_map/all_to_all | solution.py:298
  191.3 14.3 %all_to_all.187.full_ref = f32[8,32,512]{2,1,0:T(8,128)S(1)} all-to-all(f32[8,32,512]{2,1,0:T(8,128)S(1)} %get-tuple-element.114.refs_0_), channel_id=1, replica_groups=mesh['layer'=16,'tile'=8] {'tile'}, dimensions={0} | all-to-all | bytes 1048576 | tf_op jit(solution)/shard_map/all_to_all | solution.py:298
  207.0 13.6 %all_to_all.188.full_ref = f32[8,32,512]{2,1,0:T(8,128)S(1)} all-to-all(f32[8,32,512]{2,1,0:T(8,128)S(1)} %get-tuple-element.116.refs_0_), channel_id=1, replica_groups=mesh['layer'=16,'tile'=8] {'tile'}, dimensions={0} | all-to-all | bytes 1048576 | tf_op jit(solution)/shard_map/all_to_all | solution.py:298
  222.1 13.0 %all_to_all.189.full_ref = f32[8,32,512]{2,1,0:T(8,128)S(1)} all-to-all(f32[8,32,512]{2,1,0:T(8,128)S(1)} %get-tuple-element.118.refs_0_), channel_id=1, replica_groups=mesh['layer'=16,'tile'=8] {'tile'}, dimensions={0} | all-to-all | bytes 1048576 | tf_op jit(solution)/shard_map/all_to_all | solution.py:298
  238.8 4.2 collective-permute-done.7
  243.1 13.1 %all_to_all.190.full_ref = f32[8,32,512]{2,1,0:T(8,128)S(1)} all-to-all(f32[8,32,512]{2,1,0:T(8,128)S(1)} %broadcast_in_dim.24), channel_id=1, replica_groups=mesh['layer'=16,'tile'=8] {'tile'}, dimensions={0} | all-to-all | bytes 1048576 | tf_op jit(solution)/shard_map/all_to_all | solution.py:298
  257.7 12.7 %all_to_all.191.full_ref = f32[8,32,512]{2,1,0:T(8,128)S(1)} all-to-all(f32[8,32,512]{2,1,0:T(8,128)S(1)} %get-tuple-element.122.refs_0_), channel_id=1, replica_groups=mesh['layer'=16,'tile'=8] {'tile'}, dimensions={0} | all-to-all | bytes 1048576 | tf_op jit(solution)/shard_map/all_to_all | solution.py:298
  271.9 12.7 %all_to_all.192.full_ref = f32[8,32,512]{2,1,0:T(8,128)S(1)} all-to-all(f32[8,32,512]{2,1,0:T(8,128)S(1)} %get-tuple-element.124.refs_0_), channel_id=1, replica_groups=mesh['layer'=16,'tile'=8] {'tile'}, dimensions={0} | all-to-all | bytes 1048576 | tf_op jit(solution)/shard_map/all_to_all | solution.py:298
  286.1 12.9 %all_to_all.193.full_ref = f32[8,32,512]{2,1,0:T(8,128)S(1)} all-to-all(f32[8,32,512]{2,1,0:T(8,128)S(1)} %get-tuple-element.126.refs_0_), channel_id=1, replica_groups=mesh['layer'=16,'tile'=8] {'tile'}, dimensions={0} | all-to-all | bytes 1048576 | tf_op jit(solution)/shard_map/all_to_all | solution.py:298
  301.1 5.9 collective-permute-done.8
  307.0 15.5 %all_to_all.194.full_ref = f32[8,32,512]{2,1,0:T(8,128)S(1)} all-to-all(f32[8,32,512]{2,1,0:T(8,128)S(1)} %broadcast_in_dim.25), channel_id=1, replica_groups=mesh['layer'=16,'tile'=8] {'tile'}, dimensions={0} | all-to-all | bytes 1048576 | tf_op jit(solution)/shard_map/all_to_all | solution.py:298
  324.0 14.8 %all_to_all.195.full_ref = f32[8,32,512]{2,1,0:T(8,128)S(1)} all-to-all(f32[8,32,512]{2,1,0:T(8,128)S(1)} %get-tuple-element.130.refs_0_), channel_id=1, replica_groups=mesh['layer'=16,'tile'=8] {'tile'}, dimensions={0} | all-to-all | bytes 1048576 | tf_op jit(solution)/shard_map/all_to_all | solution.py:298
  340.3 12.7 %all_to_all.196.full_ref = f32[8,32,512]{2,1,0:T(8,128)S(1)} all-to-all(f32[8,32,512]{2,1,0:T(8,128)S(1)} %get-tuple-element.132.refs_0_), channel_id=1, replica_groups=mesh['layer'=16,'tile'=8] {'tile'}, dimensions={0} | all-to-all | bytes 1048576 | tf_op jit(solution)/shard_map/all_to_all | solution.py:298
  354.5 13.5 %all_to_all.197.full_ref = f32[8,32,512]{2,1,0:T(8,128)S(1)} all-to-all(f32[8,32,512]{2,1,0:T(8,128)S(1)} %get-tuple-element.134.refs_0_), channel_id=1, replica_groups=mesh['layer'=16,'tile'=8] {'tile'}, dimensions={0} | all-to-all | bytes 1048576 | tf_op jit(solution)/shard_map/all_to_all | solution.py:298
  376.0 12.7 %all_to_all.198.full_ref = f32[8,32,512]{2,1,0:T(8,128)S(1)} all-to-all(f32[8,32,512]{2,1,0:T(8,128)S(1)} %broadcast_in_dim.26), channel_id=1, replica_groups=mesh['layer'=16,'tile'=8] {'tile'}, dimensions={0} | all-to-all | bytes 1048576 | tf_op jit(solution)/shard_map/all_to_all | solution.py:298
  390.1 12.8 %all_to_all.199.full_ref = f32[8,32,512]{2,1,0:T(8,128)S(1)} all-to-all(f32[8,32,512]{2,1,0:T(8,128)S(1)} %get-tuple-element.138.refs_0_), channel_id=1, replica_groups=mesh['layer'=16,'tile'=8] {'tile'}, dimensions={0} | all-to-all | bytes 1048576 | tf_op jit(solution)/shard_map/all_to_all | solution.py:298
  404.4 13.1 %all_to_all.200.full_ref = f32[8,32,512]{2,1,0:T(8,128)S(1)} all-to-all(f32[8,32,512]{2,1,0:T(8,128)S(1)} %get-tuple-element.140.refs_0_), channel_id=1, replica_groups=mesh['layer'=16,'tile'=8] {'tile'}, dimensions={0} | all-to-all | bytes 1048576 | tf_op jit(solution)/shard_map/all_to_all | solution.py:298
  419.0 12.6 %all_to_all.201.full_ref = f32[8,32,512]{2,1,0:T(8,128)S(1)} all-to-all(f32[8,32,512]{2,1,0:T(8,128)S(1)} %get-tuple-element.142.refs_0_), channel_id=1, replica_groups=mesh['layer'=16,'tile'=8] {'tile'}, dimensions={0} | all-to-all | bytes 1048576 | tf_op jit(solution)/shard_map/all_to_all | solution.py:298
  434.1 5.4 collective-permute-done.10
  439.6 15.3 %all_to_all.202.full_ref = f32[8,32,512]{2,1,0:T(8,128)S(1)} all-to-all(f32[8,32,512]{2,1,0:T(8,128)S(1)} %broadcast_in_dim.27), channel_id=1, replica_groups=mesh['layer'=16,'tile'=8] {'tile'}, dimensions={0} | all-to-all | bytes 1048576 | tf_op jit(solution)/shard_map/all_to_all | solution.py:298
  456.4 13.4 %all_to_all.203.full_ref = f32[8,32,512]{2,1,0:T(8,128)S(1)} all-to-all(f32[8,32,512]{2,1,0:T(8,128)S(1)} %get-tuple-element.146.refs_0_), channel_id=1, replica_groups=mesh['layer'=16,'tile'=8] {'tile'}, dimensions={0} | all-to-all | bytes 1048576 | tf_op jit(solution)/shard_map/all_to_all | solution.py:298
  471.2 12.7 %all_to_all.204.full_ref = f32[8,32,512]{2,1,0:T(8,128)S(1)} all-to-all(f32[8,32,512]{2,1,0:T(8,128)S(1)} %get-tuple-element.148.refs_0_), channel_id=1, replica_groups=mesh['layer'=16,'tile'=8] {'tile'}, dimensions={0} | all-to-all | bytes 1048576 | tf_op jit(solution)/shard_map/all_to_all | solution.py:298
  485.4 13.6 %all_to_all.205.full_ref = f32[8,32,512]{2,1,0:T(8,128)S(1)} all-to-all(f32[8,32,512]{2,1,0:T(8,128)S(1)} %get-tuple-element.150.refs_0_), channel_id=1, replica_groups=mesh['layer'=16,'tile'=8] {'tile'}, dimensions={0} | all-to-all | bytes 1048576 | tf_op jit(solution)/shard_map/all_to_all | solution.py:298
  507.0 13.1 %all_to_all.206.full_ref = f32[8,32,512]{2,1,0:T(8,128)S(1)} all-to-all(f32[8,32,512]{2,1,0:T(8,128)S(1)} %broadcast_in_dim.28), channel_id=1, replica_groups=mesh['layer'=16,'tile'=8] {'tile'}, dimensions={0} | all-to-all | bytes 1048576 | tf_op jit(solution)/shard_map/all_to_all | solution.py:298
  521.6 13.6 %all_to_all.207.full_ref = f32[8,32,512]{2,1,0:T(8,128)S(1)} all-to-all(f32[8,32,512]{2,1,0:T(8,128)S(1)} %get-tuple-element.154.refs_0_), channel_id=1, replica_groups=mesh['layer'=16,'tile'=8] {'tile'}, dimensions={0} | all-to-all | bytes 1048576 | tf_op jit(solution)/shard_map/all_to_all | solution.py:298
  536.7 12.8 %all_to_all.208.full_ref = f32[8,32,512]{2,1,0:T(8,128)S(1)} all-to-all(f32[8,32,512]{2,1,0:T(8,128)S(1)} %get-tuple-element.156.refs_0_), channel_id=1, replica_groups=mesh['layer'=16,'tile'=8] {'tile'}, dimensions={0} | all-to-all | bytes 1048576 | tf_op jit(solution)/shard_map/all_to_all | solution.py:298
  551.0 12.6 %all_to_all.209.full_ref = f32[8,32,512]{2,1,0:T(8,128)S(1)} all-to-all(f32[8,32,512]{2,1,0:T(8,128)S(1)} %get-tuple-element.158.refs_0_), channel_id=1, replica_groups=mesh['layer'=16,'tile'=8] {'tile'}, dimensions={0} | all-to-all | bytes 1048576 | tf_op jit(solution)/shard_map/all_to_all | solution.py:298
  566.2 5.3 collective-permute-done.12
  571.6 12.7 %all_to_all.210.full_ref = f32[8,32,512]{2,1,0:T(8,128)S(1)} all-to-all(f32[8,32,512]{2,1,0:T(8,128)S(1)} %broadcast_in_dim.29), channel_id=1, replica_groups=mesh['layer'=16,'tile'=8] {'tile'}, dimensions={0} | all-to-all | bytes 1048576 | tf_op jit(solution)/shard_map/all_to_all | solution.py:298
  585.8 12.7 %all_to_all.211.full_ref = f32[8,32,512]{2,1,0:T(8,128)S(1)} all-to-all(f32[8,32,512]{2,1,0:T(8,128)S(1)} %get-tuple-element.162.refs_0_), channel_id=1, replica_groups=mesh['layer'=16,'tile'=8] {'tile'}, dimensions={0} | all-to-all | bytes 1048576 | tf_op jit(solution)/shard_map/all_to_all | solution.py:298
  600.0 12.7 %all_to_all.212.full_ref = f32[8,32,512]{2,1,0:T(8,128)S(1)} all-to-all(f32[8,32,512]{2,1,0:T(8,128)S(1)} %get-tuple-element.164.refs_0_), channel_id=1, replica_groups=mesh['layer'=16,'tile'=8] {'tile'}, dimensions={0} | all-to-all | bytes 1048576 | tf_op jit(solution)/shard_map/all_to_all | solution.py:298
  620.4 5.6 shard_map.112
  626.0 5.8 all-to-all-done.35.full_ref
  640.5 5.6 shard_map.114
  (134 shorter events, 122.0 us)
Async XLA Ops:
  2.2 16.7 %copy-start.12 = (bf16[512,128]{1,0:T(8,128)(2,1)S(1)}, bf16[512,128]{1,0:T(8,128)(2,1)}, u32[]{:S(2)}) copy-start(bf16[512,128]{1,0:T(8,128)(2,1)} %param.5) | copy-start | bytes 393220
  2.2 9.1 %collective-permute-start = (f32[2,2,8,512]{3,2,1,0:T(8,128)S(1)}, f32[2,2,8,512]{3,2,1,0:T(8,128)S(1)}, u32[]{:S(2)}, u32[]{:S(2)}) collective-permute-start(f32[2,2,8,512]{3,2,1,0:T(8,128)S(1)} %get-tuple-element.189), channel_id=1, source_target_pairs={{0,8},{8,0},{16,24},{24,16},{32,40},{40,32},{48,56},{56,48},{64,72... | collective-permute-start | bytes 196616 | tf_op jit(solution)/shard_map/ppermute | solution.py:316
  5.6 22.0 %collective-permute-start.2 = (f32[256,4096]{1,0:T(8,128)}, f32[256,4096]{1,0:T(8,128)}, u32[]{:S(2)}, u32[]{:S(2)}) collective-permute-start(f32[256,4096]{1,0:T(8,128)} %shard_map.68.refs_0_), channel_id=1, source_target_pairs={{0,8},{8,0},{16,24},{24,16},{32,40},{40,32},{48,56},{56,48},{64,72... | collective-permute-start | bytes 12582920 | tf_op jit(solution)/shard_map/ppermute | solution.py:321
  9.5 22.7 %collective-permute-start.1 = (f32[256,4096]{1,0:T(8,128)}, f32[256,4096]{1,0:T(8,128)}, u32[]{:S(2)}, u32[]{:S(2)}) collective-permute-start(f32[256,4096]{1,0:T(8,128)} %shard_map.69), channel_id=1, source_target_pairs={{0,8},{8,0},{16,24},{24,16},{32,40},{40,32},{48,56},{56,48},{64,72... | collective-permute-start | bytes 12582920 | tf_op jit(solution)/shard_map/ppermute | solution.py:321
  14.9 34.2 %collective-permute-start.4 = (f32[256,4096]{1,0:T(8,128)}, f32[256,4096]{1,0:T(8,128)}, u32[]{:S(2)}, u32[]{:S(2)}) collective-permute-start(f32[256,4096]{1,0:T(8,128)} %shard_map.74.refs_0_), channel_id=1, source_target_pairs={{0,8},{8,0},{16,24},{24,16},{32,40},{40,32},{48,56},{56,48},{64,72... | collective-permute-start | bytes 12582920 | tf_op jit(solution)/shard_map/ppermute | solution.py:321
  18.8 34.9 %collective-permute-start.3 = (f32[256,4096]{1,0:T(8,128)}, f32[256,4096]{1,0:T(8,128)}, u32[]{:S(2)}, u32[]{:S(2)}) collective-permute-start(f32[256,4096]{1,0:T(8,128)} %shard_map.75), channel_id=1, source_target_pairs={{0,8},{8,0},{16,24},{24,16},{32,40},{40,32},{48,56},{56,48},{64,72... | collective-permute-start | bytes 12582920 | tf_op jit(solution)/shard_map/ppermute | solution.py:321
  19.9 19.0 %all-to-all-start = ((f32[8,32,512]{2,1,0:T(8,128)}), f32[8,32,512]{2,1,0:T(8,128)S(1)}, u32[]{:S(2)}, u32[]{:S(2)}) async-start(f32[8,32,512]{2,1,0:T(8,128)} %broadcast_in_dim.21), calls=%async_computation | async-start | bytes 1048576 | tf_op jit(solution)/shard_map/all_to_all | solution.py:298
  38.8 2.2 copy-start.3
  43.9 16.1 %all-to-all-start.1 = ((f32[8,32,512]{2,1,0:T(8,128)}), f32[8,32,512]{2,1,0:T(8,128)S(1)}, u32[]{:S(2)}, u32[]{:S(2)}) async-start(f32[8,32,512]{2,1,0:T(8,128)} %get-tuple-element.93.refs_0_.refs_2_), calls=%async_computation.1 | async-start | bytes 1048576 | tf_op jit(solution)/shard_map/all_to_all | solution.py:298
  60.0 21.5 %copy-start.6 = (bf16[512,4096]{1,0:T(8,128)(2,1)S(1)}, bf16[512,4096]{1,0:T(8,128)(2,1)}, u32[]{:S(2)}) copy-start(bf16[512,4096]{1,0:T(8,128)(2,1)} %get-tuple-element.99.mat_ref) | copy-start | bytes 12582916
  60.0 2.3 copy-start.8
  62.4 34.0 %copy-start = (bf16[512,4096]{1,0:T(8,128)(2,1)S(1)}, bf16[512,4096]{1,0:T(8,128)(2,1)}, u32[]{:S(2)}) copy-start(bf16[512,4096]{1,0:T(8,128)(2,1)} %get-tuple-element.102.mat_ref) | copy-start | bytes 12582916
  98.6 6.7 %collective-permute-start.5 = (f32[32,512]{1,0:T(8,128)S(1)}, f32[32,512]{1,0:T(8,128)S(1)}, u32[]{:S(2)}, u32[]{:S(2)}) collective-permute-start(f32[32,512]{1,0:T(8,128)S(1)} %slice_bitcast_fusion.11), channel_id=1, source_target_pairs={{0,16},{8,24},{16,32},{24,40},{32,48},{40,56},{48,64},{56,72},{64,... | collective-permute-start | bytes 196616 | tf_op jit(solution)/shard_map/ppermute | solution.py:379
  118.3 2.2 copy-start.4
  120.5 15.5 %copy-start.9 = (bf16[512,4096]{1,0:T(8,128)(2,1)S(1)}, bf16[512,4096]{1,0:T(8,128)(2,1)}, u32[]{:S(2)}) copy-start(bf16[512,4096]{1,0:T(8,128)(2,1)} %get-tuple-element.96.mat_ref) | copy-start | bytes 12582916
  120.5 30.4 %copy-start.7 = (bf16[512,4096]{1,0:T(8,128)(2,1)S(1)}, bf16[512,4096]{1,0:T(8,128)(2,1)}, u32[]{:S(2)}) copy-start(bf16[512,4096]{1,0:T(8,128)(2,1)} %get-tuple-element.99.mat_ref) | copy-start | bytes 12582916
  136.0 29.7 %copy-start.1 = (bf16[512,4096]{1,0:T(8,128)(2,1)S(1)}, bf16[512,4096]{1,0:T(8,128)(2,1)}, u32[]{:S(2)}) copy-start(bf16[512,4096]{1,0:T(8,128)(2,1)} %get-tuple-element.102.mat_ref) | copy-start | bytes 12582916
  150.9 38.4 %copy-start.5 = (bf16[512,4096]{1,0:T(8,128)(2,1)S(1)}, bf16[512,4096]{1,0:T(8,128)(2,1)}, u32[]{:S(2)}) copy-start(bf16[512,4096]{1,0:T(8,128)(2,1)} %get-tuple-element.92.mat_ref) | copy-start | bytes 12582916
  167.9 6.4 collective-permute-start.6
  236.6 6.5 %collective-permute-start.7 = (f32[32,512]{1,0:T(8,128)S(1)}, f32[32,512]{1,0:T(8,128)S(1)}, u32[]{:S(2)}, u32[]{:S(2)}) collective-permute-start(f32[32,512]{1,0:T(8,128)S(1)} %slice_bitcast_fusion.9), channel_id=1, source_target_pairs={{0,16},{8,24},{16,32},{24,40},{32,48},{40,56},{48,64},{56,72},{64,... | collective-permute-start | bytes 196616 | tf_op jit(solution)/shard_map/ppermute | solution.py:379
  300.5 6.4 collective-permute-start.8
  369.5 6.4 collective-permute-start.9
  433.0 6.5 %collective-permute-start.10 = (f32[32,512]{1,0:T(8,128)S(1)}, f32[32,512]{1,0:T(8,128)S(1)}, u32[]{:S(2)}, u32[]{:S(2)}) collective-permute-start(f32[32,512]{1,0:T(8,128)S(1)} %slice_bitcast_fusion.6), channel_id=1, source_target_pairs={{0,16},{8,24},{16,32},{24,40},{32,48},{40,56},{48,64},{56,72},{64,... | collective-permute-start | bytes 196616 | tf_op jit(solution)/shard_map/ppermute | solution.py:379
  500.4 6.4 collective-permute-start.11
  565.1 6.4 collective-permute-start.12
  598.5 21.8 %copy-start.11 = (f32[2,8,4,512]{3,2,1,0:T(4,128)S(1)}, f32[2,8,4,512]{3,2,1,0:T(4,128)}, u32[]{:S(2)}) copy-start(f32[2,8,4,512]{3,2,1,0:T(4,128)} %get-tuple-element.168) | copy-start | bytes 393220
  598.5 21.8 %copy-start.10 = (f32[2,8,4,512]{3,2,1,0:T(4,128)S(1)}, f32[2,8,4,512]{3,2,1,0:T(4,128)}, u32[]{:S(2)}) copy-start(f32[2,8,4,512]{3,2,1,0:T(4,128)} %get-tuple-element.169) | copy-start | bytes 393220
  616.5 3.9 collective-permute-start.13
  616.5 15.2 %all-to-all-start.35 = ((f32[8,32,512]{2,1,0:T(8,128)}), f32[8,32,512]{2,1,0:T(8,128)S(1)}, u32[]{:S(2)}, u32[]{:S(2)}) async-start(f32[8,32,512]{2,1,0:T(8,128)} %get-tuple-element.166.refs_0_), calls=%async_computation.35 | async-start | bytes 1048576 | tf_op jit(solution)/shard_map/all_to_all | solution.py:298
  631.7 2.2 copy-start.2
  637.6 2.9 collective-permute-start.14

commit v5 on v4

--- a/solution.py
+++ b/solution.py
@@ -13,7 +13,6 @@
 PARTS = 2
 PIECES = 2
 GATHERED = 4
-SLOTS = 48
 NT = (((1,), (1,)), ((), ()))
 VMEM = pl.BlockSpec(memory_space=pltpu.VMEM)
 SMEM = pl.BlockSpec(memory_space=pltpu.SMEM)
@@ -81,49 +80,12 @@
     )(mats, other, *before)
 
 
-def step_kernel(
-    full_ref, phase_ref, mat_ref, saved_in, *refs, tick, number, layers, ticks
-):
-    out_ref, saved_ref, sum_buf, save_sems = refs[-4:]
+def step_kernel(full_ref, phase_ref, mat_ref, saved_in, out_ref, saved_ref, *, tick, number, layers):
     blocks, wide, rows = full_ref.shape
     split = wide // 2
     member = lax.axis_index("layer")
     core = lax.rem(member, CORES)
-    stage = lax.div(member, CORES)
-    left = CORES * layers - 1 - number
-    late = tick == ticks - 1 and left < 2
-    behind = (tick or number) and not (late and left == 0)
-    def chunk_of(tick):
-        return (tick >= stage) & (tick - stage < CHUNKS), jnp.clip(tick - stage, 0, CHUNKS - 1)
-
-    def entry(number, chunk):
-        kind = jnp.where(core == number // layers, 0, 1)
-        return (number % layers * CORES + kind) * CHUNKS + chunk
-
-    valid, chunk = chunk_of(tick)
-    place = entry(number, chunk)
-    block_saves = [
-        pltpu.make_async_copy(full_ref.at[b], saved_ref.at[place, b], save_sems.at[b])
-        for b in range(blocks)
-    ]
-    if behind:
-        before = (number - 1) % (CORES * layers)
-        before_valid, before_chunk = chunk_of(tick - (number == 0))
-        before_save = pltpu.make_async_copy(
-            refs[0].at[0], saved_ref.at[entry(before, before_chunk), blocks], save_sems.at[blocks]
-        )
-
-    @pl.when(valid)
-    def _():
-        for copy in block_saves:
-            copy.start()
-
-    if behind:
-
-        @pl.when(before_valid)
-        def _():
-            before_save.start()
-
+    chunk = tick - lax.div(member, CORES)
     total = jnp.zeros((wide, rows), jnp.float32)
     for b in range(blocks):
         cosine = phase_ref[number, 0, b : b + 1, :]
@@ -139,27 +101,15 @@
     for b in range(blocks):
         out_ref[b] = total
 
-    if late:
-        sum_buf[...] = total
-        sum_save = pltpu.make_async_copy(
-            sum_buf, saved_ref.at[place, blocks], save_sems.at[blocks + 1]
-        )
-
-        @pl.when(valid)
-        def _():
-            sum_save.start()
-            sum_save.wait()
-
-    @pl.when(valid)
-    def _():
-        for copy in block_saves:
-            copy.wait()
-
-    if behind:
-
-        @pl.when(before_valid)
-        def _():
-            before_save.wait()
+    for kind in range(CORES):
+        for number_chunk in range(CHUNKS):
+
+            @pl.when((chunk == number_chunk) & ((core != number // layers) == bool(kind)))
+            def _():
+                place = kind * CHUNKS + number_chunk
+                for b in range(blocks):
+                    saved_ref[place, b] = full_ref[b]
+                saved_ref[place, blocks] = total
 
 
 def allocate_kernel(out_ref):
@@ -171,12 +121,12 @@
         allocate_kernel,
         out_shape=jax.ShapeDtypeStruct(shape, jnp.float32),
         in_specs=[],
-        out_specs=ANYWHERE,
-        compiler_params=PARAMS,
+        out_specs=VMEM,
+        compiler_params=STEP_PARAMS,
     )()
 
 
-def layer_step(full, phases, mat, saved, extra, **position):
+def layer_step(full, phases, mat, saved, **position):
     blocks, wide, rows = full.shape
     return pl.pallas_call(
         functools.partial(step_kernel, **position),
@@ -184,26 +134,22 @@
             jax.ShapeDtypeStruct(full.shape, jnp.float32),
             jax.ShapeDtypeStruct(saved.shape, jnp.float32),
         ),
-        in_specs=[VMEM] * 3 + [ANYWHERE] * (1 + len(extra)),
-        out_specs=(VMEM, ANYWHERE),
+        in_specs=[VMEM] * 4,
+        out_specs=(VMEM, VMEM),
         input_output_aliases={3: 1},
-        scratch_shapes=[
-            pltpu.VMEM((wide, rows), jnp.float32),
-            pltpu.SemaphoreType.DMA((blocks + 2,)),
-        ],
         compiler_params=STEP_PARAMS,
         cost_estimate=pl.CostEstimate(
             flops=2 * wide * rows * rows * blocks,
             bytes_accessed=2 * blocks * rows * rows,
             transcendentals=0,
         ),
-    )(full, phases, mat, saved, *extra)
+    )(full, phases, mat, saved)
 
 
 def fields_kernel(
     core_ref, own_ref, other_ref, own_leave_ref, other_leave_ref, cos_ref, sin_ref, mat_ref, *refs
 ):
-    out_ref, leave_ref, token_ref, total = refs[-4:]
+    out_ref, leave_ref, total = refs[-3:]
     step = pl.program_id(0)
     chunks, gathered, wide, rows = other_ref.shape
     half = wide // 2
@@ -233,7 +179,6 @@
     @pl.when(step == 0)
     def _():
         total[...] = partial
-        token_ref[...] = jnp.zeros_like(token_ref)
         leave = [
             columns(own_leave_ref, other_leave_ref, 0, part)
             for part in (slice(0, half), slice(half, wide))
@@ -258,16 +203,15 @@
     entering = pl.BlockSpec((chunks, GATHERED, wide, rows), lambda b, c: (0, b, 0, 0))
     leave = pl.BlockSpec((chunks, 1, wide, rows), lambda b, c: (0, blocks, 0, 0))
     own_entering = pl.BlockSpec(
-        (chunks, GATHERED, wide, rows), lambda b, c: (layer * CORES, b, 0, 0)
+        (chunks, GATHERED, wide, rows), lambda b, c: (0, b, 0, 0)
     )
-    own_leave = pl.BlockSpec((chunks, 1, wide, rows), lambda b, c: (layer * CORES, blocks, 0, 0))
+    own_leave = pl.BlockSpec((chunks, 1, wide, rows), lambda b, c: (0, blocks, 0, 0))
     coef = pl.BlockSpec((GATHERED, DEPTHS, rows), lambda b, c: (b, 0, 0))
     return pl.pallas_call(
         fields_kernel,
         out_shape=(
             jax.ShapeDtypeStruct((layers, rows, cols), jnp.bfloat16),
             jax.ShapeDtypeStruct((layers, rows, width), jnp.float32),
-            jax.ShapeDtypeStruct((8, 128), jnp.float32),
         ),
         grid_spec=pltpu.PrefetchScalarGridSpec(
             num_scalar_prefetch=1,
@@ -285,7 +229,6 @@
             out_specs=(
                 pl.BlockSpec((1, rows, cols), lambda b, c: (layer, 0, 0)),
                 pl.BlockSpec((1, rows, width), lambda b, c: (layer, 0, 0)),
-                pl.BlockSpec((8, 128), lambda b, c: (0, 0)),
             ),
             scratch_shapes=[pltpu.VMEM((rows, cols), jnp.float32)],
         ),
@@ -340,18 +283,16 @@
     start = start.transpose(1, 0, 2, 3).reshape(CHUNKS, wide, rows)
 
     ticks = stages + CHUNKS - 1
-    saved = allocate((SLOTS, tiles + 1, wide, rows))
+    saved = [allocate((CORES * CHUNKS, tiles + 1, wide, rows)) for _ in range(layers)]
     results = ()
 
     def finish(layer):
-        first = (layer * CORES + 1) * CHUNKS
-        other = lax.ppermute(saved[first : first + CHUNKS], "layer", partner)
+        other = lax.ppermute(saved[layer][CHUNKS:], "layer", partner)
         return layer_fields(
-            core.reshape(1), saved, other, cosines[layer], sines[layer], eigvec, layer, results[:2]
+            core.reshape(1), saved[layer], other, cosines[layer], sines[layer], eigvec, layer, results
         )
 
     received = None
-    computed = ()
     for tick in range(ticks):
         inbox = start[min(tick, CHUNKS - 1)]
         if tick > 0:
@@ -368,19 +309,15 @@
                     pair = tuple(place(interface, arrived[number][piece], number, piece, tied))
                 for half in range(CORES):
                     mats[half * layers + number] = pair[half]
-            if tick == ticks - 1 and number == CORES * layers - 1:
-                results = finish(0)
-                computed += tuple(results[2:])
-            spread, saved = layer_step(
-                full, whole, mats[number], saved, computed,
-                tick=tick, number=number, layers=layers, ticks=ticks,
+            own = number % layers
+            spread, saved[own] = layer_step(
+                full, whole, mats[number], saved[own], tick=tick, number=number, layers=layers
             )
-            computed = (spread,)
         received = lax.ppermute(spread[0], "layer", ring)
 
-    for layer in range(1, layers):
+    for layer in range(layers):
         results = finish(layer)
-    return results[:2]
+    return results
 
 
 def solution(mesh):

time: 658 us -> 656 us (level)
  Pallas kernels: 105 us -> 95.4 us
  local copies, waits for them, and re-layouts: 14.7 us -> 21.9 us
    pallas_call x36, Pallas kernels: 62 us -> 52.3 us  [layer_step(): pl.pallas_call(functools.partial(step_kernel, **position), out_shape=(jax...]
    unnamed x27 -> x43, local copies, waits for them, and re-layouts: 9.05 us -> 17.8 us
  transfers between devices with their start and end apart: 18 -> 18, of which waited for: 12 -> 11; matrix products, arithmetic and copies ran while one was open for 0% -> 1% of each run, Pallas kernels for 6% -> 7%
where the time goes in v5:
time: 656 us; the launch traced here: 645 us
  blocking collectives  443 us (68%)
  Pallas kernels  95.4 us (15%)
  waiting for transfers between devices  52.4 us (8%)
  starting transfers between devices  28.7 us (4%)
  local copies, waits for them, and re-layouts  21.9 us (3%)
    all_to_all x33, blocking collectives, to_all(): lax.all_to_all(block, 'tile', split_axis=0, concat_axis=0, tiled=False)  443 us
    pallas_call x36, Pallas kernels, layer_step(): pl.pallas_call(functools.partial(step_kernel, **position), out_shape=(jax...  52.3 us
    ppermute x8, waiting for transfers between devices, on_device(): received = lax.ppermute(spread[0], 'layer', ring)  41.5 us
    pallas_call x4, Pallas kernels, place(): pl.pallas_call(place_kernel, out_shape=(out, out), grid=(PIECES,), in_spe...  18.4 us
    unnamed x43, local copies, waits for them, and re-layouts  17.8 us
    all_to_all x3, starting transfers between devices, to_all(): lax.all_to_all(block, 'tile', split_axis=0, concat_axis=0, tiled=False)  16.3 us
    pallas_call x4, Pallas kernels, widen(): pl.pallas_call(widen_kernel, out_shape=jax.ShapeDtypeStruct((height, orde...  13.4 us
  transfers between devices with their start and end apart: 18, of which 11 were waited for; matrix products, arithmetic and copies ran while one was open for 1% of the time, Pallas kernels for 7%

profile of v5, /device:TPU:0, one launch (start us, length us, event | category | flops | bytes accessed | tf_op | source)
XLA Modules:
  0.0 645.0 jit_solution(8211219275419854246)
XLA Ops:
  19.2 7.7 %all-to-all-start = ((f32[8,32,512]{2,1,0:T(8,128)}), f32[8,32,512]{2,1,0:T(8,128)S(1)}, u32[]{:S(2)}, u32[]{:S(2)}) async-start(f32[8,32,512]{2,1,0:T(8,128)} %broadcast_in_dim.21), calls=%async_computation | async-start | bytes 1048576 | tf_op jit(solution)/shard_map/all_to_all | solution.py:241
  26.9 4.6 shard_map.70
  31.5 4.6 shard_map.71
  42.5 5.1 all-to-all-start.1
  49.1 4.6 shard_map.76
  65.3 17.4 %all_to_all.180.full_ref = f32[8,32,512]{2,1,0:T(8,128)S(1)} all-to-all(f32[8,32,512]{2,1,0:T(8,128)S(1)} %get-tuple-element.94), channel_id=1, replica_groups=mesh['layer'=16,'tile'=8] {'tile'}, dimensions={0} | all-to-all | bytes 1048576 | tf_op jit(solution)/shard_map/all_to_all | solution.py:241
  84.2 12.9 %all_to_all.181.full_ref = f32[8,32,512]{2,1,0:T(8,128)S(1)} all-to-all(f32[8,32,512]{2,1,0:T(8,128)S(1)} %get-tuple-element.97), channel_id=1, replica_groups=mesh['layer'=16,'tile'=8] {'tile'}, dimensions={0} | all-to-all | bytes 1048576 | tf_op jit(solution)/shard_map/all_to_all | solution.py:241
  100.7 5.6 collective-permute-done.5
  106.4 13.1 %all_to_all.182.full_ref = f32[8,32,512]{2,1,0:T(8,128)S(1)} all-to-all(f32[8,32,512]{2,1,0:T(8,128)S(1)} %broadcast_in_dim.22), channel_id=1, replica_groups=mesh['layer'=16,'tile'=8] {'tile'}, dimensions={0} | all-to-all | bytes 1048576 | tf_op jit(solution)/shard_map/all_to_all | solution.py:241
  123.1 12.8 %all_to_all.183.full_ref = f32[8,32,512]{2,1,0:T(8,128)S(1)} all-to-all(f32[8,32,512]{2,1,0:T(8,128)S(1)} %get-tuple-element.102), channel_id=1, replica_groups=mesh['layer'=16,'tile'=8] {'tile'}, dimensions={0} | all-to-all | bytes 1048576 | tf_op jit(solution)/shard_map/all_to_all | solution.py:241
  137.4 12.7 %all_to_all.184.full_ref = f32[8,32,512]{2,1,0:T(8,128)S(1)} all-to-all(f32[8,32,512]{2,1,0:T(8,128)S(1)} %get-tuple-element.104), channel_id=1, replica_groups=mesh['layer'=16,'tile'=8] {'tile'}, dimensions={0} | all-to-all | bytes 1048576 | tf_op jit(solution)/shard_map/all_to_all | solution.py:241
  151.5 12.7 %all_to_all.185.full_ref = f32[8,32,512]{2,1,0:T(8,128)S(1)} all-to-all(f32[8,32,512]{2,1,0:T(8,128)S(1)} %get-tuple-element.106), channel_id=1, replica_groups=mesh['layer'=16,'tile'=8] {'tile'}, dimensions={0} | all-to-all | bytes 1048576 | tf_op jit(solution)/shard_map/all_to_all | solution.py:241
  165.8 6.4 collective-permute-done.6
  172.2 13.7 %all_to_all.186.full_ref = f32[8,32,512]{2,1,0:T(8,128)S(1)} all-to-all(f32[8,32,512]{2,1,0:T(8,128)S(1)} %broadcast_in_dim.23), channel_id=1, replica_groups=mesh['layer'=16,'tile'=8] {'tile'}, dimensions={0} | all-to-all | bytes 1048576 | tf_op jit(solution)/shard_map/all_to_all | solution.py:241
  187.3 15.9 %all_to_all.187.full_ref = f32[8,32,512]{2,1,0:T(8,128)S(1)} all-to-all(f32[8,32,512]{2,1,0:T(8,128)S(1)} %get-tuple-element.110), channel_id=1, replica_groups=mesh['layer'=16,'tile'=8] {'tile'}, dimensions={0} | all-to-all | bytes 1048576 | tf_op jit(solution)/shard_map/all_to_all | solution.py:241
  204.6 13.8 %all_to_all.188.full_ref = f32[8,32,512]{2,1,0:T(8,128)S(1)} all-to-all(f32[8,32,512]{2,1,0:T(8,128)S(1)} %get-tuple-element.112), channel_id=1, replica_groups=mesh['layer'=16,'tile'=8] {'tile'}, dimensions={0} | all-to-all | bytes 1048576 | tf_op jit(solution)/shard_map/all_to_all | solution.py:241
  219.8 12.9 %all_to_all.189.full_ref = f32[8,32,512]{2,1,0:T(8,128)S(1)} all-to-all(f32[8,32,512]{2,1,0:T(8,128)S(1)} %get-tuple-element.114), channel_id=1, replica_groups=mesh['layer'=16,'tile'=8] {'tile'}, dimensions={0} | all-to-all | bytes 1048576 | tf_op jit(solution)/shard_map/all_to_all | solution.py:241
  234.2 7.1 %collective-permute-done.7 = f32[32,512]{1,0:T(8,128)S(1)} collective-permute-done((f32[32,512]{1,0:T(8,128)S(1)}, f32[32,512]{1,0:T(8,128)S(1)}, u32[]{:S(2)}, u32[]{:S(2)}) %collective-permute-start.7) | collective-permute-done | bytes 65568 | tf_op jit(solution)/shard_map/ppermute | solution.py:316
  241.3 12.6 %all_to_all.190.full_ref = f32[8,32,512]{2,1,0:T(8,128)S(1)} all-to-all(f32[8,32,512]{2,1,0:T(8,128)S(1)} %broadcast_in_dim.24), channel_id=1, replica_groups=mesh['layer'=16,'tile'=8] {'tile'}, dimensions={0} | all-to-all | bytes 1048576 | tf_op jit(solution)/shard_map/all_to_all | solution.py:241
  255.3 12.9 %all_to_all.191.full_ref = f32[8,32,512]{2,1,0:T(8,128)S(1)} all-to-all(f32[8,32,512]{2,1,0:T(8,128)S(1)} %get-tuple-element.118), channel_id=1, replica_groups=mesh['layer'=16,'tile'=8] {'tile'}, dimensions={0} | all-to-all | bytes 1048576 | tf_op jit(solution)/shard_map/all_to_all | solution.py:241
  269.6 12.7 %all_to_all.192.full_ref = f32[8,32,512]{2,1,0:T(8,128)S(1)} all-to-all(f32[8,32,512]{2,1,0:T(8,128)S(1)} %get-tuple-element.120), channel_id=1, replica_groups=mesh['layer'=16,'tile'=8] {'tile'}, dimensions={0} | all-to-all | bytes 1048576 | tf_op jit(solution)/shard_map/all_to_all | solution.py:241
  283.7 12.7 %all_to_all.193.full_ref = f32[8,32,512]{2,1,0:T(8,128)S(1)} all-to-all(f32[8,32,512]{2,1,0:T(8,128)S(1)} %get-tuple-element.122), channel_id=1, replica_groups=mesh['layer'=16,'tile'=8] {'tile'}, dimensions={0} | all-to-all | bytes 1048576 | tf_op jit(solution)/shard_map/all_to_all | solution.py:241
  297.9 6.4 collective-permute-done.8
  304.3 15.0 %all_to_all.194.full_ref = f32[8,32,512]{2,1,0:T(8,128)S(1)} all-to-all(f32[8,32,512]{2,1,0:T(8,128)S(1)} %broadcast_in_dim.25), channel_id=1, replica_groups=mesh['layer'=16,'tile'=8] {'tile'}, dimensions={0} | all-to-all | bytes 1048576 | tf_op jit(solution)/shard_map/all_to_all | solution.py:241
  320.7 14.7 %all_to_all.195.full_ref = f32[8,32,512]{2,1,0:T(8,128)S(1)} all-to-all(f32[8,32,512]{2,1,0:T(8,128)S(1)} %get-tuple-element.126), channel_id=1, replica_groups=mesh['layer'=16,'tile'=8] {'tile'}, dimensions={0} | all-to-all | bytes 1048576 | tf_op jit(solution)/shard_map/all_to_all | solution.py:241
  336.8 12.7 %all_to_all.196.full_ref = f32[8,32,512]{2,1,0:T(8,128)S(1)} all-to-all(f32[8,32,512]{2,1,0:T(8,128)S(1)} %get-tuple-element.128), channel_id=1, replica_groups=mesh['layer'=16,'tile'=8] {'tile'}, dimensions={0} | all-to-all | bytes 1048576 | tf_op jit(solution)/shard_map/all_to_all | solution.py:241
  350.9 13.5 %all_to_all.197.full_ref = f32[8,32,512]{2,1,0:T(8,128)S(1)} all-to-all(f32[8,32,512]{2,1,0:T(8,128)S(1)} %get-tuple-element.130), channel_id=1, replica_groups=mesh['layer'=16,'tile'=8] {'tile'}, dimensions={0} | all-to-all | bytes 1048576 | tf_op jit(solution)/shard_map/all_to_all | solution.py:241
  372.3 12.7 %all_to_all.198.full_ref = f32[8,32,512]{2,1,0:T(8,128)S(1)} all-to-all(f32[8,32,512]{2,1,0:T(8,128)S(1)} %broadcast_in_dim.26), channel_id=1, replica_groups=mesh['layer'=16,'tile'=8] {'tile'}, dimensions={0} | all-to-all | bytes 1048576 | tf_op jit(solution)/shard_map/all_to_all | solution.py:241
  386.4 12.8 %all_to_all.199.full_ref = f32[8,32,512]{2,1,0:T(8,128)S(1)} all-to-all(f32[8,32,512]{2,1,0:T(8,128)S(1)} %get-tuple-element.134), channel_id=1, replica_groups=mesh['layer'=16,'tile'=8] {'tile'}, dimensions={0} | all-to-all | bytes 1048576 | tf_op jit(solution)/shard_map/all_to_all | solution.py:241
  400.6 13.2 %all_to_all.200.full_ref = f32[8,32,512]{2,1,0:T(8,128)S(1)} all-to-all(f32[8,32,512]{2,1,0:T(8,128)S(1)} %get-tuple-element.136), channel_id=1, replica_groups=mesh['layer'=16,'tile'=8] {'tile'}, dimensions={0} | all-to-all | bytes 1048576 | tf_op jit(solution)/shard_map/all_to_all | solution.py:241
  415.2 12.5 %all_to_all.201.full_ref = f32[8,32,512]{2,1,0:T(8,128)S(1)} all-to-all(f32[8,32,512]{2,1,0:T(8,128)S(1)} %get-tuple-element.138), channel_id=1, replica_groups=mesh['layer'=16,'tile'=8] {'tile'}, dimensions={0} | all-to-all | bytes 1048576 | tf_op jit(solution)/shard_map/all_to_all | solution.py:241
  430.3 5.2 collective-permute-done.10
  435.6 16.3 %all_to_all.202.full_ref = f32[8,32,512]{2,1,0:T(8,128)S(1)} all-to-all(f32[8,32,512]{2,1,0:T(8,128)S(1)} %broadcast_in_dim.27), channel_id=1, replica_groups=mesh['layer'=16,'tile'=8] {'tile'}, dimensions={0} | all-to-all | bytes 1048576 | tf_op jit(solution)/shard_map/all_to_all | solution.py:241
  453.3 12.9 %all_to_all.203.full_ref = f32[8,32,512]{2,1,0:T(8,128)S(1)} all-to-all(f32[8,32,512]{2,1,0:T(8,128)S(1)} %get-tuple-element.142), channel_id=1, replica_groups=mesh['layer'=16,'tile'=8] {'tile'}, dimensions={0} | all-to-all | bytes 1048576 | tf_op jit(solution)/shard_map/all_to_all | solution.py:241
  467.6 12.8 %all_to_all.204.full_ref = f32[8,32,512]{2,1,0:T(8,128)S(1)} all-to-all(f32[8,32,512]{2,1,0:T(8,128)S(1)} %get-tuple-element.144), channel_id=1, replica_groups=mesh['layer'=16,'tile'=8] {'tile'}, dimensions={0} | all-to-all | bytes 1048576 | tf_op jit(solution)/shard_map/all_to_all | solution.py:241
  481.8 13.5 %all_to_all.205.full_ref = f32[8,32,512]{2,1,0:T(8,128)S(1)} all-to-all(f32[8,32,512]{2,1,0:T(8,128)S(1)} %get-tuple-element.146), channel_id=1, replica_groups=mesh['layer'=16,'tile'=8] {'tile'}, dimensions={0} | all-to-all | bytes 1048576 | tf_op jit(solution)/shard_map/all_to_all | solution.py:241
  496.7 4.9 collective-permute-start.11
  503.8 13.1 %all_to_all.206.full_ref = f32[8,32,512]{2,1,0:T(8,128)S(1)} all-to-all(f32[8,32,512]{2,1,0:T(8,128)S(1)} %broadcast_in_dim.28), channel_id=1, replica_groups=mesh['layer'=16,'tile'=8] {'tile'}, dimensions={0} | all-to-all | bytes 1048576 | tf_op jit(solution)/shard_map/all_to_all | solution.py:241
  518.4 13.6 %all_to_all.207.full_ref = f32[8,32,512]{2,1,0:T(8,128)S(1)} all-to-all(f32[8,32,512]{2,1,0:T(8,128)S(1)} %get-tuple-element.150), channel_id=1, replica_groups=mesh['layer'=16,'tile'=8] {'tile'}, dimensions={0} | all-to-all | bytes 1048576 | tf_op jit(solution)/shard_map/all_to_all | solution.py:241
  533.3 12.7 %all_to_all.208.full_ref = f32[8,32,512]{2,1,0:T(8,128)S(1)} all-to-all(f32[8,32,512]{2,1,0:T(8,128)S(1)} %get-tuple-element.152), channel_id=1, replica_groups=mesh['layer'=16,'tile'=8] {'tile'}, dimensions={0} | all-to-all | bytes 1048576 | tf_op jit(solution)/shard_map/all_to_all | solution.py:241
  547.4 13.0 %all_to_all.209.full_ref = f32[8,32,512]{2,1,0:T(8,128)S(1)} all-to-all(f32[8,32,512]{2,1,0:T(8,128)S(1)} %get-tuple-element.154), channel_id=1, replica_groups=mesh['layer'=16,'tile'=8] {'tile'}, dimensions={0} | all-to-all | bytes 1048576 | tf_op jit(solution)/shard_map/all_to_all | solution.py:241
  562.8 5.4 collective-permute-done.12
  568.3 13.8 %all_to_all.210.full_ref = f32[8,32,512]{2,1,0:T(8,128)S(1)} all-to-all(f32[8,32,512]{2,1,0:T(8,128)S(1)} %broadcast_in_dim.29), channel_id=1, replica_groups=mesh['layer'=16,'tile'=8] {'tile'}, dimensions={0} | all-to-all | bytes 1048576 | tf_op jit(solution)/shard_map/all_to_all | solution.py:241
  583.6 12.7 %all_to_all.211.full_ref = f32[8,32,512]{2,1,0:T(8,128)S(1)} all-to-all(f32[8,32,512]{2,1,0:T(8,128)S(1)} %get-tuple-element.158), channel_id=1, replica_groups=mesh['layer'=16,'tile'=8] {'tile'}, dimensions={0} | all-to-all | bytes 1048576 | tf_op jit(solution)/shard_map/all_to_all | solution.py:241
  597.7 12.7 %all_to_all.212.full_ref = f32[8,32,512]{2,1,0:T(8,128)S(1)} all-to-all(f32[8,32,512]{2,1,0:T(8,128)S(1)} %get-tuple-element.160), channel_id=1, replica_groups=mesh['layer'=16,'tile'=8] {'tile'}, dimensions={0} | all-to-all | bytes 1048576 | tf_op jit(solution)/shard_map/all_to_all | solution.py:241
  617.2 8.4 %all-to-all-done.35.full_ref = f32[8,32,512]{2,1,0:T(8,128)S(1)} async-done(((f32[8,32,512]{2,1,0:T(8,128)}), f32[8,32,512]{2,1,0:T(8,128)S(1)}, u32[]{:S(2)}, u32[]{:S(2)}) %all-to-all-start.35) | async-done | bytes 524320 | tf_op jit(solution)/shard_map/all_to_all | solution.py:241
  633.3 5.8 shard_map.114
  639.1 5.5 shard_map.115
  (151 shorter events, 112.7 us)
Async XLA Ops:
  2.2 8.4 %collective-permute-start = (f32[2,2,8,512]{3,2,1,0:T(8,128)S(1)}, f32[2,2,8,512]{3,2,1,0:T(8,128)S(1)}, u32[]{:S(2)}, u32[]{:S(2)}) collective-permute-start(f32[2,2,8,512]{3,2,1,0:T(8,128)S(1)} %get-tuple-element.183), channel_id=1, source_target_pairs={{0,8},{8,0},{16,24},{24,16},{32,40},{40,32},{48,56},{56,48},{64,72... | collective-permute-start | bytes 196616 | tf_op jit(solution)/shard_map/ppermute | solution.py:259
  5.5 21.4 %collective-permute-start.2 = (f32[256,4096]{1,0:T(8,128)}, f32[256,4096]{1,0:T(8,128)}, u32[]{:S(2)}, u32[]{:S(2)}) collective-permute-start(f32[256,4096]{1,0:T(8,128)} %shard_map.68.refs_0_), channel_id=1, source_target_pairs={{0,8},{8,0},{16,24},{24,16},{32,40},{40,32},{48,56},{56,48},{64,72... | collective-permute-start | bytes 12582920 | tf_op jit(solution)/shard_map/ppermute | solution.py:264
  9.4 22.1 %collective-permute-start.1 = (f32[256,4096]{1,0:T(8,128)}, f32[256,4096]{1,0:T(8,128)}, u32[]{:S(2)}, u32[]{:S(2)}) collective-permute-start(f32[256,4096]{1,0:T(8,128)} %shard_map.69), channel_id=1, source_target_pairs={{0,8},{8,0},{16,24},{24,16},{32,40},{40,32},{48,56},{56,48},{64,72... | collective-permute-start | bytes 12582920 | tf_op jit(solution)/shard_map/ppermute | solution.py:264
  14.2 4.0 copy-start.20
  14.2 34.9 %collective-permute-start.4 = (f32[256,4096]{1,0:T(8,128)}, f32[256,4096]{1,0:T(8,128)}, u32[]{:S(2)}, u32[]{:S(2)}) collective-permute-start(f32[256,4096]{1,0:T(8,128)} %shard_map.74.refs_0_), channel_id=1, source_target_pairs={{0,8},{8,0},{16,24},{24,16},{32,40},{40,32},{48,56},{56,48},{64,72... | collective-permute-start | bytes 12582920 | tf_op jit(solution)/shard_map/ppermute | solution.py:264
  18.1 35.6 %collective-permute-start.3 = (f32[256,4096]{1,0:T(8,128)}, f32[256,4096]{1,0:T(8,128)}, u32[]{:S(2)}, u32[]{:S(2)}) collective-permute-start(f32[256,4096]{1,0:T(8,128)} %shard_map.75), channel_id=1, source_target_pairs={{0,8},{8,0},{16,24},{24,16},{32,40},{40,32},{48,56},{56,48},{64,72... | collective-permute-start | bytes 12582920 | tf_op jit(solution)/shard_map/ppermute | solution.py:264
  19.2 19.0 %all-to-all-start = ((f32[8,32,512]{2,1,0:T(8,128)}), f32[8,32,512]{2,1,0:T(8,128)S(1)}, u32[]{:S(2)}, u32[]{:S(2)}) async-start(f32[8,32,512]{2,1,0:T(8,128)} %broadcast_in_dim.21), calls=%async_computation | async-start | bytes 1048576 | tf_op jit(solution)/shard_map/all_to_all | solution.py:241
  38.2 2.2 copy-start.10
  42.5 16.1 %all-to-all-start.1 = ((f32[8,32,512]{2,1,0:T(8,128)}), f32[8,32,512]{2,1,0:T(8,128)S(1)}, u32[]{:S(2)}, u32[]{:S(2)}) async-start(f32[8,32,512]{2,1,0:T(8,128)} %get-tuple-element.90.refs_0_.refs_2_), calls=%async_computation.1 | async-start | bytes 1048576 | tf_op jit(solution)/shard_map/all_to_all | solution.py:241
  47.7 1.4 copy-start
  58.6 1.7 copy-start.1
  60.3 2.2 copy-start.15
  62.5 20.2 %copy-start.13 = (bf16[512,4096]{1,0:T(8,128)(2,1)S(1)}, bf16[512,4096]{1,0:T(8,128)(2,1)}, u32[]{:S(2)}) copy-start(bf16[512,4096]{1,0:T(8,128)(2,1)} %get-tuple-element.95.mat_ref) | copy-start | bytes 12582916
  63.9 1.4 copy-start.2
  82.7 14.3 %copy-start.3 = (f32[4,9,32,512]{3,2,1,0:T(8,128)S(1)}, f32[4,9,32,512]{3,2,1,0:T(8,128)}, u32[]{:S(2)}) copy-start(f32[4,9,32,512]{3,2,1,0:T(8,128)} %copy-done.2) | copy-start | bytes 7077892
  82.7 14.3 %copy-start.17 = (bf16[512,4096]{1,0:T(8,128)(2,1)S(1)}, bf16[512,4096]{1,0:T(8,128)(2,1)}, u32[]{:S(2)}) copy-start(bf16[512,4096]{1,0:T(8,128)(2,1)} %get-tuple-element.98.mat_ref) | copy-start | bytes 12582916
  98.4 1.4 copy-start.4
  99.8 6.5 %collective-permute-start.5 = (f32[32,512]{1,0:T(8,128)S(1)}, f32[32,512]{1,0:T(8,128)S(1)}, u32[]{:S(2)}, u32[]{:S(2)}) collective-permute-start(f32[32,512]{1,0:T(8,128)S(1)} %slice_bitcast_fusion.11), channel_id=1, source_target_pairs={{0,16},{8,24},{16,32},{24,40},{32,48},{40,56},{48,64},{56,72},{64,... | collective-permute-start | bytes 196616 | tf_op jit(solution)/shard_map/ppermute | solution.py:316
  119.5 2.2 copy-start.11
  121.7 14.3 %copy-start.5 = (f32[4,9,32,512]{3,2,1,0:T(8,128)S(1)}, f32[4,9,32,512]{3,2,1,0:T(8,128)}, u32[]{:S(2)}) copy-start(f32[4,9,32,512]{3,2,1,0:T(8,128)} %copy-done.4) | copy-start | bytes 7077892
  121.7 14.3 %copy-start.16 = (bf16[512,4096]{1,0:T(8,128)(2,1)S(1)}, bf16[512,4096]{1,0:T(8,128)(2,1)}, u32[]{:S(2)}) copy-start(bf16[512,4096]{1,0:T(8,128)(2,1)} %get-tuple-element.93.mat_ref) | copy-start | bytes 12582916
  136.0 14.2 %copy-start.14 = (bf16[512,4096]{1,0:T(8,128)(2,1)S(1)}, bf16[512,4096]{1,0:T(8,128)(2,1)}, u32[]{:S(2)}) copy-start(bf16[512,4096]{1,0:T(8,128)(2,1)} %get-tuple-element.95.mat_ref) | copy-start | bytes 12582916
  150.1 14.2 %copy-start.18 = (bf16[512,4096]{1,0:T(8,128)(2,1)S(1)}, bf16[512,4096]{1,0:T(8,128)(2,1)}, u32[]{:S(2)}) copy-start(bf16[512,4096]{1,0:T(8,128)(2,1)} %get-tuple-element.98.mat_ref) | copy-start | bytes 12582916
  164.3 21.6 %copy-start.12 = (bf16[512,4096]{1,0:T(8,128)(2,1)S(1)}, bf16[512,4096]{1,0:T(8,128)(2,1)}, u32[]{:S(2)}) copy-start(bf16[512,4096]{1,0:T(8,128)(2,1)} %get-tuple-element.89.mat_ref) | copy-start | bytes 12582916
  165.7 6.4 collective-permute-start.6
  234.1 7.1 %collective-permute-start.7 = (f32[32,512]{1,0:T(8,128)S(1)}, f32[32,512]{1,0:T(8,128)S(1)}, u32[]{:S(2)}, u32[]{:S(2)}) collective-permute-start(f32[32,512]{1,0:T(8,128)S(1)} %slice_bitcast_fusion.9), channel_id=1, source_target_pairs={{0,16},{8,24},{16,32},{24,40},{32,48},{40,56},{48,64},{56,72},{64,... | collective-permute-start | bytes 196616 | tf_op jit(solution)/shard_map/ppermute | solution.py:316
  297.8 6.4 collective-permute-start.8
  365.8 6.4 collective-permute-start.9
  429.1 6.4 collective-permute-start.10
  496.7 7.0 %collective-permute-start.11 = (f32[32,512]{1,0:T(8,128)S(1)}, f32[32,512]{1,0:T(8,128)S(1)}, u32[]{:S(2)}, u32[]{:S(2)}) collective-permute-start(f32[32,512]{1,0:T(8,128)S(1)} %slice_bitcast_fusion.5), channel_id=1, source_target_pairs={{0,16},{8,24},{16,32},{24,40},{32,48},{40,56},{48,64},{56,72},{64,... | collective-permute-start | bytes 196616 | tf_op jit(solution)/shard_map/ppermute | solution.py:316
  561.8 6.4 collective-permute-start.12
  597.7 14.9 %copy-start.6 = (f32[4,9,32,512]{3,2,1,0:T(8,128)}, f32[4,9,32,512]{3,2,1,0:T(8,128)S(1)}, u32[]{:S(2)}) copy-start(f32[4,9,32,512]{3,2,1,0:T(8,128)S(1)} %get-tuple-element.163.saved_in) | copy-start | bytes 7077892
  612.6 13.1 %all-to-all-start.35 = ((f32[8,32,512]{2,1,0:T(8,128)}), f32[8,32,512]{2,1,0:T(8,128)S(1)}, u32[]{:S(2)}, u32[]{:S(2)}) async-start(f32[8,32,512]{2,1,0:T(8,128)} %get-tuple-element.162), calls=%async_computation.35 | async-start | bytes 1048576 | tf_op jit(solution)/shard_map/all_to_all | solution.py:241
  617.2 16.1 %collective-permute-start.14 = (f32[2,9,32,512]{3,2,1,0:T(8,128)}, f32[2,9,32,512]{3,2,1,0:T(8,128)}, u32[]{:S(2)}, u32[]{:S(2)}) collective-permute-start(f32[2,9,32,512]{3,2,1,0:T(8,128)} %slice.92), channel_id=1, source_target_pairs={{0,8},{8,0},{16,24},{24,16},{32,40},{40,32},{48,56},{56,48},{64,72... | collective-permute-start | bytes 3538952 | tf_op jit(solution)/shard_map/ppermute | solution.py:290
  625.7 1.7 copy-start.7
  627.3 2.2 copy-start.19
  631.8 1.4 copy-start.8
  633.2 5.8 collective-permute-start.13
  633.3 5.8 copy-start.9

commit v6 on v5

--- a/solution.py
+++ b/solution.py
@@ -18,7 +18,7 @@
 SMEM = pl.BlockSpec(memory_space=pltpu.SMEM)
 ANYWHERE = pl.BlockSpec(memory_space=pl.ANY)
 PLACE_PARAMS = pltpu.CompilerParams(vmem_limit_bytes=58 * 1024 * 1024)
-STEP_PARAMS = pltpu.CompilerParams(vmem_limit_bytes=36 * 1024 * 1024)
+STEP_PARAMS = pltpu.CompilerParams(vmem_limit_bytes=12 * 1024 * 1024)
 PARAMS = pltpu.CompilerParams(vmem_limit_bytes=48 * 1024 * 1024)
 
 
@@ -112,18 +112,18 @@
                 saved_ref[place, blocks] = total
 
 
-def allocate_kernel(out_ref):
+def allocate_kernel(after_ref, out_ref):
     pass
 
 
-def allocate(shape):
+def allocate(shape, after):
     return pl.pallas_call(
         allocate_kernel,
         out_shape=jax.ShapeDtypeStruct(shape, jnp.float32),
-        in_specs=[],
+        in_specs=[ANYWHERE],
         out_specs=VMEM,
         compiler_params=STEP_PARAMS,
-    )()
+    )(after)
 
 
 def layer_step(full, phases, mat, saved, **position):
@@ -283,7 +283,7 @@
     start = start.transpose(1, 0, 2, 3).reshape(CHUNKS, wide, rows)
 
     ticks = stages + CHUNKS - 1
-    saved = [allocate((CORES * CHUNKS, tiles + 1, wide, rows)) for _ in range(layers)]
+    saved = []
     results = ()
 
     def finish(layer):
@@ -310,11 +310,15 @@
                 for half in range(CORES):
                     mats[half * layers + number] = pair[half]
             own = number % layers
+            if tick == 0 and number < layers:
+                after = full if number else spread
+                saved.append(allocate((CORES * CHUNKS, tiles + 1, wide, rows), after))
             spread, saved[own] = layer_step(
                 full, whole, mats[number], saved[own], tick=tick, number=number, layers=layers
             )
         received = lax.ppermute(spread[0], "layer", ring)
 
+    saved = lax.optimization_barrier(saved)
     for layer in range(layers):
         results = finish(layer)
     return results

time: 656 us -> 649 us (0.989)
  starting transfers between devices: 28.7 us -> 16.9 us
  blocking collectives: 443 us -> 454 us
  local copies, waits for them, and re-layouts: 21.9 us -> 12.8 us
    all_to_all x33 -> x34, blocking collectives: 443 us -> 454 us  [to_all(): lax.all_to_all(block, 'tile', split_axis=0, concat_axis=0, tiled=False)]
    ppermute x8, waiting for transfers between devices: 41.5 us -> 50.9 us  [on_device(): received = lax.ppermute(spread[0], 'layer', ring)]
    ppermute x8, starting transfers between devices: 11.3 us -> 2.37 us  [on_device(): received = lax.ppermute(spread[0], 'layer', ring)]
    unnamed x43 -> x33, local copies, waits for them, and re-layouts: 17.8 us -> 9.78 us
    all_to_all x3 -> x2, waiting for transfers between devices: 10.8 us -> 3.88 us  [to_all(): lax.all_to_all(block, 'tile', split_axis=0, concat_axis=0, tiled=False)]
    all_to_all x3 -> x2, starting transfers between devices: 16.3 us -> 12.8 us  [to_all(): lax.all_to_all(block, 'tile', split_axis=0, concat_axis=0, tiled=False)]
  transfers between devices with their start and end apart: 18 -> 17, of which waited for: 11 -> 11; matrix products, arithmetic and copies ran while one was open for 1% -> 0% of each run, Pallas kernels for 7% -> 6%
where the time goes in v6:
time: 649 us; the launch traced here: 638 us
  blocking collectives  454 us (70%)
  Pallas kernels  94.3 us (15%)
  waiting for transfers between devices  56.9 us (9%)
  starting transfers between devices  16.9 us (3%)
  local copies, waits for them, and re-layouts  12.8 us (2%)
    all_to_all x34, blocking collectives, to_all(): lax.all_to_all(block, 'tile', split_axis=0, concat_axis=0, tiled=False)  454 us
    pallas_call x36, Pallas kernels, layer_step(): pl.pallas_call(functools.partial(step_kernel, **position), out_shape=(jax...  51.6 us
    ppermute x8, waiting for transfers between devices, on_device(): received = lax.ppermute(spread[0], 'layer', ring)  50.9 us
    pallas_call x4, Pallas kernels, place(): pl.pallas_call(place_kernel, out_shape=(out, out), grid=(PIECES,), in_spe...  18.3 us
    pallas_call x4, Pallas kernels, widen(): pl.pallas_call(widen_kernel, out_shape=jax.ShapeDtypeStruct((height, orde...  13.4 us
  transfers between devices with their start and end apart: 17, of which 11 were waited for; matrix products, arithmetic and copies ran while one was open for 0% of the time, Pallas kernels for 6%

profile of v6, /device:TPU:0, one launch (start us, length us, event | category | flops | bytes accessed | tf_op | source)
XLA Modules:
  0.0 638.5 jit_solution(5930940108953178959)
XLA Ops:
  19.2 7.7 %all-to-all-start = ((f32[8,32,512]{2,1,0:T(8,128)}), f32[8,32,512]{2,1,0:T(8,128)S(1)}, u32[]{:S(2)}, u32[]{:S(2)}) async-start(f32[8,32,512]{2,1,0:T(8,128)} %broadcast_in_dim.21.after_ref), calls=%async_computation | async-start | bytes 1048576 | tf_op jit(solution)/shard_map/all_to_all | solution.py:241
  26.9 4.6 shard_map.70
  42.5 5.1 all-to-all-start.1
  47.6 4.6 shard_map.76
  62.2 16.1 %all_to_all.180.full_ref = f32[8,32,512]{2,1,0:T(8,128)S(1)} all-to-all(f32[8,32,512]{2,1,0:T(8,128)S(1)} %get-tuple-element.96), channel_id=1, replica_groups=mesh['layer'=16,'tile'=8] {'tile'}, dimensions={0} | all-to-all | bytes 1048576 | tf_op jit(solution)/shard_map/all_to_all | solution.py:241
  79.8 12.7 %all_to_all.181.full_ref = f32[8,32,512]{2,1,0:T(8,128)S(1)} all-to-all(f32[8,32,512]{2,1,0:T(8,128)S(1)} %get-tuple-element.99), channel_id=1, replica_groups=mesh['layer'=16,'tile'=8] {'tile'}, dimensions={0} | all-to-all | bytes 1048576 | tf_op jit(solution)/shard_map/all_to_all | solution.py:241
  94.9 5.6 collective-permute-done.5
  100.6 13.1 %all_to_all.182.full_ref = f32[8,32,512]{2,1,0:T(8,128)S(1)} all-to-all(f32[8,32,512]{2,1,0:T(8,128)S(1)} %broadcast_in_dim.22), channel_id=1, replica_groups=mesh['layer'=16,'tile'=8] {'tile'}, dimensions={0} | all-to-all | bytes 1048576 | tf_op jit(solution)/shard_map/all_to_all | solution.py:241
  120.3 12.7 %all_to_all.183.full_ref = f32[8,32,512]{2,1,0:T(8,128)S(1)} all-to-all(f32[8,32,512]{2,1,0:T(8,128)S(1)} %get-tuple-element.104), channel_id=1, replica_groups=mesh['layer'=16,'tile'=8] {'tile'}, dimensions={0} | all-to-all | bytes 1048576 | tf_op jit(solution)/shard_map/all_to_all | solution.py:241
  134.5 12.9 %all_to_all.184.full_ref = f32[8,32,512]{2,1,0:T(8,128)S(1)} all-to-all(f32[8,32,512]{2,1,0:T(8,128)S(1)} %get-tuple-element.106), channel_id=1, replica_groups=mesh['layer'=16,'tile'=8] {'tile'}, dimensions={0} | all-to-all | bytes 1048576 | tf_op jit(solution)/shard_map/all_to_all | solution.py:241
  148.8 12.7 %all_to_all.185.full_ref = f32[8,32,512]{2,1,0:T(8,128)S(1)} all-to-all(f32[8,32,512]{2,1,0:T(8,128)S(1)} %get-tuple-element.108), channel_id=1, replica_groups=mesh['layer'=16,'tile'=8] {'tile'}, dimensions={0} | all-to-all | bytes 1048576 | tf_op jit(solution)/shard_map/all_to_all | solution.py:241
  163.0 6.4 collective-permute-done.6
  169.4 13.7 %all_to_all.186.full_ref = f32[8,32,512]{2,1,0:T(8,128)S(1)} all-to-all(f32[8,32,512]{2,1,0:T(8,128)S(1)} %broadcast_in_dim.23), channel_id=1, replica_groups=mesh['layer'=16,'tile'=8] {'tile'}, dimensions={0} | all-to-all | bytes 1048576 | tf_op jit(solution)/shard_map/all_to_all | solution.py:241
  184.5 15.9 %all_to_all.187.full_ref = f32[8,32,512]{2,1,0:T(8,128)S(1)} all-to-all(f32[8,32,512]{2,1,0:T(8,128)S(1)} %get-tuple-element.112), channel_id=1, replica_groups=mesh['layer'=16,'tile'=8] {'tile'}, dimensions={0} | all-to-all | bytes 1048576 | tf_op jit(solution)/shard_map/all_to_all | solution.py:241
  201.9 13.8 %all_to_all.188.full_ref = f32[8,32,512]{2,1,0:T(8,128)S(1)} all-to-all(f32[8,32,512]{2,1,0:T(8,128)S(1)} %get-tuple-element.114), channel_id=1, replica_groups=mesh['layer'=16,'tile'=8] {'tile'}, dimensions={0} | all-to-all | bytes 1048576 | tf_op jit(solution)/shard_map/all_to_all | solution.py:241
  217.0 12.9 %all_to_all.189.full_ref = f32[8,32,512]{2,1,0:T(8,128)S(1)} all-to-all(f32[8,32,512]{2,1,0:T(8,128)S(1)} %get-tuple-element.116), channel_id=1, replica_groups=mesh['layer'=16,'tile'=8] {'tile'}, dimensions={0} | all-to-all | bytes 1048576 | tf_op jit(solution)/shard_map/all_to_all | solution.py:241
  231.4 7.1 %collective-permute-done.7 = f32[32,512]{1,0:T(8,128)S(1)} collective-permute-done((f32[32,512]{1,0:T(8,128)S(1)}, f32[32,512]{1,0:T(8,128)S(1)}, u32[]{:S(2)}, u32[]{:S(2)}) %collective-permute-start.7) | collective-permute-done | bytes 65568 | tf_op jit(solution)/shard_map/ppermute | solution.py:319
  238.5 12.6 %all_to_all.190.full_ref = f32[8,32,512]{2,1,0:T(8,128)S(1)} all-to-all(f32[8,32,512]{2,1,0:T(8,128)S(1)} %broadcast_in_dim.24), channel_id=1, replica_groups=mesh['layer'=16,'tile'=8] {'tile'}, dimensions={0} | all-to-all | bytes 1048576 | tf_op jit(solution)/shard_map/all_to_all | solution.py:241
  252.5 12.9 %all_to_all.191.full_ref = f32[8,32,512]{2,1,0:T(8,128)S(1)} all-to-all(f32[8,32,512]{2,1,0:T(8,128)S(1)} %get-tuple-element.120), channel_id=1, replica_groups=mesh['layer'=16,'tile'=8] {'tile'}, dimensions={0} | all-to-all | bytes 1048576 | tf_op jit(solution)/shard_map/all_to_all | solution.py:241
  266.8 12.7 %all_to_all.192.full_ref = f32[8,32,512]{2,1,0:T(8,128)S(1)} all-to-all(f32[8,32,512]{2,1,0:T(8,128)S(1)} %get-tuple-element.122), channel_id=1, replica_groups=mesh['layer'=16,'tile'=8] {'tile'}, dimensions={0} | all-to-all | bytes 1048576 | tf_op jit(solution)/shard_map/all_to_all | solution.py:241
  280.9 12.7 %all_to_all.193.full_ref = f32[8,32,512]{2,1,0:T(8,128)S(1)} all-to-all(f32[8,32,512]{2,1,0:T(8,128)S(1)} %get-tuple-element.124), channel_id=1, replica_groups=mesh['layer'=16,'tile'=8] {'tile'}, dimensions={0} | all-to-all | bytes 1048576 | tf_op jit(solution)/shard_map/all_to_all | solution.py:241
  295.1 6.4 collective-permute-done.8
  301.6 15.5 %all_to_all.194.full_ref = f32[8,32,512]{2,1,0:T(8,128)S(1)} all-to-all(f32[8,32,512]{2,1,0:T(8,128)S(1)} %broadcast_in_dim.25), channel_id=1, replica_groups=mesh['layer'=16,'tile'=8] {'tile'}, dimensions={0} | all-to-all | bytes 1048576 | tf_op jit(solution)/shard_map/all_to_all | solution.py:241
  318.5 14.5 %all_to_all.195.full_ref = f32[8,32,512]{2,1,0:T(8,128)S(1)} all-to-all(f32[8,32,512]{2,1,0:T(8,128)S(1)} %get-tuple-element.128), channel_id=1, replica_groups=mesh['layer'=16,'tile'=8] {'tile'}, dimensions={0} | all-to-all | bytes 1048576 | tf_op jit(solution)/shard_map/all_to_all | solution.py:241
  334.3 12.9 %all_to_all.196.full_ref = f32[8,32,512]{2,1,0:T(8,128)S(1)} all-to-all(f32[8,32,512]{2,1,0:T(8,128)S(1)} %get-tuple-element.130), channel_id=1, replica_groups=mesh['layer'=16,'tile'=8] {'tile'}, dimensions={0} | all-to-all | bytes 1048576 | tf_op jit(solution)/shard_map/all_to_all | solution.py:241
  348.6 13.5 %all_to_all.197.full_ref = f32[8,32,512]{2,1,0:T(8,128)S(1)} all-to-all(f32[8,32,512]{2,1,0:T(8,128)S(1)} %get-tuple-element.132), channel_id=1, replica_groups=mesh['layer'=16,'tile'=8] {'tile'}, dimensions={0} | all-to-all | bytes 1048576 | tf_op jit(solution)/shard_map/all_to_all | solution.py:241
  363.8 6.5 %collective-permute-done.9 = f32[32,512]{1,0:T(8,128)S(1)} collective-permute-done((f32[32,512]{1,0:T(8,128)S(1)}, f32[32,512]{1,0:T(8,128)S(1)}, u32[]{:S(2)}, u32[]{:S(2)}) %collective-permute-start.9) | collective-permute-done | bytes 65568 | tf_op jit(solution)/shard_map/ppermute | solution.py:319
  370.3 12.9 %all_to_all.198.full_ref = f32[8,32,512]{2,1,0:T(8,128)S(1)} all-to-all(f32[8,32,512]{2,1,0:T(8,128)S(1)} %broadcast_in_dim.26), channel_id=1, replica_groups=mesh['layer'=16,'tile'=8] {'tile'}, dimensions={0} | all-to-all | bytes 1048576 | tf_op jit(solution)/shard_map/all_to_all | solution.py:241
  384.6 12.7 %all_to_all.199.full_ref = f32[8,32,512]{2,1,0:T(8,128)S(1)} all-to-all(f32[8,32,512]{2,1,0:T(8,128)S(1)} %get-tuple-element.136), channel_id=1, replica_groups=mesh['layer'=16,'tile'=8] {'tile'}, dimensions={0} | all-to-all | bytes 1048576 | tf_op jit(solution)/shard_map/all_to_all | solution.py:241
  398.7 13.0 %all_to_all.200.full_ref = f32[8,32,512]{2,1,0:T(8,128)S(1)} all-to-all(f32[8,32,512]{2,1,0:T(8,128)S(1)} %get-tuple-element.138), channel_id=1, replica_groups=mesh['layer'=16,'tile'=8] {'tile'}, dimensions={0} | all-to-all | bytes 1048576 | tf_op jit(solution)/shard_map/all_to_all | solution.py:241
  413.1 12.7 %all_to_all.201.full_ref = f32[8,32,512]{2,1,0:T(8,128)S(1)} all-to-all(f32[8,32,512]{2,1,0:T(8,128)S(1)} %get-tuple-element.140), channel_id=1, replica_groups=mesh['layer'=16,'tile'=8] {'tile'}, dimensions={0} | all-to-all | bytes 1048576 | tf_op jit(solution)/shard_map/all_to_all | solution.py:241
  427.3 6.4 collective-permute-done.10
  433.7 15.4 %all_to_all.202.full_ref = f32[8,32,512]{2,1,0:T(8,128)S(1)} all-to-all(f32[8,32,512]{2,1,0:T(8,128)S(1)} %broadcast_in_dim.27), channel_id=1, replica_groups=mesh['layer'=16,'tile'=8] {'tile'}, dimensions={0} | all-to-all | bytes 1048576 | tf_op jit(solution)/shard_map/all_to_all | solution.py:241
  450.5 13.1 %all_to_all.203.full_ref = f32[8,32,512]{2,1,0:T(8,128)S(1)} all-to-all(f32[8,32,512]{2,1,0:T(8,128)S(1)} %get-tuple-element.144), channel_id=1, replica_groups=mesh['layer'=16,'tile'=8] {'tile'}, dimensions={0} | all-to-all | bytes 1048576 | tf_op jit(solution)/shard_map/all_to_all | solution.py:241
  465.0 12.8 %all_to_all.204.full_ref = f32[8,32,512]{2,1,0:T(8,128)S(1)} all-to-all(f32[8,32,512]{2,1,0:T(8,128)S(1)} %get-tuple-element.146), channel_id=1, replica_groups=mesh['layer'=16,'tile'=8] {'tile'}, dimensions={0} | all-to-all | bytes 1048576 | tf_op jit(solution)/shard_map/all_to_all | solution.py:241
  479.2 15.3 %all_to_all.205.full_ref = f32[8,32,512]{2,1,0:T(8,128)S(1)} all-to-all(f32[8,32,512]{2,1,0:T(8,128)S(1)} %get-tuple-element.148), channel_id=1, replica_groups=mesh['layer'=16,'tile'=8] {'tile'}, dimensions={0} | all-to-all | bytes 1048576 | tf_op jit(solution)/shard_map/all_to_all | solution.py:241
  496.0 6.7 %collective-permute-done.11 = f32[32,512]{1,0:T(8,128)S(1)} collective-permute-done((f32[32,512]{1,0:T(8,128)S(1)}, f32[32,512]{1,0:T(8,128)S(1)}, u32[]{:S(2)}, u32[]{:S(2)}) %collective-permute-start.11) | collective-permute-done | bytes 65568 | tf_op jit(solution)/shard_map/ppermute | solution.py:319
  502.8 13.0 %all_to_all.206.full_ref = f32[8,32,512]{2,1,0:T(8,128)S(1)} all-to-all(f32[8,32,512]{2,1,0:T(8,128)S(1)} %broadcast_in_dim.28), channel_id=1, replica_groups=mesh['layer'=16,'tile'=8] {'tile'}, dimensions={0} | all-to-all | bytes 1048576 | tf_op jit(solution)/shard_map/all_to_all | solution.py:241
  517.2 12.8 %all_to_all.207.full_ref = f32[8,32,512]{2,1,0:T(8,128)S(1)} all-to-all(f32[8,32,512]{2,1,0:T(8,128)S(1)} %get-tuple-element.152), channel_id=1, replica_groups=mesh['layer'=16,'tile'=8] {'tile'}, dimensions={0} | all-to-all | bytes 1048576 | tf_op jit(solution)/shard_map/all_to_all | solution.py:241
  531.4 12.7 %all_to_all.208.full_ref = f32[8,32,512]{2,1,0:T(8,128)S(1)} all-to-all(f32[8,32,512]{2,1,0:T(8,128)S(1)} %get-tuple-element.154), channel_id=1, replica_groups=mesh['layer'=16,'tile'=8] {'tile'}, dimensions={0} | all-to-all | bytes 1048576 | tf_op jit(solution)/shard_map/all_to_all | solution.py:241
  545.5 13.0 %all_to_all.209.full_ref = f32[8,32,512]{2,1,0:T(8,128)S(1)} all-to-all(f32[8,32,512]{2,1,0:T(8,128)S(1)} %get-tuple-element.156), channel_id=1, replica_groups=mesh['layer'=16,'tile'=8] {'tile'}, dimensions={0} | all-to-all | bytes 1048576 | tf_op jit(solution)/shard_map/all_to_all | solution.py:241
  560.7 5.9 collective-permute-done.12
  566.7 12.9 %all_to_all.210.full_ref = f32[8,32,512]{2,1,0:T(8,128)S(1)} all-to-all(f32[8,32,512]{2,1,0:T(8,128)S(1)} %broadcast_in_dim.29), channel_id=1, replica_groups=mesh['layer'=16,'tile'=8] {'tile'}, dimensions={0} | all-to-all | bytes 1048576 | tf_op jit(solution)/shard_map/all_to_all | solution.py:241
  581.0 12.7 %all_to_all.211.full_ref = f32[8,32,512]{2,1,0:T(8,128)S(1)} all-to-all(f32[8,32,512]{2,1,0:T(8,128)S(1)} %get-tuple-element.160), channel_id=1, replica_groups=mesh['layer'=16,'tile'=8] {'tile'}, dimensions={0} | all-to-all | bytes 1048576 | tf_op jit(solution)/shard_map/all_to_all | solution.py:241
  595.1 12.7 %all_to_all.212.full_ref = f32[8,32,512]{2,1,0:T(8,128)S(1)} all-to-all(f32[8,32,512]{2,1,0:T(8,128)S(1)} %get-tuple-element.162), channel_id=1, replica_groups=mesh['layer'=16,'tile'=8] {'tile'}, dimensions={0} | all-to-all | bytes 1048576 | tf_op jit(solution)/shard_map/all_to_all | solution.py:241
  609.2 12.7 %all_to_all.213.full_ref = f32[8,32,512]{2,1,0:T(8,128)S(1)} all-to-all(f32[8,32,512]{2,1,0:T(8,128)S(1)} %get-tuple-element.165), channel_id=1, replica_groups=mesh['layer'=16,'tile'=8] {'tile'}, dimensions={0} | all-to-all | bytes 1048576 | tf_op jit(solution)/shard_map/all_to_all | solution.py:241
  627.2 5.4 shard_map.114
  632.6 5.4 shard_map.115
  (140 shorter events, 98.7 us)
Async XLA Ops:
  2.2 8.4 %collective-permute-start = (f32[2,2,8,512]{3,2,1,0:T(8,128)S(1)}, f32[2,2,8,512]{3,2,1,0:T(8,128)S(1)}, u32[]{:S(2)}, u32[]{:S(2)}) collective-permute-start(f32[2,2,8,512]{3,2,1,0:T(8,128)S(1)} %get-tuple-element.187), channel_id=1, source_target_pairs={{0,8},{8,0},{16,24},{24,16},{32,40},{40,32},{48,56},{56,48},{64,72... | collective-permute-start | bytes 196616 | tf_op jit(solution)/shard_map/ppermute | solution.py:259
  5.5 21.4 %collective-permute-start.2 = (f32[256,4096]{1,0:T(8,128)}, f32[256,4096]{1,0:T(8,128)}, u32[]{:S(2)}, u32[]{:S(2)}) collective-permute-start(f32[256,4096]{1,0:T(8,128)} %shard_map.68.refs_0_), channel_id=1, source_target_pairs={{0,8},{8,0},{16,24},{24,16},{32,40},{40,32},{48,56},{56,48},{64,72... | collective-permute-start | bytes 12582920 | tf_op jit(solution)/shard_map/ppermute | solution.py:264
  9.4 22.1 %collective-permute-start.1 = (f32[256,4096]{1,0:T(8,128)}, f32[256,4096]{1,0:T(8,128)}, u32[]{:S(2)}, u32[]{:S(2)}) collective-permute-start(f32[256,4096]{1,0:T(8,128)} %shard_map.69), channel_id=1, source_target_pairs={{0,8},{8,0},{16,24},{24,16},{32,40},{40,32},{48,56},{56,48},{64,72... | collective-permute-start | bytes 12582920 | tf_op jit(solution)/shard_map/ppermute | solution.py:264
  14.2 3.9 copy-start.15
  14.2 33.4 %collective-permute-start.4 = (f32[256,4096]{1,0:T(8,128)}, f32[256,4096]{1,0:T(8,128)}, u32[]{:S(2)}, u32[]{:S(2)}) collective-permute-start(f32[256,4096]{1,0:T(8,128)} %shard_map.74.refs_0_), channel_id=1, source_target_pairs={{0,8},{8,0},{16,24},{24,16},{32,40},{40,32},{48,56},{56,48},{64,72... | collective-permute-start | bytes 12582920 | tf_op jit(solution)/shard_map/ppermute | solution.py:264
  18.1 34.2 %collective-permute-start.3 = (f32[256,4096]{1,0:T(8,128)}, f32[256,4096]{1,0:T(8,128)}, u32[]{:S(2)}, u32[]{:S(2)}) collective-permute-start(f32[256,4096]{1,0:T(8,128)} %shard_map.75), channel_id=1, source_target_pairs={{0,8},{8,0},{16,24},{24,16},{32,40},{40,32},{48,56},{56,48},{64,72... | collective-permute-start | bytes 12582920 | tf_op jit(solution)/shard_map/ppermute | solution.py:264
  19.2 19.0 %all-to-all-start = ((f32[8,32,512]{2,1,0:T(8,128)}), f32[8,32,512]{2,1,0:T(8,128)S(1)}, u32[]{:S(2)}, u32[]{:S(2)}) async-start(f32[8,32,512]{2,1,0:T(8,128)} %broadcast_in_dim.21.after_ref), calls=%async_computation | async-start | bytes 1048576 | tf_op jit(solution)/shard_map/all_to_all | solution.py:241
  38.1 2.2 copy-start.6
  42.5 9.7 %copy-start = (f32[4,9,32,512]{3,2,1,0:T(8,128)}, f32[4,9,32,512]{3,2,1,0:T(8,128)S(1)}, u32[]{:S(2)}) copy-start(f32[4,9,32,512]{3,2,1,0:T(8,128)S(1)} %get-tuple-element.98.saved_in) | copy-start | bytes 7077892
  42.5 16.1 %all-to-all-start.1 = ((f32[8,32,512]{2,1,0:T(8,128)}), f32[8,32,512]{2,1,0:T(8,128)S(1)}, u32[]{:S(2)}, u32[]{:S(2)}) async-start(f32[8,32,512]{2,1,0:T(8,128)} %get-tuple-element.92.refs_0_.refs_2_), calls=%async_computation.1 | async-start | bytes 1048576 | tf_op jit(solution)/shard_map/all_to_all | solution.py:241
  58.6 2.2 copy-start.11
  60.8 17.5 %copy-start.1 = (f32[4,9,32,512]{3,2,1,0:T(8,128)S(1)}, f32[4,9,32,512]{3,2,1,0:T(8,128)}, u32[]{:S(2)}) copy-start(f32[4,9,32,512]{3,2,1,0:T(8,128)} %copy-done) | copy-start | bytes 7077892
  60.8 17.5 %copy-start.9 = (bf16[512,4096]{1,0:T(8,128)(2,1)S(1)}, bf16[512,4096]{1,0:T(8,128)(2,1)}, u32[]{:S(2)}) copy-start(bf16[512,4096]{1,0:T(8,128)(2,1)} %get-tuple-element.97.mat_ref) | copy-start | bytes 12582916
  78.3 14.2 %copy-start.13 = (bf16[512,4096]{1,0:T(8,128)(2,1)S(1)}, bf16[512,4096]{1,0:T(8,128)(2,1)}, u32[]{:S(2)}) copy-start(bf16[512,4096]{1,0:T(8,128)(2,1)} %get-tuple-element.100.mat_ref) | copy-start | bytes 12582916
  79.7 14.2 %copy-start.2 = (f32[4,9,32,512]{3,2,1,0:T(8,128)}, f32[4,9,32,512]{3,2,1,0:T(8,128)S(1)}, u32[]{:S(2)}) copy-start(f32[4,9,32,512]{3,2,1,0:T(8,128)S(1)} %get-tuple-element.103.saved_in) | copy-start | bytes 7077892
  93.9 6.6 %collective-permute-start.5 = (f32[32,512]{1,0:T(8,128)S(1)}, f32[32,512]{1,0:T(8,128)S(1)}, u32[]{:S(2)}, u32[]{:S(2)}) collective-permute-start(f32[32,512]{1,0:T(8,128)S(1)} %slice_bitcast_fusion.11), channel_id=1, source_target_pairs={{0,16},{8,24},{16,32},{24,40},{32,48},{40,56},{48,64},{56,72},{64,... | collective-permute-start | bytes 196616 | tf_op jit(solution)/shard_map/ppermute | solution.py:319
  113.7 1.7 copy-start.3
  115.3 2.2 copy-start.7
  117.5 15.5 %copy-start.12 = (bf16[512,4096]{1,0:T(8,128)(2,1)S(1)}, bf16[512,4096]{1,0:T(8,128)(2,1)}, u32[]{:S(2)}) copy-start(bf16[512,4096]{1,0:T(8,128)(2,1)} %get-tuple-element.95.mat_ref) | copy-start | bytes 12582916
  118.9 1.4 copy-start.4
  133.0 14.3 %copy-start.5 = (f32[4,9,32,512]{3,2,1,0:T(8,128)S(1)}, f32[4,9,32,512]{3,2,1,0:T(8,128)}, u32[]{:S(2)}) copy-start(f32[4,9,32,512]{3,2,1,0:T(8,128)} %copy-done.4) | copy-start | bytes 7077892
  133.0 14.3 %copy-start.10 = (bf16[512,4096]{1,0:T(8,128)(2,1)S(1)}, bf16[512,4096]{1,0:T(8,128)(2,1)}, u32[]{:S(2)}) copy-start(bf16[512,4096]{1,0:T(8,128)(2,1)} %get-tuple-element.97.mat_ref) | copy-start | bytes 12582916
  147.3 14.2 %copy-start.14 = (bf16[512,4096]{1,0:T(8,128)(2,1)S(1)}, bf16[512,4096]{1,0:T(8,128)(2,1)}, u32[]{:S(2)}) copy-start(bf16[512,4096]{1,0:T(8,128)(2,1)} %get-tuple-element.100.mat_ref) | copy-start | bytes 12582916
  161.5 21.7 %copy-start.8 = (bf16[512,4096]{1,0:T(8,128)(2,1)S(1)}, bf16[512,4096]{1,0:T(8,128)(2,1)}, u32[]{:S(2)}) copy-start(bf16[512,4096]{1,0:T(8,128)(2,1)} %get-tuple-element.91.mat_ref) | copy-start | bytes 12582916
  162.9 6.4 %collective-permute-start.6 = (f32[32,512]{1,0:T(8,128)S(1)}, f32[32,512]{1,0:T(8,128)S(1)}, u32[]{:S(2)}, u32[]{:S(2)}) collective-permute-start(f32[32,512]{1,0:T(8,128)S(1)} %slice_bitcast_fusion.10), channel_id=1, source_target_pairs={{0,16},{8,24},{16,32},{24,40},{32,48},{40,56},{48,64},{56,72},{64,... | collective-permute-start | bytes 196616 | tf_op jit(solution)/shard_map/ppermute | solution.py:319
  231.3 7.1 %collective-permute-start.7 = (f32[32,512]{1,0:T(8,128)S(1)}, f32[32,512]{1,0:T(8,128)S(1)}, u32[]{:S(2)}, u32[]{:S(2)}) collective-permute-start(f32[32,512]{1,0:T(8,128)S(1)} %slice_bitcast_fusion.9), channel_id=1, source_target_pairs={{0,16},{8,24},{16,32},{24,40},{32,48},{40,56},{48,64},{56,72},{64,... | collective-permute-start | bytes 196616 | tf_op jit(solution)/shard_map/ppermute | solution.py:319
  295.1 6.4 %collective-permute-start.8 = (f32[32,512]{1,0:T(8,128)S(1)}, f32[32,512]{1,0:T(8,128)S(1)}, u32[]{:S(2)}, u32[]{:S(2)}) collective-permute-start(f32[32,512]{1,0:T(8,128)S(1)} %slice_bitcast_fusion.8), channel_id=1, source_target_pairs={{0,16},{8,24},{16,32},{24,40},{32,48},{40,56},{48,64},{56,72},{64,... | collective-permute-start | bytes 196616 | tf_op jit(solution)/shard_map/ppermute | solution.py:319
  363.5 6.7 %collective-permute-start.9 = (f32[32,512]{1,0:T(8,128)S(1)}, f32[32,512]{1,0:T(8,128)S(1)}, u32[]{:S(2)}, u32[]{:S(2)}) collective-permute-start(f32[32,512]{1,0:T(8,128)S(1)} %slice_bitcast_fusion.7), channel_id=1, source_target_pairs={{0,16},{8,24},{16,32},{24,40},{32,48},{40,56},{48,64},{56,72},{64,... | collective-permute-start | bytes 196616 | tf_op jit(solution)/shard_map/ppermute | solution.py:319
  427.2 6.4 %collective-permute-start.10 = (f32[32,512]{1,0:T(8,128)S(1)}, f32[32,512]{1,0:T(8,128)S(1)}, u32[]{:S(2)}, u32[]{:S(2)}) collective-permute-start(f32[32,512]{1,0:T(8,128)S(1)} %slice_bitcast_fusion.6), channel_id=1, source_target_pairs={{0,16},{8,24},{16,32},{24,40},{32,48},{40,56},{48,64},{56,72},{64,... | collective-permute-start | bytes 196616 | tf_op jit(solution)/shard_map/ppermute | solution.py:319
  496.0 6.8 %collective-permute-start.11 = (f32[32,512]{1,0:T(8,128)S(1)}, f32[32,512]{1,0:T(8,128)S(1)}, u32[]{:S(2)}, u32[]{:S(2)}) collective-permute-start(f32[32,512]{1,0:T(8,128)S(1)} %slice_bitcast_fusion.5), channel_id=1, source_target_pairs={{0,16},{8,24},{16,32},{24,40},{32,48},{40,56},{48,64},{56,72},{64,... | collective-permute-start | bytes 196616 | tf_op jit(solution)/shard_map/ppermute | solution.py:319
  559.9 6.7 %collective-permute-start.12 = (f32[32,512]{1,0:T(8,128)S(1)}, f32[32,512]{1,0:T(8,128)S(1)}, u32[]{:S(2)}, u32[]{:S(2)}) collective-permute-start(f32[32,512]{1,0:T(8,128)S(1)} %slice_bitcast_fusion.4), channel_id=1, source_target_pairs={{0,16},{8,24},{16,32},{24,40},{32,48},{40,56},{48,64},{56,72},{64,... | collective-permute-start | bytes 196616 | tf_op jit(solution)/shard_map/ppermute | solution.py:319
  624.2 2.9 collective-permute-start.14
  624.4 8.2 %collective-permute-start.13 = (f32[2,9,32,512]{3,2,1,0:T(8,128)S(1)}, f32[2,9,32,512]{3,2,1,0:T(8,128)S(1)}, u32[]{:S(2)}, u32[]{:S(2)}) collective-permute-start(f32[2,9,32,512]{3,2,1,0:T(8,128)S(1)} %slice.89), channel_id=1, source_target_pairs={{0,8},{8,0},{16,24},{24,16},{32,40},{40,32},{48,56},{56,48},{64,72... | collective-permute-start | bytes 3538952 | tf_op jit(solution)/shard_map/ppermute | solution.py:290

commit v7 on v6

--- a/solution.py
+++ b/solution.py
@@ -11,7 +11,7 @@
 CHUNKS = 2
 CORES = 2
 PARTS = 2
-PIECES = 2
+PIECES = 1
 GATHERED = 4
 NT = (((1,), (1,)), ((), ()))
 VMEM = pl.BlockSpec(memory_space=pltpu.VMEM)
@@ -272,11 +272,6 @@
     scale = jnp.exp(-all_phases[1])
     whole = jnp.stack([scale * jnp.cos(all_phases[0]), scale * jnp.sin(all_phases[0])], axis=1)
     fracs = (jnp.arange(1, DEPTHS + 1, dtype=jnp.float32) / DEPTHS).reshape(1, 1, DEPTHS, 1)
-    scale = jnp.exp(-fracs * phases[1][:, :, None, :])
-    cosines = scale * jnp.cos(fracs * phases[0][:, :, None, :])
-    sines = scale * jnp.sin(fracs * phases[0][:, :, None, :])
-
-    whole, cosines, sines = lax.optimization_barrier((whole, cosines, sines))
 
     start = incident.astype(jnp.float32).T.reshape(2, CORES, CHUNKS, part, rows)
     start = jnp.where(core == 0, start[:, 0], start[:, 1])
@@ -310,12 +305,19 @@
                 for half in range(CORES):
                     mats[half * layers + number] = pair[half]
             own = number % layers
+            if tick == 0 and number == 1:
+                scale = jnp.exp(-fracs * later_phases[1][:, :, None, :])
+                cosines = scale * jnp.cos(fracs * later_phases[0][:, :, None, :])
+                sines = scale * jnp.sin(fracs * later_phases[0][:, :, None, :])
+                full, cosines, sines = lax.optimization_barrier((full, cosines, sines))
             if tick == 0 and number < layers:
                 after = full if number else spread
                 saved.append(allocate((CORES * CHUNKS, tiles + 1, wide, rows), after))
             spread, saved[own] = layer_step(
                 full, whole, mats[number], saved[own], tick=tick, number=number, layers=layers
             )
+            if tick == 0 and number == 0:
+                spread, later_phases = lax.optimization_barrier((spread, phases))
         received = lax.ppermute(spread[0], "layer", ring)
 
     saved = lax.optimization_barrier(saved)

time: 649 us -> 655 us (level)
  transfers between devices with their start and end apart: 17 -> 17, of which waited for: 11 -> 10; matrix products, arithmetic and copies ran while one was open for 0% -> 0% of each run, Pallas kernels for 6% -> 7%
where the time goes in v7:
time: 655 us; the launch traced here: 644 us
  blocking collectives  456 us (70%)
  Pallas kernels  100 us (15%)
  waiting for transfers between devices  53.9 us (8%)
  starting transfers between devices  18.1 us (3%)
  local copies, waits for them, and re-layouts  12.9 us (2%)
    all_to_all x34, blocking collectives, to_all(): lax.all_to_all(block, 'tile', split_axis=0, concat_axis=0, tiled=False)  456 us
    pallas_call x36, Pallas kernels, layer_step(): pl.pallas_call(functools.partial(step_kernel, **position), out_shape=(jax...  51.6 us
    ppermute x8, waiting for transfers between devices, on_device(): received = lax.ppermute(spread[0], 'layer', ring)  51.6 us
    pallas_call x4, Pallas kernels, place(): pl.pallas_call(place_kernel, out_shape=(out, out), grid=(PIECES,), in_spe...  22.2 us
    pallas_call x4, Pallas kernels, widen(): pl.pallas_call(widen_kernel, out_shape=jax.ShapeDtypeStruct((height, orde...  15.4 us
    all_to_all x2, starting transfers between devices, to_all(): lax.all_to_all(block, 'tile', split_axis=0, concat_axis=0, tiled=False)  14.7 us
  transfers between devices with their start and end apart: 17, of which 10 were waited for; matrix products, arithmetic and copies ran while one was open for 0% of the time, Pallas kernels for 7%

profile of v7, /device:TPU:0, one launch (start us, length us, event | category | flops | bytes accessed | tf_op | source)
XLA Modules:
  0.0 644.0 jit_solution(7986798996652214977)
XLA Ops:
  20.0 7.7 %all-to-all-start = ((f32[8,32,512]{2,1,0:T(8,128)}), f32[8,32,512]{2,1,0:T(8,128)S(1)}, u32[]{:S(2)}, u32[]{:S(2)}) async-start(f32[8,32,512]{2,1,0:T(8,128)} %broadcast_in_dim.21.after_ref), calls=%async_computation | async-start | bytes 1048576 | tf_op jit(solution)/shard_map/all_to_all | solution.py:241
  27.7 5.5 shard_map.70
  33.2 5.6 shard_map.71
  43.3 7.0 %all-to-all-start.1 = ((f32[8,32,512]{2,1,0:T(8,128)}), f32[8,32,512]{2,1,0:T(8,128)S(1)}, u32[]{:S(2)}, u32[]{:S(2)}) async-start(f32[8,32,512]{2,1,0:T(8,128)} %get-tuple-element.94.refs_0_.refs_2_), calls=%async_computation.1 | async-start | bytes 1048576 | tf_op jit(solution)/shard_map/all_to_all | solution.py:241
  51.5 5.6 shard_map.76
  57.1 5.5 shard_map.77
  66.2 17.9 %all_to_all.180.full_ref = f32[8,32,512]{2,1,0:T(8,128)S(1)} all-to-all(f32[8,32,512]{2,1,0:T(8,128)S(1)} %get-tuple-element.100), channel_id=1, replica_groups=mesh['layer'=16,'tile'=8] {'tile'}, dimensions={0} | all-to-all | bytes 1048576 | tf_op jit(solution)/shard_map/all_to_all | solution.py:241
  85.6 13.2 %all_to_all.181.full_ref = f32[8,32,512]{2,1,0:T(8,128)S(1)} all-to-all(f32[8,32,512]{2,1,0:T(8,128)S(1)} %get-tuple-element.103), channel_id=1, replica_groups=mesh['layer'=16,'tile'=8] {'tile'}, dimensions={0} | all-to-all | bytes 1048576 | tf_op jit(solution)/shard_map/all_to_all | solution.py:241
  101.2 5.9 collective-permute-done.5
  107.1 12.4 %all_to_all.182.full_ref = f32[8,32,512]{2,1,0:T(8,128)S(1)} all-to-all(f32[8,32,512]{2,1,0:T(8,128)S(1)} %broadcast_in_dim.22), channel_id=1, replica_groups=mesh['layer'=16,'tile'=8] {'tile'}, dimensions={0} | all-to-all | bytes 1048576 | tf_op jit(solution)/shard_map/all_to_all | solution.py:241
  126.1 12.7 %all_to_all.183.full_ref = f32[8,32,512]{2,1,0:T(8,128)S(1)} all-to-all(f32[8,32,512]{2,1,0:T(8,128)S(1)} %get-tuple-element.108), channel_id=1, replica_groups=mesh['layer'=16,'tile'=8] {'tile'}, dimensions={0} | all-to-all | bytes 1048576 | tf_op jit(solution)/shard_map/all_to_all | solution.py:241
  140.3 12.9 %all_to_all.184.full_ref = f32[8,32,512]{2,1,0:T(8,128)S(1)} all-to-all(f32[8,32,512]{2,1,0:T(8,128)S(1)} %get-tuple-element.110), channel_id=1, replica_groups=mesh['layer'=16,'tile'=8] {'tile'}, dimensions={0} | all-to-all | bytes 1048576 | tf_op jit(solution)/shard_map/all_to_all | solution.py:241
  154.6 12.7 %all_to_all.185.full_ref = f32[8,32,512]{2,1,0:T(8,128)S(1)} all-to-all(f32[8,32,512]{2,1,0:T(8,128)S(1)} %get-tuple-element.112), channel_id=1, replica_groups=mesh['layer'=16,'tile'=8] {'tile'}, dimensions={0} | all-to-all | bytes 1048576 | tf_op jit(solution)/shard_map/all_to_all | solution.py:241
  168.8 6.4 collective-permute-done.6
  175.3 13.7 %all_to_all.186.full_ref = f32[8,32,512]{2,1,0:T(8,128)S(1)} all-to-all(f32[8,32,512]{2,1,0:T(8,128)S(1)} %broadcast_in_dim.23), channel_id=1, replica_groups=mesh['layer'=16,'tile'=8] {'tile'}, dimensions={0} | all-to-all | bytes 1048576 | tf_op jit(solution)/shard_map/all_to_all | solution.py:241
  190.4 15.9 %all_to_all.187.full_ref = f32[8,32,512]{2,1,0:T(8,128)S(1)} all-to-all(f32[8,32,512]{2,1,0:T(8,128)S(1)} %get-tuple-element.116), channel_id=1, replica_groups=mesh['layer'=16,'tile'=8] {'tile'}, dimensions={0} | all-to-all | bytes 1048576 | tf_op jit(solution)/shard_map/all_to_all | solution.py:241
  207.7 13.8 %all_to_all.188.full_ref = f32[8,32,512]{2,1,0:T(8,128)S(1)} all-to-all(f32[8,32,512]{2,1,0:T(8,128)S(1)} %get-tuple-element.118), channel_id=1, replica_groups=mesh['layer'=16,'tile'=8] {'tile'}, dimensions={0} | all-to-all | bytes 1048576 | tf_op jit(solution)/shard_map/all_to_all | solution.py:241
  222.9 12.9 %all_to_all.189.full_ref = f32[8,32,512]{2,1,0:T(8,128)S(1)} all-to-all(f32[8,32,512]{2,1,0:T(8,128)S(1)} %get-tuple-element.120), channel_id=1, replica_groups=mesh['layer'=16,'tile'=8] {'tile'}, dimensions={0} | all-to-all | bytes 1048576 | tf_op jit(solution)/shard_map/all_to_all | solution.py:241
  237.2 7.1 %collective-permute-done.7 = f32[32,512]{1,0:T(8,128)S(1)} collective-permute-done((f32[32,512]{1,0:T(8,128)S(1)}, f32[32,512]{1,0:T(8,128)S(1)}, u32[]{:S(2)}, u32[]{:S(2)}) %collective-permute-start.7) | collective-permute-done | bytes 65568 | tf_op jit(solution)/shard_map/ppermute | solution.py:321
  244.4 12.6 %all_to_all.190.full_ref = f32[8,32,512]{2,1,0:T(8,128)S(1)} all-to-all(f32[8,32,512]{2,1,0:T(8,128)S(1)} %broadcast_in_dim.24), channel_id=1, replica_groups=mesh['layer'=16,'tile'=8] {'tile'}, dimensions={0} | all-to-all | bytes 1048576 | tf_op jit(solution)/shard_map/all_to_all | solution.py:241
  258.3 12.7 %all_to_all.191.full_ref = f32[8,32,512]{2,1,0:T(8,128)S(1)} all-to-all(f32[8,32,512]{2,1,0:T(8,128)S(1)} %get-tuple-element.124), channel_id=1, replica_groups=mesh['layer'=16,'tile'=8] {'tile'}, dimensions={0} | all-to-all | bytes 1048576 | tf_op jit(solution)/shard_map/all_to_all | solution.py:241
  272.5 12.7 %all_to_all.192.full_ref = f32[8,32,512]{2,1,0:T(8,128)S(1)} all-to-all(f32[8,32,512]{2,1,0:T(8,128)S(1)} %get-tuple-element.126), channel_id=1, replica_groups=mesh['layer'=16,'tile'=8] {'tile'}, dimensions={0} | all-to-all | bytes 1048576 | tf_op jit(solution)/shard_map/all_to_all | solution.py:241
  286.6 12.7 %all_to_all.193.full_ref = f32[8,32,512]{2,1,0:T(8,128)S(1)} all-to-all(f32[8,32,512]{2,1,0:T(8,128)S(1)} %get-tuple-element.128), channel_id=1, replica_groups=mesh['layer'=16,'tile'=8] {'tile'}, dimensions={0} | all-to-all | bytes 1048576 | tf_op jit(solution)/shard_map/all_to_all | solution.py:241
  300.8 6.4 collective-permute-done.8
  307.2 15.5 %all_to_all.194.full_ref = f32[8,32,512]{2,1,0:T(8,128)S(1)} all-to-all(f32[8,32,512]{2,1,0:T(8,128)S(1)} %broadcast_in_dim.25), channel_id=1, replica_groups=mesh['layer'=16,'tile'=8] {'tile'}, dimensions={0} | all-to-all | bytes 1048576 | tf_op jit(solution)/shard_map/all_to_all | solution.py:241
  324.1 14.5 %all_to_all.195.full_ref = f32[8,32,512]{2,1,0:T(8,128)S(1)} all-to-all(f32[8,32,512]{2,1,0:T(8,128)S(1)} %get-tuple-element.132), channel_id=1, replica_groups=mesh['layer'=16,'tile'=8] {'tile'}, dimensions={0} | all-to-all | bytes 1048576 | tf_op jit(solution)/shard_map/all_to_all | solution.py:241
  340.0 12.9 %all_to_all.196.full_ref = f32[8,32,512]{2,1,0:T(8,128)S(1)} all-to-all(f32[8,32,512]{2,1,0:T(8,128)S(1)} %get-tuple-element.134), channel_id=1, replica_groups=mesh['layer'=16,'tile'=8] {'tile'}, dimensions={0} | all-to-all | bytes 1048576 | tf_op jit(solution)/shard_map/all_to_all | solution.py:241
  354.3 13.4 %all_to_all.197.full_ref = f32[8,32,512]{2,1,0:T(8,128)S(1)} all-to-all(f32[8,32,512]{2,1,0:T(8,128)S(1)} %get-tuple-element.136), channel_id=1, replica_groups=mesh['layer'=16,'tile'=8] {'tile'}, dimensions={0} | all-to-all | bytes 1048576 | tf_op jit(solution)/shard_map/all_to_all | solution.py:241
  369.2 6.5 %collective-permute-done.9 = f32[32,512]{1,0:T(8,128)S(1)} collective-permute-done((f32[32,512]{1,0:T(8,128)S(1)}, f32[32,512]{1,0:T(8,128)S(1)}, u32[]{:S(2)}, u32[]{:S(2)}) %collective-permute-start.9) | collective-permute-done | bytes 65568 | tf_op jit(solution)/shard_map/ppermute | solution.py:321
  375.8 12.8 %all_to_all.198.full_ref = f32[8,32,512]{2,1,0:T(8,128)S(1)} all-to-all(f32[8,32,512]{2,1,0:T(8,128)S(1)} %broadcast_in_dim.26), channel_id=1, replica_groups=mesh['layer'=16,'tile'=8] {'tile'}, dimensions={0} | all-to-all | bytes 1048576 | tf_op jit(solution)/shard_map/all_to_all | solution.py:241
  390.0 13.0 %all_to_all.199.full_ref = f32[8,32,512]{2,1,0:T(8,128)S(1)} all-to-all(f32[8,32,512]{2,1,0:T(8,128)S(1)} %get-tuple-element.140), channel_id=1, replica_groups=mesh['layer'=16,'tile'=8] {'tile'}, dimensions={0} | all-to-all | bytes 1048576 | tf_op jit(solution)/shard_map/all_to_all | solution.py:241
  404.4 12.8 %all_to_all.200.full_ref = f32[8,32,512]{2,1,0:T(8,128)S(1)} all-to-all(f32[8,32,512]{2,1,0:T(8,128)S(1)} %get-tuple-element.142), channel_id=1, replica_groups=mesh['layer'=16,'tile'=8] {'tile'}, dimensions={0} | all-to-all | bytes 1048576 | tf_op jit(solution)/shard_map/all_to_all | solution.py:241
  418.5 12.7 %all_to_all.201.full_ref = f32[8,32,512]{2,1,0:T(8,128)S(1)} all-to-all(f32[8,32,512]{2,1,0:T(8,128)S(1)} %get-tuple-element.144), channel_id=1, replica_groups=mesh['layer'=16,'tile'=8] {'tile'}, dimensions={0} | all-to-all | bytes 1048576 | tf_op jit(solution)/shard_map/all_to_all | solution.py:241
  432.8 6.6 %collective-permute-done.10 = f32[32,512]{1,0:T(8,128)S(1)} collective-permute-done((f32[32,512]{1,0:T(8,128)S(1)}, f32[32,512]{1,0:T(8,128)S(1)}, u32[]{:S(2)}, u32[]{:S(2)}) %collective-permute-start.10) | collective-permute-done | bytes 65568 | tf_op jit(solution)/shard_map/ppermute | solution.py:321
  439.4 15.4 %all_to_all.202.full_ref = f32[8,32,512]{2,1,0:T(8,128)S(1)} all-to-all(f32[8,32,512]{2,1,0:T(8,128)S(1)} %broadcast_in_dim.27), channel_id=1, replica_groups=mesh['layer'=16,'tile'=8] {'tile'}, dimensions={0} | all-to-all | bytes 1048576 | tf_op jit(solution)/shard_map/all_to_all | solution.py:241
  456.2 12.9 %all_to_all.203.full_ref = f32[8,32,512]{2,1,0:T(8,128)S(1)} all-to-all(f32[8,32,512]{2,1,0:T(8,128)S(1)} %get-tuple-element.148), channel_id=1, replica_groups=mesh['layer'=16,'tile'=8] {'tile'}, dimensions={0} | all-to-all | bytes 1048576 | tf_op jit(solution)/shard_map/all_to_all | solution.py:241
  470.4 12.8 %all_to_all.204.full_ref = f32[8,32,512]{2,1,0:T(8,128)S(1)} all-to-all(f32[8,32,512]{2,1,0:T(8,128)S(1)} %get-tuple-element.150), channel_id=1, replica_groups=mesh['layer'=16,'tile'=8] {'tile'}, dimensions={0} | all-to-all | bytes 1048576 | tf_op jit(solution)/shard_map/all_to_all | solution.py:241
  484.7 14.1 %all_to_all.205.full_ref = f32[8,32,512]{2,1,0:T(8,128)S(1)} all-to-all(f32[8,32,512]{2,1,0:T(8,128)S(1)} %get-tuple-element.152), channel_id=1, replica_groups=mesh['layer'=16,'tile'=8] {'tile'}, dimensions={0} | all-to-all | bytes 1048576 | tf_op jit(solution)/shard_map/all_to_all | solution.py:241
  500.3 6.4 collective-permute-done.11
  506.7 14.2 %all_to_all.206.full_ref = f32[8,32,512]{2,1,0:T(8,128)S(1)} all-to-all(f32[8,32,512]{2,1,0:T(8,128)S(1)} %broadcast_in_dim.28), channel_id=1, replica_groups=mesh['layer'=16,'tile'=8] {'tile'}, dimensions={0} | all-to-all | bytes 1048576 | tf_op jit(solution)/shard_map/all_to_all | solution.py:241
  522.3 12.8 %all_to_all.207.full_ref = f32[8,32,512]{2,1,0:T(8,128)S(1)} all-to-all(f32[8,32,512]{2,1,0:T(8,128)S(1)} %get-tuple-element.156), channel_id=1, replica_groups=mesh['layer'=16,'tile'=8] {'tile'}, dimensions={0} | all-to-all | bytes 1048576 | tf_op jit(solution)/shard_map/all_to_all | solution.py:241
  536.5 13.0 %all_to_all.208.full_ref = f32[8,32,512]{2,1,0:T(8,128)S(1)} all-to-all(f32[8,32,512]{2,1,0:T(8,128)S(1)} %get-tuple-element.158), channel_id=1, replica_groups=mesh['layer'=16,'tile'=8] {'tile'}, dimensions={0} | all-to-all | bytes 1048576 | tf_op jit(solution)/shard_map/all_to_all | solution.py:241
  550.9 12.7 %all_to_all.209.full_ref = f32[8,32,512]{2,1,0:T(8,128)S(1)} all-to-all(f32[8,32,512]{2,1,0:T(8,128)S(1)} %get-tuple-element.160), channel_id=1, replica_groups=mesh['layer'=16,'tile'=8] {'tile'}, dimensions={0} | all-to-all | bytes 1048576 | tf_op jit(solution)/shard_map/all_to_all | solution.py:241
  565.3 6.4 collective-permute-done.12
  571.8 13.2 %all_to_all.210.full_ref = f32[8,32,512]{2,1,0:T(8,128)S(1)} all-to-all(f32[8,32,512]{2,1,0:T(8,128)S(1)} %broadcast_in_dim.29), channel_id=1, replica_groups=mesh['layer'=16,'tile'=8] {'tile'}, dimensions={0} | all-to-all | bytes 1048576 | tf_op jit(solution)/shard_map/all_to_all | solution.py:241
  586.4 12.7 %all_to_all.211.full_ref = f32[8,32,512]{2,1,0:T(8,128)S(1)} all-to-all(f32[8,32,512]{2,1,0:T(8,128)S(1)} %get-tuple-element.164), channel_id=1, replica_groups=mesh['layer'=16,'tile'=8] {'tile'}, dimensions={0} | all-to-all | bytes 1048576 | tf_op jit(solution)/shard_map/all_to_all | solution.py:241
  600.6 12.7 %all_to_all.212.full_ref = f32[8,32,512]{2,1,0:T(8,128)S(1)} all-to-all(f32[8,32,512]{2,1,0:T(8,128)S(1)} %get-tuple-element.166), channel_id=1, replica_groups=mesh['layer'=16,'tile'=8] {'tile'}, dimensions={0} | all-to-all | bytes 1048576 | tf_op jit(solution)/shard_map/all_to_all | solution.py:241
  614.7 12.7 %all_to_all.213.full_ref = f32[8,32,512]{2,1,0:T(8,128)S(1)} all-to-all(f32[8,32,512]{2,1,0:T(8,128)S(1)} %get-tuple-element.169), channel_id=1, replica_groups=mesh['layer'=16,'tile'=8] {'tile'}, dimensions={0} | all-to-all | bytes 1048576 | tf_op jit(solution)/shard_map/all_to_all | solution.py:241
  (141 shorter events, 98.0 us)
Async XLA Ops:
  2.2 8.2 %collective-permute-start = (f32[2,2,8,512]{3,2,1,0:T(8,128)S(1)}, f32[2,2,8,512]{3,2,1,0:T(8,128)S(1)}, u32[]{:S(2)}, u32[]{:S(2)}) collective-permute-start(f32[2,2,8,512]{3,2,1,0:T(8,128)S(1)} %bitcast_dynamic-update-slice_fusion), channel_id=1, source_target_pairs={{0,8},{8,0},{16,24},{24,16},{32,40},{40,32},{48,56},{56,48},{64,72... | collective-permute-start | bytes 196616 | tf_op jit(solution)/shard_map/ppermute | solution.py:259
  6.0 21.7 %collective-permute-start.2 = (f32[256,4096]{1,0:T(8,128)}, f32[256,4096]{1,0:T(8,128)}, u32[]{:S(2)}, u32[]{:S(2)}) collective-permute-start(f32[256,4096]{1,0:T(8,128)} %shard_map.68.refs_0_), channel_id=1, source_target_pairs={{0,8},{8,0},{16,24},{24,16},{32,40},{40,32},{48,56},{56,48},{64,72... | collective-permute-start | bytes 12582920 | tf_op jit(solution)/shard_map/ppermute | solution.py:264
  10.4 22.8 %collective-permute-start.1 = (f32[256,4096]{1,0:T(8,128)}, f32[256,4096]{1,0:T(8,128)}, u32[]{:S(2)}, u32[]{:S(2)}) collective-permute-start(f32[256,4096]{1,0:T(8,128)} %shard_map.69), channel_id=1, source_target_pairs={{0,8},{8,0},{16,24},{24,16},{32,40},{40,32},{48,56},{56,48},{64,72... | collective-permute-start | bytes 12582920 | tf_op jit(solution)/shard_map/ppermute | solution.py:264
  14.5 4.4 copy-start.15
  14.5 37.0 %collective-permute-start.4 = (f32[256,4096]{1,0:T(8,128)}, f32[256,4096]{1,0:T(8,128)}, u32[]{:S(2)}, u32[]{:S(2)}) collective-permute-start(f32[256,4096]{1,0:T(8,128)} %shard_map.74.refs_0_), channel_id=1, source_target_pairs={{0,8},{8,0},{16,24},{24,16},{32,40},{40,32},{48,56},{56,48},{64,72... | collective-permute-start | bytes 12582920 | tf_op jit(solution)/shard_map/ppermute | solution.py:264
  18.9 38.2 %collective-permute-start.3 = (f32[256,4096]{1,0:T(8,128)}, f32[256,4096]{1,0:T(8,128)}, u32[]{:S(2)}, u32[]{:S(2)}) collective-permute-start(f32[256,4096]{1,0:T(8,128)} %shard_map.75), channel_id=1, source_target_pairs={{0,8},{8,0},{16,24},{24,16},{32,40},{40,32},{48,56},{56,48},{64,72... | collective-permute-start | bytes 12582920 | tf_op jit(solution)/shard_map/ppermute | solution.py:264
  20.0 19.0 %all-to-all-start = ((f32[8,32,512]{2,1,0:T(8,128)}), f32[8,32,512]{2,1,0:T(8,128)S(1)}, u32[]{:S(2)}, u32[]{:S(2)}) async-start(f32[8,32,512]{2,1,0:T(8,128)} %broadcast_in_dim.21.after_ref), calls=%async_computation | async-start | bytes 1048576 | tf_op jit(solution)/shard_map/all_to_all | solution.py:241
  38.9 2.2 copy-start.6
  43.3 13.8 %copy-start = (f32[4,9,32,512]{3,2,1,0:T(8,128)}, f32[4,9,32,512]{3,2,1,0:T(8,128)S(1)}, u32[]{:S(2)}) copy-start(f32[4,9,32,512]{3,2,1,0:T(8,128)S(1)} %get-tuple-element.102.saved_in) | copy-start | bytes 7077892
  43.3 19.3 %all-to-all-start.1 = ((f32[8,32,512]{2,1,0:T(8,128)}), f32[8,32,512]{2,1,0:T(8,128)S(1)}, u32[]{:S(2)}, u32[]{:S(2)}) async-start(f32[8,32,512]{2,1,0:T(8,128)} %get-tuple-element.94.refs_0_.refs_2_), calls=%async_computation.1 | async-start | bytes 1048576 | tf_op jit(solution)/shard_map/all_to_all | solution.py:241
  62.6 2.2 copy-start.11
  64.8 19.3 %copy-start.1 = (f32[4,9,32,512]{3,2,1,0:T(8,128)S(1)}, f32[4,9,32,512]{3,2,1,0:T(8,128)}, u32[]{:S(2)}) copy-start(f32[4,9,32,512]{3,2,1,0:T(8,128)} %copy-done) | copy-start | bytes 7077892
  64.8 19.3 %copy-start.9 = (bf16[512,4096]{1,0:T(8,128)(2,1)S(1)}, bf16[512,4096]{1,0:T(8,128)(2,1)}, u32[]{:S(2)}) copy-start(bf16[512,4096]{1,0:T(8,128)(2,1)} %get-tuple-element.101.mat_ref) | copy-start | bytes 12582916
  84.1 14.6 %copy-start.13 = (bf16[512,4096]{1,0:T(8,128)(2,1)S(1)}, bf16[512,4096]{1,0:T(8,128)(2,1)}, u32[]{:S(2)}) copy-start(bf16[512,4096]{1,0:T(8,128)(2,1)} %get-tuple-element.104.mat_ref) | copy-start | bytes 12582916
  85.6 14.6 %copy-start.2 = (f32[4,9,32,512]{3,2,1,0:T(8,128)}, f32[4,9,32,512]{3,2,1,0:T(8,128)S(1)}, u32[]{:S(2)}) copy-start(f32[4,9,32,512]{3,2,1,0:T(8,128)S(1)} %get-tuple-element.107.saved_in) | copy-start | bytes 7077892
  100.2 6.8 %collective-permute-start.5 = (f32[32,512]{1,0:T(8,128)S(1)}, f32[32,512]{1,0:T(8,128)S(1)}, u32[]{:S(2)}, u32[]{:S(2)}) collective-permute-start(f32[32,512]{1,0:T(8,128)S(1)} %slice_bitcast_fusion.11), channel_id=1, source_target_pairs={{0,16},{8,24},{16,32},{24,40},{32,48},{40,56},{48,64},{56,72},{64,... | collective-permute-start | bytes 196616 | tf_op jit(solution)/shard_map/ppermute | solution.py:321
  119.5 1.7 copy-start.3
  121.1 2.2 copy-start.7
  123.3 15.5 %copy-start.12 = (bf16[512,4096]{1,0:T(8,128)(2,1)S(1)}, bf16[512,4096]{1,0:T(8,128)(2,1)}, u32[]{:S(2)}) copy-start(bf16[512,4096]{1,0:T(8,128)(2,1)} %get-tuple-element.99.mat_ref) | copy-start | bytes 12582916
  124.7 1.4 copy-start.4
  138.9 14.3 %copy-start.5 = (f32[4,9,32,512]{3,2,1,0:T(8,128)S(1)}, f32[4,9,32,512]{3,2,1,0:T(8,128)}, u32[]{:S(2)}) copy-start(f32[4,9,32,512]{3,2,1,0:T(8,128)} %copy-done.4) | copy-start | bytes 7077892
  138.9 14.3 %copy-start.10 = (bf16[512,4096]{1,0:T(8,128)(2,1)S(1)}, bf16[512,4096]{1,0:T(8,128)(2,1)}, u32[]{:S(2)}) copy-start(bf16[512,4096]{1,0:T(8,128)(2,1)} %get-tuple-element.101.mat_ref) | copy-start | bytes 12582916
  153.2 14.2 %copy-start.14 = (bf16[512,4096]{1,0:T(8,128)(2,1)S(1)}, bf16[512,4096]{1,0:T(8,128)(2,1)}, u32[]{:S(2)}) copy-start(bf16[512,4096]{1,0:T(8,128)(2,1)} %get-tuple-element.104.mat_ref) | copy-start | bytes 12582916
  167.3 21.7 %copy-start.8 = (bf16[512,4096]{1,0:T(8,128)(2,1)S(1)}, bf16[512,4096]{1,0:T(8,128)(2,1)}, u32[]{:S(2)}) copy-start(bf16[512,4096]{1,0:T(8,128)(2,1)} %get-tuple-element.92.mat_ref) | copy-start | bytes 12582916
  168.8 6.4 %collective-permute-start.6 = (f32[32,512]{1,0:T(8,128)S(1)}, f32[32,512]{1,0:T(8,128)S(1)}, u32[]{:S(2)}, u32[]{:S(2)}) collective-permute-start(f32[32,512]{1,0:T(8,128)S(1)} %slice_bitcast_fusion.10), channel_id=1, source_target_pairs={{0,16},{8,24},{16,32},{24,40},{32,48},{40,56},{48,64},{56,72},{64,... | collective-permute-start | bytes 196616 | tf_op jit(solution)/shard_map/ppermute | solution.py:321
  237.2 7.1 %collective-permute-start.7 = (f32[32,512]{1,0:T(8,128)S(1)}, f32[32,512]{1,0:T(8,128)S(1)}, u32[]{:S(2)}, u32[]{:S(2)}) collective-permute-start(f32[32,512]{1,0:T(8,128)S(1)} %slice_bitcast_fusion.9), channel_id=1, source_target_pairs={{0,16},{8,24},{16,32},{24,40},{32,48},{40,56},{48,64},{56,72},{64,... | collective-permute-start | bytes 196616 | tf_op jit(solution)/shard_map/ppermute | solution.py:321
  300.7 6.4 %collective-permute-start.8 = (f32[32,512]{1,0:T(8,128)S(1)}, f32[32,512]{1,0:T(8,128)S(1)}, u32[]{:S(2)}, u32[]{:S(2)}) collective-permute-start(f32[32,512]{1,0:T(8,128)S(1)} %slice_bitcast_fusion.8), channel_id=1, source_target_pairs={{0,16},{8,24},{16,32},{24,40},{32,48},{40,56},{48,64},{56,72},{64,... | collective-permute-start | bytes 196616 | tf_op jit(solution)/shard_map/ppermute | solution.py:321
  369.1 6.6 %collective-permute-start.9 = (f32[32,512]{1,0:T(8,128)S(1)}, f32[32,512]{1,0:T(8,128)S(1)}, u32[]{:S(2)}, u32[]{:S(2)}) collective-permute-start(f32[32,512]{1,0:T(8,128)S(1)} %slice_bitcast_fusion.7), channel_id=1, source_target_pairs={{0,16},{8,24},{16,32},{24,40},{32,48},{40,56},{48,64},{56,72},{64,... | collective-permute-start | bytes 196616 | tf_op jit(solution)/shard_map/ppermute | solution.py:321
  432.7 6.7 %collective-permute-start.10 = (f32[32,512]{1,0:T(8,128)S(1)}, f32[32,512]{1,0:T(8,128)S(1)}, u32[]{:S(2)}, u32[]{:S(2)}) collective-permute-start(f32[32,512]{1,0:T(8,128)S(1)} %slice_bitcast_fusion.6), channel_id=1, source_target_pairs={{0,16},{8,24},{16,32},{24,40},{32,48},{40,56},{48,64},{56,72},{64,... | collective-permute-start | bytes 196616 | tf_op jit(solution)/shard_map/ppermute | solution.py:321
  500.2 6.4 %collective-permute-start.11 = (f32[32,512]{1,0:T(8,128)S(1)}, f32[32,512]{1,0:T(8,128)S(1)}, u32[]{:S(2)}, u32[]{:S(2)}) collective-permute-start(f32[32,512]{1,0:T(8,128)S(1)} %slice_bitcast_fusion.5), channel_id=1, source_target_pairs={{0,16},{8,24},{16,32},{24,40},{32,48},{40,56},{48,64},{56,72},{64,... | collective-permute-start | bytes 196616 | tf_op jit(solution)/shard_map/ppermute | solution.py:321
  565.0 6.7 %collective-permute-start.12 = (f32[32,512]{1,0:T(8,128)S(1)}, f32[32,512]{1,0:T(8,128)S(1)}, u32[]{:S(2)}, u32[]{:S(2)}) collective-permute-start(f32[32,512]{1,0:T(8,128)S(1)} %slice_bitcast_fusion.4), channel_id=1, source_target_pairs={{0,16},{8,24},{16,32},{24,40},{32,48},{40,56},{48,64},{56,72},{64,... | collective-permute-start | bytes 196616 | tf_op jit(solution)/shard_map/ppermute | solution.py:321
  629.7 2.9 collective-permute-start.14
  629.9 8.2 %collective-permute-start.13 = (f32[2,9,32,512]{3,2,1,0:T(8,128)S(1)}, f32[2,9,32,512]{3,2,1,0:T(8,128)S(1)}, u32[]{:S(2)}, u32[]{:S(2)}) collective-permute-start(f32[2,9,32,512]{3,2,1,0:T(8,128)S(1)} %slice.93), channel_id=1, source_target_pairs={{0,8},{8,0},{16,24},{24,16},{32,40},{40,32},{48,56},{56,48},{64,72... | collective-permute-start | bytes 3538952 | tf_op jit(solution)/shard_map/ppermute | solution.py:285
